TPU v7x, 32 devices: a whole 2x2x4 slice. The times are simulated.
32 devices in a mesh: img: 4 (over y, x), seq: 8 (over z, core).
Axes of the slice: x: 2, y: 2, z: 4, core: 2. Of those that a mesh axis runs over, the one named last changes fastest.
Arguments:
- query_proj: bfloat16 [4, 1024, 1280], P('img', 'seq'), may hold values from -6 to 6
- key_proj: bfloat16 [4, 1024, 1280], P('img', 'seq'), may hold values from -6 to 6
- value_proj: bfloat16 [4, 1024, 1280], P('img', 'seq'), may hold values from -12 to 12
- merge_cells: int32 [4, 256, 4], P('img', 'seq'), may hold values from 0 to 1023, as said below
- unmerge: int32 [4, 1024], P('img', 'seq'), may hold values from 0 to 255, as said below
- grad_out: bfloat16 [4, 1024, 1280], P('img', 'seq'), may hold values from -9 to 9
- query_gain: float32 [64], replicated, may hold values from 1 to 2.5
- key_gain: float32 [64], replicated, may hold values from 1 to 2.5
Outputs:
- attended: bfloat16 [4, 1024, 1280], P('img', 'seq')
- grad_query: bfloat16 [4, 1024, 1280], P('img', 'seq')
- grad_key: bfloat16 [4, 1024, 1280], P('img', 'seq')
- grad_value: bfloat16 [4, 1024, 1280], P('img', 'seq')
- grad_query_gain: float32 [64], replicated
- grad_key_gain: float32 [64], replicated
Inputs may be any that keep to these rules, and one draw needn't show every extreme that they name: `merge_cells`: row c of an image lists, in some order, the four tokens of one 2x2 cell: columns j and j + 1 (modulo 64) of image rows 2 i and 2 i + 1, where token r * 64 + s stands at row r and column s and j has one parity within each pair of rows; every token lies in exactly one cell; cell c and its four tokens are held by the same seq index. `unmerge`: entry t is the row of merge_cells of the same image that lists token t.
All inputs are finite; a program needn't handle non-finite values.
Results may differ from a plain program's by a relative error of at most 0.012.
Values may be sent and summed in bfloat16 or wider, within the bound.
No kernel may reach another device: no remote copies, remote signals or barrier semaphores. Data moves between devices by JAX's collectives and lax.ppermute only.
A program may use at most 128 MiB of HBM per device.

v0:
```python
import math

import jax
import jax.numpy as jnp
from jax import lax
from jax.sharding import PartitionSpec as P

EPSILON = 1e-06
PRECISE = lax.Precision.HIGHEST


def partner(array, axis, apart):
    return lax.ppermute(array, axis, [(i, i ^ 1 << apart) for i in range(lax.axis_size(axis))])


def shifted(value, axis, steps):
    count = lax.axis_size(axis)
    pairs = [(source, (source + steps) % count) for source in range(count)]
    return lax.ppermute(value, axis, pairs)


def normalize(inputs, gain_row):
    row_scale = lax.rsqrt(jnp.mean(inputs * inputs, axis=-1, keepdims=True) + EPSILON)
    unit_vals = inputs * row_scale
    return (unit_vals, row_scale, unit_vals * gain_row)


def norm_back(grad_normed, unit_vals, row_scale, gain_row):
    grad_unit = grad_normed * gain_row
    mean_inner = jnp.mean(grad_unit * unit_vals, axis=-1, keepdims=True)
    return row_scale * (grad_unit - unit_vals * mean_inner)


def attention_pass(queries, upstream, keys_all, values_all):
    tok_rows, group_heads, head_dim = queries.shape
    group_lanes = group_heads * head_dim
    cell_count = keys_all.shape[0]
    block_rows = math.gcd(cell_count, 512)
    block_count = cell_count // block_rows
    key_blocks = keys_all.reshape(block_count, block_rows, group_lanes)
    value_blocks = values_all.reshape(block_count, block_rows, group_lanes)

    def scores_of(key_rows):
        return (
            jnp.einsum(
                "thd,khd->thk",
                queries,
                key_rows.reshape(-1, group_heads, head_dim),
                preferred_element_type=jnp.float32,
            )
            * 0.125
        )

    def forward_step(running, pieces):
        row_total, weighted = running
        key_rows, value_rows = pieces
        exp_scores = jnp.exp(scores_of(key_rows))
        row_total = row_total + jnp.sum(exp_scores, axis=-1)
        weighted = weighted + jnp.einsum(
            "thk,khd->thd",
            exp_scores.astype(jnp.bfloat16),
            value_rows.reshape(-1, group_heads, head_dim),
            preferred_element_type=jnp.float32,
        )
        return ((row_total, weighted), None)

    initial = (
        jnp.zeros((tok_rows, group_heads), jnp.float32),
        jnp.zeros((tok_rows, group_heads, head_dim), jnp.float32),
    )
    (row_total, weighted), unused = lax.scan(forward_step, initial, (key_blocks, value_blocks))
    attended = (weighted / row_total[:, :, None]).astype(jnp.bfloat16)
    row_inner = jnp.sum(upstream.astype(jnp.float32) * attended.astype(jnp.float32), axis=-1)

    def local_grads(key_rows, value_rows):
        attention = jnp.exp(scores_of(key_rows)) / row_total[:, :, None]
        grad_weights = jnp.einsum(
            "thd,khd->thk",
            upstream,
            value_rows.reshape(-1, group_heads, head_dim),
            preferred_element_type=jnp.float32,
        )
        grad_scores = (attention * (grad_weights - row_inner[:, :, None])).astype(jnp.bfloat16)
        return (attention.astype(jnp.bfloat16), grad_scores)

    def key_terms(key_rows, attention_bf, grad_scores):
        row_count = key_rows.shape[0]
        grad_keys = (
            jnp.einsum("thk,thd->khd", grad_scores, queries, preferred_element_type=jnp.float32)
            * 0.125
        )
        grad_values = jnp.einsum(
            "thk,thd->khd", attention_bf, upstream, preferred_element_type=jnp.float32
        )
        return jnp.concatenate(
            [
                grad_keys.reshape(row_count, group_lanes),
                grad_values.reshape(row_count, group_lanes),
            ],
            axis=1,
        )

    def query_term(key_rows, grad_scores):
        return (
            jnp.einsum(
                "thk,khd->thd",
                grad_scores,
                key_rows.reshape(-1, group_heads, head_dim),
                preferred_element_type=jnp.float32,
            )
            * 0.125
        )

    query_zero = jnp.zeros((tok_rows, group_heads, head_dim), jnp.float32)

    def backward_step(running, pieces):
        key_rows, value_rows = pieces
        attention_bf, grad_scores = local_grads(key_rows, value_rows)
        return (
            running + query_term(key_rows, grad_scores),
            key_terms(key_rows, attention_bf, grad_scores),
        )

    grad_q_group, term_blocks = lax.scan(backward_step, query_zero, (key_blocks, value_blocks))
    return (attended, grad_q_group, term_blocks.reshape(cell_count, 2 * group_lanes), None)


def pair_exchange(array, seq_index, outbound):
    first_bit = seq_index % 2
    second_bit = seq_index // 2 % 2
    kept_part = jnp.where(first_bit == 0, array[:, 0], array[:, 1])
    sent_part = jnp.where(first_bit == 0, array[:, 1], array[:, 0])
    if outbound:
        arrived = partner(sent_part, "seq", 0)
    else:
        arrived = partner(sent_part, "seq", 0)
    combined = jnp.stack(
        [
            jnp.where(first_bit == 0, kept_part, arrived),
            jnp.where(first_bit == 0, arrived, kept_part),
        ],
        axis=1,
    )
    kept_part = jnp.where(second_bit == 0, combined[0], combined[1])
    sent_part = jnp.where(second_bit == 0, combined[1], combined[0])
    if outbound:
        arrived = partner(sent_part, "seq", 1)
    else:
        arrived = partner(sent_part, "seq", 1)
    return jnp.stack(
        [
            jnp.where(second_bit == 0, kept_part, arrived),
            jnp.where(second_bit == 0, arrived, kept_part),
        ],
        axis=0,
    )


def to_slots(array, lane_part):
    row_count = array.shape[0]
    return (
        array.reshape(row_count, 4, lane_part)
        .transpose(1, 0, 2)
        .reshape(2, 2, row_count, lane_part)
    )


def from_slots(block):
    row_count = block.shape[1]
    return block.transpose(1, 0, 2).reshape(row_count, 4 * block.shape[2])


def local(query_proj, key_proj, value_proj, merge_cells, unmerge, grad_out, query_gain, key_gain):
    tok_dev = query_proj.shape[1]
    total_lanes = query_proj.shape[2]
    head_dim = query_gain.shape[0]
    head_count = total_lanes // head_dim
    cells_dev = merge_cells.shape[1]
    cell_count = cells_dev * lax.axis_size("seq")
    seq_index = lax.axis_index("seq")
    q_unit, q_scale, q_normed = normalize(
        query_proj[0].astype(jnp.float32).reshape(tok_dev, head_count, head_dim), query_gain
    )
    q_bf = q_normed.reshape(tok_dev, total_lanes).astype(jnp.bfloat16)
    k_unit, k_scale, k_normed = normalize(
        key_proj[0].astype(jnp.float32).reshape(tok_dev, head_count, head_dim), key_gain
    )
    tok_ids = seq_index * tok_dev + jnp.arange(tok_dev, dtype=jnp.int32)
    member = jnp.sum(
        (merge_cells[0][:, :, None] == tok_ids[None, None, :]).astype(jnp.float32), axis=1
    )
    k_merged = (
        jnp.dot(member, k_normed.reshape(tok_dev, total_lanes), precision=PRECISE) * 0.25
    ).astype(jnp.bfloat16)
    v_merged = (
        jnp.dot(member.astype(jnp.bfloat16), value_proj[0], preferred_element_type=jnp.float32)
        * 0.25
    ).astype(jnp.bfloat16)
    lane_part = total_lanes // 4
    heads_part = head_count // 4
    inbound = jnp.concatenate(
        [
            to_slots(q_bf, lane_part),
            to_slots(grad_out[0], lane_part),
            to_slots(k_merged, lane_part),
            to_slots(v_merged, lane_part),
        ],
        axis=2,
    )
    arrived = pair_exchange(inbound, seq_index, False).reshape(
        4, 2 * tok_dev + 2 * cells_dev, lane_part
    )
    queries = arrived[:, :tok_dev].reshape(4 * tok_dev, heads_part, head_dim)
    upstream = arrived[:, tok_dev : 2 * tok_dev].reshape(4 * tok_dev, heads_part, head_dim)
    group_rows = 4 * cells_dev
    pair_block = jnp.stack(
        [
            arrived[:, 2 * tok_dev : 2 * tok_dev + cells_dev].reshape(group_rows, lane_part),
            arrived[:, 2 * tok_dev + cells_dev :].reshape(group_rows, lane_part),
        ]
    )
    circle = lax.axis_size("seq") // 4
    group_index = seq_index // 4
    stored = jnp.zeros((2, cell_count, lane_part), jnp.bfloat16)
    stored = lax.dynamic_update_slice_in_dim(stored, pair_block, group_index * group_rows, 1)

    def gather_step(turn_index, carry):
        current, buffer = carry
        current = shifted(current, "seq", 4)
        source = (group_index - turn_index) % circle
        buffer = lax.dynamic_update_slice_in_dim(buffer, current, source * group_rows, 1)
        return (current, buffer)

    current, stored = lax.fori_loop(1, circle, gather_step, (pair_block, stored))
    attended, grad_q_group, term_rows, unused = attention_pass(
        queries, upstream, stored[0], stored[1]
    )

    def block_of(block_index):
        return lax.dynamic_slice_in_dim(term_rows, block_index * group_rows, group_rows, 0)

    def reduce_step(turn_index, partial_sum):
        return shifted(partial_sum, "seq", 4) + block_of((group_index - 1 - turn_index) % circle)

    reduced = lax.fori_loop(1, circle, reduce_step, block_of((group_index - 1) % circle))
    outbound = jnp.concatenate(
        [
            attended.astype(jnp.float32).reshape(4, tok_dev, lane_part),
            grad_q_group.reshape(4, tok_dev, lane_part),
            reduced[:, :lane_part].reshape(4, cells_dev, lane_part),
            reduced[:, lane_part:].reshape(4, cells_dev, lane_part),
        ],
        axis=1,
    )
    returned = pair_exchange(
        outbound.reshape(2, 2, 2 * tok_dev + 2 * cells_dev, lane_part), seq_index, True
    ).reshape(4, 2 * tok_dev + 2 * cells_dev, lane_part)
    attended_all = from_slots(returned[:, :tok_dev]).astype(jnp.bfloat16)
    grad_q_normed = from_slots(returned[:, tok_dev : 2 * tok_dev]).reshape(
        tok_dev, head_count, head_dim
    )
    grad_merged_k = from_slots(returned[:, 2 * tok_dev : 2 * tok_dev + cells_dev])
    grad_merged_v = from_slots(returned[:, 2 * tok_dev + cells_dev :])
    cell_ids = seq_index * cells_dev + jnp.arange(cells_dev, dtype=jnp.int32)
    unmerge_table = (unmerge[0][:, None] == cell_ids[None, :]).astype(jnp.float32)
    grad_k_normed = (jnp.dot(unmerge_table, grad_merged_k, precision=PRECISE) * 0.25).reshape(
        tok_dev, head_count, head_dim
    )
    grad_value = (jnp.dot(unmerge_table, grad_merged_v, precision=PRECISE) * 0.25).astype(
        jnp.bfloat16
    )
    gain_terms = (
        jnp.sum(grad_q_normed * q_unit, axis=(0, 1)),
        jnp.sum(grad_k_normed * k_unit, axis=(0, 1)),
    )
    grad_query_gain, grad_key_gain = lax.psum((gain_terms[0], gain_terms[1]), ("img", "seq"))
    grad_query = (
        norm_back(grad_q_normed, q_unit, q_scale, query_gain)
        .reshape(tok_dev, total_lanes)
        .astype(jnp.bfloat16)
    )
    grad_key = (
        norm_back(grad_k_normed, k_unit, k_scale, key_gain)
        .reshape(tok_dev, total_lanes)
        .astype(jnp.bfloat16)
    )
    return (
        attended_all[None],
        grad_query[None],
        grad_key[None],
        grad_value[None],
        grad_query_gain,
        grad_key_gain,
    )


def solution(mesh):
    placed = (
        P("img", "seq", None),
        P("img", "seq", None),
        P("img", "seq", None),
        P("img", "seq", None),
        P("img", "seq"),
        P("img", "seq", None),
        P(),
        P(),
    )
    return jax.shard_map(
        local,
        mesh=mesh,
        in_specs=placed,
        out_specs=(
            P("img", "seq", None),
            P("img", "seq", None),
            P("img", "seq", None),
            P("img", "seq", None),
            P(),
            P(),
        ),
        check_vma=False,
    )
```

profile of v0, /device:TPU:0, one launch (start us, length us, event | category | flops | bytes accessed | tf_op | source)
XLA Modules:
  0.0 167.1 jit_solution(1000217355713323992)
XLA Ops:
  0.7 0.8 convert_reduce_fusion
  2.0 0.2 copy.79
  2.2 0.7 mul.241
  3.0 1.1 copy.76
  4.3 0.7 copy-done.3
  4.9 0.2 copy.77
  5.2 0.5 fusion.5
  5.9 0.2 copy.78
  6.1 0.2 copy.75
  6.3 1.2 copy.74
  8.0 0.3 copy-done.5
  8.3 0.4 copy-done.2
  8.7 0.3 pad_maximum_fusion.3
  9.0 0.5 collective-permute-start
  9.5 1.6 collective-permute-done
  11.2 1.1 select_bitcast_fusion.5
  12.5 3.0 %collective-permute-start.1 = (bf16[2,320,320]{1,2,0:T(8,128)(2,1)S(1)}, bf16[2,320,320]{1,2,0:T(8,128)(2,1)S(1)}, u32[]{:S(2)}, u32[]{:S(2)}) collective-permute-start(bf16[2,320,320]{1,2,0:T(8,128)(2,1)S(1)} %fusion.26), channel_id=1, source_target_pairs={{0,2},{1,3},{2,0},{3,1},{4,6},{5,7},{6,4},{7,5},{8,10},{9,11},{10,... | collective-permute-start | bytes 1228808 | tf_op jit(solution)/shard_map/ppermute | solution.py:13
  15.5 11.5 %collective-permute-done.1 = bf16[2,320,320]{1,2,0:T(8,128)(2,1)S(1)} collective-permute-done((bf16[2,320,320]{1,2,0:T(8,128)(2,1)S(1)}, bf16[2,320,320]{1,2,0:T(8,128)(2,1)S(1)}, u32[]{:S(2)}, u32[]{:S(2)}) %collective-permute-start.1) | collective-permute-done | bytes 409632 | tf_op jit(solution)/shard_map/ppermute | solution.py:13
  27.0 0.3 select_bitcast_fusion.3
  27.3 0.2 pad_maximum_fusion.4
  28.0 0.7 pad_maximum_fusion.6
  28.7 2.8 %collective-permute-start.2 = (bf16[2,128,320]{2,1,0:T(8,128)(2,1)}, bf16[2,128,320]{2,1,0:T(8,128)(2,1)}, u32[]{:S(2)}, u32[]{:S(2)}) collective-permute-start(bf16[2,128,320]{2,1,0:T(8,128)(2,1)} %pad_maximum_fusion.6), channel_id=1, source_target_pairs={{0,4},{1,5},{2,6},{3,7},{4,0},{5,1},{6,2},{7,3},{8,12},{9,13},{10,... | collective-permute-start | bytes 491528 | tf_op jit(solution)/shard_map/while/body/eval_jaxpr/ppermute | solution.py:19
  31.6 1.1 copy.90
  32.7 0.3 copy.118
  33.1 0.3 copy.119
  33.6 7.0 %collective-permute-done.2 = bf16[2,128,320]{2,1,0:T(8,128)(2,1)} collective-permute-done((bf16[2,128,320]{2,1,0:T(8,128)(2,1)}, bf16[2,128,320]{2,1,0:T(8,128)(2,1)}, u32[]{:S(2)}, u32[]{:S(2)}) %collective-permute-start.2) | collective-permute-done | bytes 163872 | tf_op jit(solution)/shard_map/while/body/eval_jaxpr/ppermute | solution.py:19
  40.6 1.1 copy.91
  41.8 0.6 bitcast_reduce_fusion
  42.4 1.3 fusion.7
  43.7 1.4 multiply_reduce_fusion.3
  45.1 1.7 %fusion.1 = bf16[512,5,256]{0,2,1:T(8,128)(2,1)S(1)} fusion(bf16[256,5,64]{0,2,1:T(8,128)(2,1)S(1)} %bitcast.278, bf16[512,5,64]{0,2,1:T(8,128)(2,1)} %copy-done.8, f32[512,5]{0,1:T(8,128)S(1)} %get-tuple-element.117, f32[512,5]{0,1:T(8,128)S(1)} %get-tuple-element.115, f32[5,256,512]{2,1,0:T(8,128)S(1)} %get-tuple-element.116), kind=kOutput, calls=%fused_computation.2 | convolution fusion | flops 87162880 | bytes 4444160 | tf_op jit(solution)/shard_map/while/body/eval_jaxpr/thd,khd->thk/dot_general | solution.py:77
  46.8 0.5 convolution_multiply_fusion.4
  47.5 1.1 copy.99
  48.7 0.9 fusion.33
  49.5 2.1 %fusion.12 = f32[512,5,64]{0,2,1:T(8,128)} fusion(bf16[256,5,64]{0,2,1:T(8,128)(2,1)} %bitcast.263, bf16[512,5,256]{0,2,1:T(8,128)(2,1)S(1)} %fusion.1), kind=kOutput, calls=%fused_computation.25 | convolution fusion | flops 84049920 | bytes 2129920 | tf_op jit(solution)/shard_map/while/body/eval_jaxpr/thk,khd->thd/dot_general | solution.py:105
  51.6 1.5 concatenate.21
  53.2 2.4 %concatenate.20 = f32[2,2,128,320]{2,1,0,3:T(2,128)} reshape(f32[512,5,64]{0,2,1:T(8,128)} %get-tuple-element.118) | data formatting | bytes 1310720 | tf_op jit(solution)/shard_map/concatenate | solution.py:246
  55.5 1.1 copy.100
  56.7 9.8 %collective-permute-done.3 = f32[128,640]{1,0:T(8,128)} collective-permute-done((f32[128,640]{1,0:T(8,128)}, f32[128,640]{1,0:T(8,128)}, u32[]{:S(2)}, u32[]{:S(2)}) %collective-permute-start.3) | collective-permute-done | bytes 327712 | tf_op jit(solution)/shard_map/while/body/eval_jaxpr/ppermute | solution.py:19
  66.5 1.1 fusion.32
  67.6 0.8 fusion.49
  68.4 1.2 copy.103
  69.5 2.0 %copy.102 = f32[2,2,32,320]{2,3,0,1:T(8,128)} copy(f32[2,2,32,320]{3,2,1,0:T(8,128)} %bitcast.270) | data formatting | bytes 327680 | tf_op jit(solution)/shard_map/concatenate | solution.py:246
  71.5 1.4 pad_maximum_fusion
  73.1 2.6 %collective-permute-done.4 = f32[2,320,320]{1,2,0:T(8,128)S(1)} collective-permute-done((f32[2,320,320]{1,2,0:T(8,128)S(1)}, f32[2,320,320]{1,2,0:T(8,128)S(1)}, u32[]{:S(2)}, u32[]{:S(2)}) %collective-permute-start.4) | collective-permute-done | bytes 819232 | tf_op jit(solution)/shard_map/ppermute | solution.py:13
  75.8 1.1 select_bitcast_fusion
  77.0 24.0 %collective-permute-done.5 = f32[2,320,320]{1,2,0:T(8,128)} collective-permute-done((f32[2,320,320]{1,2,0:T(8,128)}, f32[2,320,320]{1,2,0:T(8,128)}, u32[]{:S(2)}, u32[]{:S(2)}) %collective-permute-start.5) | collective-permute-done | bytes 819232 | tf_op jit(solution)/shard_map/ppermute | solution.py:13
  101.0 1.4 fusion.16
  102.5 0.8 slice.171
  103.3 0.9 slice.106
  104.2 1.2 fusion.46
  105.4 1.9 %copy.108 = bf16[1,128,1280]{2,1,0:T(8,128)(2,1)} copy(bf16[1,128,1280]{1,2,0:T(8,128)(2,1)} %bitcast.268) | data formatting | bytes 655360
  107.3 1.3 multiply_reduce_fusion.2
  108.6 2.2 %fusion.22 = bf16[1,128,1280]{1,2,0:T(8,128)(2,1)} fusion(f32[128,20]{0,1:T(8,128)S(1)} %broadcast_multiply_fusion.2, f32[1280]{0:T(1024)S(1)} %mul.259, f32[128,20]{0,1:T(8,128)S(1)} %add_rsqrt_fusion.1, bf16[1,128,1280]{1,2,0:T(8,128)(2,1)} %copy-done.5, f32[1,128,1280]{1,2,0:T(8,128)} %bitcast.252), kind=kLoop, calls=%fused_computation.56 | loop fusion | flops 1146880 | bytes 1336320 | tf_op jit(solution)/shard_map/convert_element_type | solution.py:280
  110.7 2.1 %copy.109 = bf16[1,128,1280]{2,1,0:T(8,128)(2,1)} copy(bf16[1,128,1280]{1,2,0:T(8,128)(2,1)} %fusion.22) | data formatting | bytes 655360
  112.8 2.6 %broadcast_multiply_fusion = (f32[128,1280]{1,0:T(8,128)}, f32[128,1280]{1,0:T(8,128)}) fusion(f32[32,1280]{0,1:T(8,128)} %bitcast.257, s32[32]{0:T(128)S(1)} %iota_add_fusion, s32[128]{0:T(128)S(1)} %bitcast.279), kind=kOutput, calls=%fused_computation.90 | convolution fusion | flops 63082496 | bytes 1475200 | tf_op jit(solution)/shard_map/dot_general | solution.py:266
  115.4 2.2 %copy.105 = f32[128,1280]{0,1:T(8,128)} copy(f32[128,1280]{1,0:T(8,128)} %get-tuple-element.119) | data formatting | bytes 1310720 | tf_op jit(solution)/shard_map/mul | solution.py:266
  117.6 1.5 multiply_reduce_fusion.1
  119.1 0.9 mul.281
  120.0 2.2 %copy.106 = f32[128,1280]{1,0:T(8,128)} copy(f32[128,1280]{0,1:T(8,128)} %bitcast.260) | data formatting | bytes 1310720 | tf_op jit(solution)/shard_map/mul | solution.py:31
  122.2 2.3 %fusion.3 = bf16[1,128,1280]{2,1,0:T(8,128)(2,1)} fusion(f32[32,1280]{0,1:T(8,128)} %bitcast.258, s32[32]{0:T(128)S(1)} %iota_add_fusion, s32[128]{0:T(128)S(1)} %bitcast.280), kind=kOutput, calls=%fused_computation.9 | convolution fusion | flops 63246336 | bytes 492160 | tf_op jit(solution)/shard_map/dot_general | solution.py:269
  124.5 1.4 fusion.23
  125.9 2.4 %multiply_reduce_fusion = (f32[1280]{0:T(1024)S(1)}, bf16[1,128,1280]{2,1,0:T(8,128)(2,1)}) fusion(f32[128,1280]{1,0:T(8,128)} %copy-done.1, bf16[1,128,1280]{2,1,0:T(8,128)(2,1)S(1)} %copy-done.4, f32[128,1280]{1,0:T(8,128)} %get-tuple-element.120, f32[128,1280]{1,0:T(8,128)} %copy.106, f32[1280]{0:T(1024)S(1)} %broadcast_multiply_fusion.3), kind=kLoop, calls=%fused_computation.63 | loop fusion | flops 1637120 | bytes 2631680 | tf_op jit(solution)/shard_map/reduce_sum | solution.py:274
  128.4 38.7 %all-reduce = (f32[64]{0:T(128)}, f32[64]{0:T(128)}) all-reduce(f32[64]{0:T(128)S(1)} %reduce_sum.105, f32[64]{0:T(128)S(1)} %reduce_sum.108), channel_id=1, replica_groups=mesh['img'=4,'seq'=8] {'img','seq'}, use_global_device_ids=true, to_apply=%region_9.10 | all-reduce | flops 128 | bytes 1024 | tf_op jit(solution)/shard_map/psum | solution.py:276
  (66 shorter events, 3.5 us)
Async XLA Ops:
  0.6 1.0 copy-start
  2.0 3.2 %copy-start.4 = (bf16[1,128,1280]{2,1,0:T(8,128)(2,1)S(1)}, bf16[1,128,1280]{2,1,0:T(8,128)(2,1)}, u32[]{:S(2)}) copy-start(bf16[1,128,1280]{2,1,0:T(8,128)(2,1)} %param.9) | copy-start | bytes 983044
  4.1 0.8 copy-start.3
  4.2 1.9 %copy-start.7 = (bf16[1,128,1280]{2,1,0:T(8,128)(2,1)S(1)}, bf16[1,128,1280]{2,1,0:T(8,128)(2,1)}, u32[]{:S(2)}) copy-start(bf16[1,128,1280]{2,1,0:T(8,128)(2,1)} %param.13) | copy-start | bytes 983044
  5.2 1.2 copy-start.1
  5.2 2.4 %copy-start.9 = (f32[64]{0:T(128)S(1)}, f32[64]{0:T(128)}, u32[]{:S(2)}) copy-start(f32[64]{0:T(128)} %param.14) | copy-start | bytes 772
  7.5 0.7 copy-start.5
  7.8 0.8 copy-start.2
  9.0 2.1 %collective-permute-start = (bf16[2,320,320]{1,2,0:T(8,128)(2,1)S(1)}, bf16[2,320,320]{1,2,0:T(8,128)(2,1)}, u32[]{:S(2)}, u32[]{:S(2)}) collective-permute-start(bf16[2,320,320]{1,2,0:T(8,128)(2,1)S(1)} %fusion.25), channel_id=1, source_target_pairs={{0,1},{1,0},{2,3},{3,2},{4,5},{5,4},{6,7},{7,6},{8,9},{9,8},{10,11... | collective-permute-start | bytes 1228808 | tf_op jit(solution)/shard_map/ppermute | solution.py:13
  12.5 14.5 %collective-permute-start.1 = (bf16[2,320,320]{1,2,0:T(8,128)(2,1)S(1)}, bf16[2,320,320]{1,2,0:T(8,128)(2,1)S(1)}, u32[]{:S(2)}, u32[]{:S(2)}) collective-permute-start(bf16[2,320,320]{1,2,0:T(8,128)(2,1)S(1)} %fusion.26), channel_id=1, source_target_pairs={{0,2},{1,3},{2,0},{3,1},{4,6},{5,7},{6,4},{7,5},{8,10},{9,11},{10,... | collective-permute-start | bytes 1228808 | tf_op jit(solution)/shard_map/ppermute | solution.py:13
  28.7 11.9 %collective-permute-start.2 = (bf16[2,128,320]{2,1,0:T(8,128)(2,1)}, bf16[2,128,320]{2,1,0:T(8,128)(2,1)}, u32[]{:S(2)}, u32[]{:S(2)}) collective-permute-start(bf16[2,128,320]{2,1,0:T(8,128)(2,1)} %pad_maximum_fusion.6), channel_id=1, source_target_pairs={{0,4},{1,5},{2,6},{3,7},{4,0},{5,1},{6,2},{7,3},{8,12},{9,13},{10,... | collective-permute-start | bytes 491528 | tf_op jit(solution)/shard_map/while/body/eval_jaxpr/ppermute | solution.py:19
  33.5 10.2 %copy-start.8 = (bf16[512,5,64]{0,2,1:T(8,128)(2,1)}, bf16[512,5,64]{0,2,1:T(8,128)(2,1)S(1)}, u32[]{:S(2)}) copy-start(bf16[512,5,64]{0,2,1:T(8,128)(2,1)S(1)} %reshape.251) | copy-start | bytes 983044
  41.8 1.9 %copy-start.6 = (bf16[1,256,320]{1,2,0:T(8,128)(2,1)}, bf16[1,256,320]{1,2,0:T(8,128)(2,1)S(1)}, u32[]{:S(2)}) copy-start(bf16[1,256,320]{1,2,0:T(8,128)(2,1)S(1)} %get-tuple-element.113) | copy-start | bytes 491524
  49.5 17.0 %collective-permute-start.3 = (f32[128,640]{1,0:T(8,128)}, f32[128,640]{1,0:T(8,128)}, u32[]{:S(2)}, u32[]{:S(2)}) collective-permute-start(f32[128,640]{1,0:T(8,128)} %fusion.33), channel_id=1, source_target_pairs={{0,4},{1,5},{2,6},{3,7},{4,0},{5,1},{6,2},{7,3},{8,12},{9,13},{10,... | collective-permute-start | bytes 983048 | tf_op jit(solution)/shard_map/while/body/eval_jaxpr/ppermute | solution.py:19
  73.0 2.6 %collective-permute-start.4 = (f32[2,320,320]{1,2,0:T(8,128)S(1)}, f32[2,320,320]{1,2,0:T(8,128)S(1)}, u32[]{:S(2)}, u32[]{:S(2)}) collective-permute-start(f32[2,320,320]{1,2,0:T(8,128)S(1)} %select_bitcast_fusion.1), channel_id=1, source_target_pairs={{0,1},{1,0},{2,3},{3,2},{4,5},{5,4},{6,7},{7,6},{8,9},{9,8},{10,11... | collective-permute-start | bytes 2457608 | tf_op jit(solution)/shard_map/ppermute | solution.py:13
  76.9 24.1 %collective-permute-start.5 = (f32[2,320,320]{1,2,0:T(8,128)}, f32[2,320,320]{1,2,0:T(8,128)}, u32[]{:S(2)}, u32[]{:S(2)}) collective-permute-start(f32[2,320,320]{1,2,0:T(8,128)} %select_bitcast_fusion), channel_id=1, source_target_pairs={{0,2},{1,3},{2,0},{3,1},{4,6},{5,7},{6,4},{7,5},{8,10},{9,11},{10,... | collective-permute-start | bytes 2457608 | tf_op jit(solution)/shard_map/ppermute | solution.py:13
  105.4 7.4 %copy-start.11 = (s32[1,128]{1,0:T(1,128)S(1)}, s32[1,128]{1,0:T(1,128)}, u32[]{:S(2)}) copy-start(s32[1,128]{1,0:T(1,128)} %param.12) | copy-start | bytes 1540
  110.7 6.9 %copy-start.10 = (f32[64]{0:T(128)S(1)}, f32[64]{0:T(128)}, u32[]{:S(2)}) copy-start(f32[64]{0:T(128)} %param.15) | copy-start | bytes 772
where the time goes:
time: 168 us; the launch traced here: 167 us
  waiting for transfers between devices  56.5 us (34%)
  blocking collectives  38.7 us (23%)
  local copies, waits for them, and re-layouts  32.3 us (19%)
  other arithmetic  18.8 us (11%)
  matrix products  13.3 us (8%)
  starting transfers between devices  6.36 us (4%)
    ppermute x4, waiting for transfers between devices, partner(): lax.ppermute(array, axis, [(i, i ^ 1 << apart) for i in range(lax.axis_si...  39.7 us
    psum x1, blocking collectives, local(): lax.psum((gain_terms[0], gain_terms[1]), ('img', 'seq'))  38.7 us
    ppermute x2, waiting for transfers between devices, shifted(): return lax.ppermute(value, axis, pairs)  16.8 us
    concatenate x6, local copies, waits for them, and re-layouts, local(): jnp.concatenate([attended.astype(jnp.float32).reshape(4, tok_dev, lane_pa...  8.18 us
    unnamed x32, local copies, waits for them, and re-layouts  7.71 us
    ppermute x4, starting transfers between devices, partner(): lax.ppermute(array, axis, [(i, i ^ 1 << apart) for i in range(lax.axis_si...  3.61 us
  transfers between devices with their start and end apart: 6, of which 6 were waited for; matrix products, arithmetic and copies ran while one was open for 6% of the time, Pallas kernels for 0%

commit v1 on v0

v1 whole, which is shorter than its diff:
```python
import functools
import math

import jax
import jax.numpy as jnp
from jax import lax
from jax.experimental import pallas as pl
from jax.experimental.pallas import tpu as pltpu
from jax.sharding import PartitionSpec as P

EPSILON = 1e-06
TILE = 128
CORES = 2
BF16 = jnp.bfloat16
F32 = jnp.float32
VMEM_BYTES = 40 * 1024 * 1024


def call(kernel, out_shapes, inputs, scratch=()):
    in_vmem = pl.BlockSpec(memory_space=pltpu.VMEM)
    return pl.pallas_call(
        kernel,
        out_shape=[jax.ShapeDtypeStruct(shape, kind) for shape, kind in out_shapes],
        in_specs=[in_vmem] * len(inputs),
        out_specs=[in_vmem] * len(out_shapes),
        scratch_shapes=[pltpu.VMEM(shape, kind) for shape, kind in scratch],
        compiler_params=pltpu.CompilerParams(vmem_limit_bytes=VMEM_BYTES),
    )(*inputs)


def core_side():
    return lax.rem(lax.axis_index("seq"), CORES)


def lanes_at(index):
    return pl.ds(pl.multiple_of(index * TILE, TILE), TILE)


def dot(left, right, contract=((1,), (0,))):
    return lax.dot_general(left, right, (contract, ((), ())), preferred_element_type=F32)


def halves(array):
    high = array.astype(BF16)
    return high, (array - high.astype(F32)).astype(BF16)


def exact_dot(left, right, contract=((1,), (0,))):
    high, low = halves(right)
    return dot(left, high, contract) + dot(left, low, contract)


def head_mean(array, head_dim):
    rows = lax.broadcasted_iota(jnp.int32, (TILE, TILE), 0) // head_dim
    cols = lax.broadcasted_iota(jnp.int32, (TILE, TILE), 1) // head_dim
    same = jnp.where(rows == cols, 1.0 / head_dim, 0.0).astype(BF16)
    high, low = halves(array)
    return dot(high, same) + dot(low, same)


def unit_rows(array, head_dim):
    scale = lax.rsqrt(head_mean(array * array, head_dim) + EPSILON)
    return array * scale, scale


def norm_back(grad_normed, unit_vals, scale, gain_row, head_dim):
    grad_unit = grad_normed * gain_row
    return scale * (grad_unit - unit_vals * head_mean(grad_unit * unit_vals, head_dim))


def merge_kernel(head_dim, bounds, key_ref, value_ref, cells_ref, gain_ref, *refs):
    count = len(bounds)
    own_refs, send_refs, merged = refs[:count], refs[count : 2 * count], refs[2 * count :]
    tok, lanes = key_ref.shape
    half = lanes // CORES
    cells = cells_ref.shape[0]
    side = core_side()
    listed = lax.rem(cells_ref[...], tok)
    ids = lax.broadcasted_iota(jnp.int32, (cells, tok), 1)
    member = sum(
        (listed[:, j : j + 1] == ids).astype(F32) for j in range(cells_ref.shape[1])
    ).astype(BF16)
    gain_row = gain_ref[...] * 0.25
    for part in range(CORES):
        for chunk, (start, stop) in enumerate(bounds):
            for at in range(start, stop, TILE):
                source = slice(part * half + at, part * half + at + TILE)
                unit_vals, _ = unit_rows(key_ref[:, source].astype(F32), head_dim)
                keys = exact_dot(member, unit_vals) * gain_row
                values = dot(member, value_ref[:, source]) * 0.25
                merged[chunk][part, :, at - start : at - start + TILE] = keys.astype(BF16)
                there = stop - start + at - start
                merged[chunk][part, :, there : there + TILE] = values.astype(BF16)
    for chunk in range(count):
        own_refs[chunk][...] = merged[chunk][side]
        send_refs[chunk][...] = merged[chunk][1 - side]


def pack_kernel(query_ref, upstream_ref, send_ref):
    half = query_ref.shape[1] // CORES
    other = 1 - core_side()
    for tile in range(half // TILE):
        source = lanes_at(other * (half // TILE) + tile)
        send_ref[:, tile * TILE : (tile + 1) * TILE] = query_ref[:, source]
        send_ref[:, half + tile * TILE : half + (tile + 1) * TILE] = upstream_ref[:, source]


def query_kernel(head_dim, query_ref, upstream_ref, arrived_ref, gain_ref, out_ref, grad_ref):
    tok, lanes = query_ref.shape
    half = lanes // CORES
    side = core_side()
    for tile in range(half // TILE):
        lane = slice(tile * TILE, (tile + 1) * TILE)
        other = slice(half + tile * TILE, half + (tile + 1) * TILE)
        source = lanes_at(side * (half // TILE) + tile)
        for row, queries in ((0, query_ref[:, source]), (tok, arrived_ref[:, lane])):
            unit_vals, _ = unit_rows(queries.astype(F32), head_dim)
            out_ref[row : row + tok, lane] = (unit_vals * gain_ref[...]).astype(BF16)
        grad_ref[:tok, lane] = upstream_ref[:, source]
        grad_ref[tok:, lane] = arrived_ref[:, other]


def attend_kernel(head_dim, start, blocks, group, *refs):
    query_ref, upstream_ref, gain_ref = refs[:3]
    block_refs = refs[3 : 3 + blocks]
    attended_ref, grad_ref, gain_out_ref = refs[3 + blocks : 6 + blocks]
    part_refs = refs[6 + blocks :]
    rows = query_ref.shape[0]
    block_rows, width = block_refs[0].shape
    width = width // 2
    per = TILE // head_dim
    cells = group * block_rows
    scale = head_dim**-0.5
    exponent = scale * math.log2(math.e)
    lane_head = lax.broadcasted_iota(jnp.int32, (1, TILE), 1) // head_dim
    cell_heads = lax.broadcasted_iota(jnp.int32, (cells, TILE), 1) // head_dim
    masks = [(cell_heads == head).astype(F32).astype(BF16) for head in range(per)]

    def spread(array):
        return jnp.concatenate([array * mask for mask in masks], axis=0)

    def by_lane(parts):
        result = parts[0]
        for head in range(1, per):
            result = jnp.where(lane_head == head, parts[head], result)
        return result

    def folded(array):
        return by_lane([array[head * cells : (head + 1) * cells] for head in range(per)])

    def one_tile(tile, gain_sum):
        lane = lanes_at(tile)
        value_lane = lanes_at(width // TILE + tile)
        source = lanes_at(start // TILE + tile)
        queries = query_ref[:, source]
        upstream = upstream_ref[:, source]
        weighted = jnp.zeros((rows, TILE), F32)
        totals = [jnp.zeros((rows, 1), F32) for _ in range(per)]
        held = []
        for first in range(0, blocks, group):
            members = block_refs[first : first + group]
            keys = jnp.concatenate([ref[:, lane] for ref in members], axis=0)
            spread_keys = spread(keys)
            spread_values = spread(
                jnp.concatenate([ref[:, value_lane] for ref in members], axis=0)
            )
            scores = dot(queries, spread_keys, ((1,), (1,)))
            exp_scores = jnp.exp2(scores * exponent)
            weighted += dot(exp_scores.astype(BF16), spread_values)
            exp_parts = [exp_scores[:, h * cells : (h + 1) * cells] for h in range(per)]
            totals = [
                total + jnp.sum(part, axis=1, keepdims=True)
                for total, part in zip(totals, exp_parts)
            ]
            held.append((keys, spread_keys, spread_values, exp_parts))
        inverses = [1.0 / total for total in totals]
        attended = (weighted * by_lane(inverses)).astype(BF16)
        attended_ref[:, lane] = attended
        products = upstream.astype(F32) * attended.astype(F32)
        inners = [
            jnp.sum(jnp.where(lane_head == h, products, 0.0), axis=1, keepdims=True)
            for h in range(per)
        ]
        grad_queries = jnp.zeros((rows, TILE), F32)
        for index, (keys, spread_keys, spread_values, exp_parts) in enumerate(held):
            grad_weights = dot(upstream, spread_values, ((1,), (1,)))
            attention = [part * inverse for part, inverse in zip(exp_parts, inverses)]
            grad_scores = jnp.concatenate(
                [
                    (attention[h] * (grad_weights[:, h * cells : (h + 1) * cells] - inners[h]))
                    .astype(BF16)
                    for h in range(per)
                ],
                axis=1,
            )
            attention_bf = jnp.concatenate([part.astype(BF16) for part in attention], axis=1)
            grad_queries += dot(grad_scores, spread_keys)
            grad_keys = folded(dot(grad_scores, queries, ((0,), (0,)))) * scale
            grad_values = folded(dot(attention_bf, upstream, ((0,), (0,))))
            gain_sum += jnp.sum(grad_keys * keys.astype(F32), axis=0, keepdims=True)
            for member in range(group):
                ref = part_refs[index * group + member]
                here = slice(member * block_rows, (member + 1) * block_rows)
                ref[:, lane] = grad_keys[here].astype(ref.dtype)
                ref[:, value_lane] = grad_values[here].astype(ref.dtype)
        grad_ref[:, lane] = grad_queries * scale
        return gain_sum

    gain_sum = jnp.zeros((1, TILE), F32)
    if blocks == group:
        for tile in range(width // TILE):
            gain_sum = one_tile(tile, gain_sum)
    else:
        gain_sum = lax.fori_loop(0, width // TILE, one_tile, gain_sum)
    gain_out_ref[...] = gain_sum / gain_ref[...]


def query_back_kernel(head_dim, bounds, query_ref, arrived_ref, gain_ref, *refs):
    count = len(bounds)
    attended_refs, grad_refs, gain_refs = (
        refs[i * count : (i + 1) * count] for i in range(3)
    )
    own_ref, send_ref, gain_out_ref = refs[3 * count :]
    tok, lanes = query_ref.shape
    half = lanes // CORES
    side = core_side()
    query_sum = jnp.zeros((1, TILE), F32)
    for (start, stop), attended_ref, grad_ref in zip(bounds, attended_refs, grad_refs):
        for at in range(start, stop, TILE):
            here = slice(at - start, at - start + TILE)
            lane = slice(at, at + TILE)
            grad_lane = slice(half + at, half + at + TILE)
            source = lanes_at(side * (half // TILE) + at // TILE)
            for row, queries, out_ref in (
                (0, query_ref[:, source], own_ref),
                (tok, arrived_ref[:, lane], send_ref),
            ):
                unit_vals, scale = unit_rows(queries.astype(F32), head_dim)
                grad_normed = grad_ref[row : row + tok, here]
                query_sum += jnp.sum(grad_normed * unit_vals, axis=0, keepdims=True)
                out_ref[:, lane] = attended_ref[row : row + tok, here]
                out_ref[:, grad_lane] = norm_back(
                    grad_normed, unit_vals, scale, gain_ref[...], head_dim
                ).astype(BF16)
    key_sum = gain_refs[0][...]
    for ref in gain_refs[1:]:
        key_sum += ref[...]

    def per_channel(row):
        return sum(row[:, at : at + head_dim] for at in range(0, TILE, head_dim))

    gain_out_ref[...] = jnp.concatenate([per_channel(query_sum), per_channel(key_sum)], axis=1)


def place_kernel(own_ref, arrived_ref, attended_ref, grad_ref):
    half = own_ref.shape[1] // 2
    tiles = half // TILE
    side = core_side()
    for source_ref, at_side in ((own_ref, side), (arrived_ref, 1 - side)):
        for tile in range(tiles):
            there = lanes_at(at_side * tiles + tile)
            attended_ref[:, there] = source_ref[:, tile * TILE : (tile + 1) * TILE]
            grad_ref[:, there] = source_ref[:, half + tile * TILE : half + (tile + 1) * TILE]


def key_back_kernel(head_dim, bounds, terms, key_ref, unmerge_ref, gain_ref, *refs):
    count = len(bounds)
    term_refs = [refs[chunk * terms : (chunk + 1) * terms] for chunk in range(count)]
    arrived_refs = refs[count * terms : count * (terms + 1)]
    grad_key_ref, grad_value_ref = refs[count * (terms + 1) : count * (terms + 1) + 2]
    merged = refs[count * (terms + 1) + 2 :]
    tok, lanes = key_ref.shape
    half = lanes // CORES
    cells = arrived_refs[0].shape[0]
    side = core_side()
    for chunk in range(count):
        total = term_refs[chunk][0][:cells].astype(F32)
        for ref in term_refs[chunk][1:]:
            total += ref[:cells].astype(F32)
        merged[chunk][side] = total
        merged[chunk][1 - side] = arrived_refs[chunk][...]
    owner = lax.rem(unmerge_ref[...], cells)
    table = (lax.broadcasted_iota(jnp.int32, (cells, tok), 0) == owner).astype(F32).astype(BF16)
    for part in range(CORES):
        for chunk, (start, stop) in enumerate(bounds):
            for at in range(start, stop, TILE):
                here = at - start
                there = stop - start + here
                lane = slice(part * half + at, part * half + at + TILE)
                grad_keys = merged[chunk][part, :, here : here + TILE]
                grad_values = merged[chunk][part, :, there : there + TILE]
                unit_vals, scale = unit_rows(key_ref[:, lane].astype(F32), head_dim)
                grad_normed = exact_dot(table, grad_keys, ((0,), (0,))) * 0.25
                grad_key_ref[:, lane] = norm_back(
                    grad_normed, unit_vals, scale, gain_ref[...], head_dim
                ).astype(BF16)
                grad_value_ref[:, lane] = (
                    exact_dot(table, grad_values, ((0,), (0,))) * 0.25
                ).astype(BF16)


def exchange(array, axis, apart):
    return lax.ppermute(array, axis, [(i, i ^ apart) for i in range(lax.axis_size(axis))])


def chip_gather(block, chips):
    if chips == 1:
        return [block]
    mirrored = exchange(block, "seq", CORES * (chips - 1))
    low = chip_gather(block, chips // 2)
    high = chip_gather(mirrored, chips // 2)
    return low + high[::-1]


def chip_reduce(parts):
    chips = len(parts)
    if chips == 1:
        return [parts[0]]
    high = chip_reduce(parts[: chips // 2 - 1 : -1])
    sent = high[0].astype(F32)
    for term in high[1:]:
        sent += term.astype(F32)
    mirrored = exchange(sent.astype(BF16), "seq", CORES * (chips - 1))
    return chip_reduce(parts[: chips // 2]) + [mirrored]


def device_sum(array):
    for axis in ("seq", "img"):
        apart = 1
        while apart < lax.axis_size(axis):
            array = array + exchange(array, axis, apart)
            apart *= 2
    return array


def chunk_bounds(half):
    return ((0, half),)


def local(query_proj, key_proj, value_proj, merge_cells, unmerge, grad_out, query_gain, key_gain):
    queries, key_rows, value_rows = query_proj[0], key_proj[0], value_proj[0]
    upstream = grad_out[0]
    tok, lanes = queries.shape
    half = lanes // CORES
    head_dim = query_gain.shape[0]
    cells = merge_cells.shape[1]
    chips = lax.axis_size("seq") // CORES
    bounds = chunk_bounds(half)
    widths = [stop - start for start, stop in bounds]
    query_row = jnp.tile(query_gain, TILE // head_dim)[None]
    key_row = jnp.tile(key_gain, TILE // head_dim)[None]

    merged = call(
        functools.partial(merge_kernel, head_dim, bounds),
        [((cells, 2 * width), BF16) for width in widths] * 2,
        [key_rows, value_rows, merge_cells[0], key_row],
        [((CORES, cells, 2 * width), BF16) for width in widths],
    )
    gathered = []
    for own, sent in zip(merged[: len(bounds)], merged[len(bounds) :]):
        block = jnp.concatenate([own, exchange(sent, "seq", 1)], axis=0)
        gathered.append(chip_gather(block, chips))

    (packed,) = call(pack_kernel, [((tok, lanes), BF16)], [queries, upstream])
    arrived = exchange(packed, "seq", 1)
    normed, both_upstream = call(
        functools.partial(query_kernel, head_dim),
        [((CORES * tok, half), BF16)] * 2,
        [queries, upstream, arrived, query_row],
    )

    group = min(chips, 4)
    attended, grads, key_sums, terms = [], [], [], []
    for (start, stop), width, blocks in zip(bounds, widths, gathered):
        results = call(
            functools.partial(attend_kernel, head_dim, start, chips, group),
            [
                ((CORES * tok, width), BF16),
                ((CORES * tok, width), F32),
                ((1, TILE), F32),
                ((CORES * cells, 2 * width), F32),
            ]
            + [((CORES * cells, 2 * width), BF16)] * (chips - 1),
            [normed, both_upstream, key_row] + blocks,
        )
        attended.append(results[0])
        grads.append(results[1])
        key_sums.append(results[2])
        terms.append(chip_reduce(results[3:]))

    own_part, sent_part, gain_sums = call(
        functools.partial(query_back_kernel, head_dim, bounds),
        [((tok, lanes), BF16)] * 2 + [((1, 2 * head_dim), F32)],
        [queries, arrived, query_row] + attended + grads + key_sums,
    )
    attended_all, grad_query = call(
        place_kernel,
        [((tok, lanes), BF16)] * 2,
        [own_part, exchange(sent_part, "seq", 1)],
    )
    gain_total = device_sum(gain_sums)[0]

    returned = []
    for chunk in terms:
        sent = chunk[0][cells:].astype(F32)
        for term in chunk[1:]:
            sent = sent + term[cells:].astype(F32)
        returned.append(exchange(sent, "seq", 1))
    grad_key, grad_value = call(
        functools.partial(key_back_kernel, head_dim, bounds, len(terms[0])),
        [((tok, lanes), BF16)] * 2,
        [key_rows, unmerge, key_row] + [term for chunk in terms for term in chunk] + returned,
        [((CORES, cells, 2 * width), F32) for width in widths],
    )
    return (
        attended_all[None],
        grad_query[None],
        grad_key[None],
        grad_value[None],
        gain_total[:head_dim],
        gain_total[head_dim:],
    )


def solution(mesh):
    rows = P("img", "seq", None)
    return jax.shard_map(
        local,
        mesh=mesh,
        in_specs=(rows, rows, rows, rows, P("img", "seq"), rows, P(), P()),
        out_specs=(rows, rows, rows, rows, P(), P()),
        check_vma=False,
    )
```

time: 168 us -> 57.9 us (0.34)
  blocking collectives: 38.7 us -> 0 us
  waiting for transfers between devices: 56.5 us -> 24.1 us
  local copies, waits for them, and re-layouts: 32.3 us -> 4.07 us
  other arithmetic: 18.8 us -> 0.09 us
  matrix products: 13.3 us -> 0 us
  starting transfers between devices: 6.36 us -> 18.3 us
  Pallas kernels: 0 us -> 10.4 us
    psum x1 -> x0, blocking collectives: 38.7 us -> none  [local(): lax.psum((gain_terms[0], gain_terms[1]), ('img', 'seq'))]
    ppermute x6 -> x15, waiting for transfers between devices: 56.5 us -> 24.1 us  [exchange(): lax.ppermute(array, axis, [(i, i ^ apart) for i in range(lax.axis_size(ax...]
    dot_general x10 -> x0, matrix products: 13.3 us -> none  [the longest x1 2.65 us: local(): jnp.dot(unmerge_table, grad_merged_k, precision=PRECISE) * 0.25]
    ppermute x6 -> x15, starting transfers between devices: 6.36 us -> 18.3 us  [exchange(): lax.ppermute(array, axis, [(i, i ^ apart) for i in range(lax.axis_size(ax...]
    pallas_call x0 -> x7, Pallas kernels: none -> 10.4 us  [call(): pl.pallas_call(kernel, out_shape=[jax.ShapeDtypeStruct(shape, kind) for s...]
    concatenate x6 -> x1, local copies, waits for them, and re-layouts: 8.18 us -> 0.01 us  [local(): block = jnp.concatenate([own, exchange(sent, 'seq', 1)], axis=0)]
    reduce_sum x9 -> x0, other arithmetic: 7.48 us -> none  [the longest x2 2.71 us: norm_back(): mean_inner = jnp.mean(grad_unit * unit_vals, axis=-1, keepdims=True)]
    mul x12 -> x0, local copies, waits for them, and re-layouts: 6.46 us -> none  [the longest x2 3.07 us: norm_back(): return row_scale * (grad_unit - unit_vals * mean_inner)]
  transfers between devices with their start and end apart: 6 -> 15, of which waited for: 6 -> 9; matrix products, arithmetic and copies ran while one was open for 6% -> 1% of each run, Pallas kernels for 0% -> 4%
where the time goes in v1:
time: 57.9 us; the launch traced here: 57.7 us
  waiting for transfers between devices  24.1 us (42%)
  starting transfers between devices  18.3 us (32%)
  Pallas kernels  10.4 us (18%)
  local copies, waits for them, and re-layouts  4.07 us (7%)
  between operations  0.72 us (1%)
    ppermute x15, waiting for transfers between devices, exchange(): lax.ppermute(array, axis, [(i, i ^ apart) for i in range(lax.axis_size(ax...  24.1 us
    ppermute x15, starting transfers between devices, exchange(): lax.ppermute(array, axis, [(i, i ^ apart) for i in range(lax.axis_size(ax...  18.3 us
    pallas_call x7, Pallas kernels, call(): pl.pallas_call(kernel, out_shape=[jax.ShapeDtypeStruct(shape, kind) for s...  10.4 us
    unnamed x17, local copies, waits for them, and re-layouts  2.57 us
  transfers between devices with their start and end apart: 15, of which 9 were waited for; matrix products, arithmetic and copies ran while one was open for 1% of the time, Pallas kernels for 4%

profile of v1, /device:TPU:0, one launch (start us, length us, event | category | flops | bytes accessed | tf_op | source)
XLA Modules:
  0.0 57.7 jit_solution(15217121964515941812)
XLA Ops:
  0.6 0.7 %tile.5 = f32[2,64]{1,0:T(2,128)S(1)} broadcast(f32[64]{0:T(128)} %param.15), dimensions={1} | broadcast | bytes 768 | tf_op jit(solution)/shard_map/tile | solution.py:351
  1.3 0.0 copy-start.6
  1.3 0.1 broadcast_in_dim_tile.7.gain_ref.refs_2_
  1.4 0.6 %copy-done.6 = s32[1,32,4]{1,2,0:T(4,128)S(1)} copy-done((s32[1,32,4]{1,2,0:T(4,128)S(1)}, s32[1,32,4]{1,2,0:T(4,128)}, u32[]{:S(2)}) %copy-start.6) | copy-done | bytes 536
  2.0 0.1 copy.14.cells_ref
  2.1 0.0 copy-start.2
  2.1 1.0 %copy-done.2 = bf16[1,128,1280]{2,1,0:T(8,128)(2,1)S(1)} copy-done((bf16[1,128,1280]{2,1,0:T(8,128)(2,1)S(1)}, bf16[1,128,1280]{2,1,0:T(8,128)(2,1)}, u32[]{:S(2)}) %copy-start.2) | copy-done | bytes 327704
  3.0 0.0 copy-start.4
  3.0 1.0 %copy-done.4 = bf16[1,128,1280]{2,1,0:T(8,128)(2,1)S(1)} copy-done((bf16[1,128,1280]{2,1,0:T(8,128)(2,1)S(1)}, bf16[1,128,1280]{2,1,0:T(8,128)(2,1)}, u32[]{:S(2)}) %copy-start.4) | copy-done | bytes 327704
  4.0 0.0 copy-start
  4.0 0.0 copy-start.1
  4.0 2.1 %shard_map.129 = (bf16[32,1280]{1,0:T(8,128)(2,1)S(1)}, bf16[32,1280]{1,0:T(8,128)(2,1)S(1)}) custom-call(bf16[128,1280]{1,0:T(8,128)(2,1)S(1)} %bitcast.18, bf16[128,1280]{1,0:T(8,128)(2,1)S(1)} %bitcast.20, s32[32,4]{1,0:T(8,128)S(1)} %copy.14.cells_ref, f32[1,128]{1,0:T(1,128)S(1)} %broadcast_in_dim_tile.7.gain_ref.refs_2_), custom_call_target="tpu_custom_call" | custom-call | tf_op jit(solution)/shard_map/pallas_call | solution.py:21
  6.1 0.5 collective-permute-start.1
  6.5 0.0 copy-done
  6.5 0.0 copy-done.1
  6.5 0.1 shard_map.127
  6.6 0.1 collective-permute-start
  6.7 0.0 copy-start.7
  6.7 0.7 %collective-permute-done.1 = bf16[32,1280]{1,0:T(8,128)(2,1)S(1)} collective-permute-done((bf16[32,1280]{1,0:T(8,128)(2,1)S(1)}, bf16[32,1280]{1,0:T(8,128)(2,1)S(1)}, u32[]{:S(2)}, u32[]{:S(2)}) %collective-permute-start.1) | collective-permute-done | bytes 81952 | tf_op jit(solution)/shard_map/ppermute | solution.py:303
  7.5 4.9 %collective-permute-start.3 = (bf16[64,1280]{1,0:T(8,128)(2,1)S(1)}, bf16[64,1280]{1,0:T(8,128)(2,1)S(1)}, u32[]{:S(2)}, u32[]{:S(2)}) collective-permute-start(bf16[64,1280]{1,0:T(8,128)(2,1)S(1)} %constant_dynamic-update-slice_fusion.refs_3_), channel_id=1, source_target_pairs={{0,6},{1,7},{2,4},{3,5},{4,2},{5,3},{6,0},{7,1},{8,14},{9,15},{10,... | collective-permute-start | bytes 491528 | tf_op jit(solution)/shard_map/ppermute | solution.py:303
  12.4 0.0 collective-permute-start.2
  12.4 5.0 %collective-permute-done.3.refs_6_ = bf16[64,1280]{1,0:T(8,128)(2,1)S(1)} collective-permute-done((bf16[64,1280]{1,0:T(8,128)(2,1)S(1)}, bf16[64,1280]{1,0:T(8,128)(2,1)S(1)}, u32[]{:S(2)}, u32[]{:S(2)}) %collective-permute-start.3) | collective-permute-done | bytes 163872 | tf_op jit(solution)/shard_map/ppermute | solution.py:303
  17.5 2.7 %collective-permute-start.4 = (bf16[64,1280]{1,0:T(8,128)(2,1)S(1)}, bf16[64,1280]{1,0:T(8,128)(2,1)S(1)}, u32[]{:S(2)}, u32[]{:S(2)}) collective-permute-start(bf16[64,1280]{1,0:T(8,128)(2,1)S(1)} %collective-permute-done.3.refs_6_), channel_id=1, source_target_pairs={{0,2},{1,3},{2,0},{3,1},{4,6},{5,7},{6,4},{7,5},{8,10},{9,11},{10,... | collective-permute-start | bytes 491528 | tf_op jit(solution)/shard_map/ppermute | solution.py:303
  20.2 0.0 copy-done.7
  20.2 0.1 broadcast_in_dim_tile.6.gain_ref
  20.3 0.0 collective-permute-done.arrived_ref
  20.3 0.4 shard_map.128
  20.6 0.0 collective-permute-done.2.refs_4_
  20.6 3.4 %collective-permute-done.4.refs_5_ = bf16[64,1280]{1,0:T(8,128)(2,1)S(1)} collective-permute-done((bf16[64,1280]{1,0:T(8,128)(2,1)S(1)}, bf16[64,1280]{1,0:T(8,128)(2,1)S(1)}, u32[]{:S(2)}, u32[]{:S(2)}) %collective-permute-start.4) | collective-permute-done | bytes 163872 | tf_op jit(solution)/shard_map/ppermute | solution.py:303
  24.1 3.4 %shard_map.130 = (bf16[256,640]{1,0:T(8,128)(2,1)S(1)}, f32[256,640]{1,0:T(8,128)S(1)}, f32[1,128]{1,0:T(1,128)S(1)}, f32[64,1280]{1,0:T(8,128)S(1)}, bf16[64,12...) custom-call(bf16[256,640]{1,0:T(8,128)(2,1)S(1)} %get-tuple-element.24.refs_0_, ...), custom_call_target="tpu_custom_call" | custom-call | tf_op jit(solution)/shard_map/pallas_call | solution.py:21
  27.4 1.7 %collective-permute-start.7 = (bf16[64,1280]{1,0:T(8,128)(2,1)S(1)}, bf16[64,1280]{1,0:T(8,128)(2,1)S(1)}, u32[]{:S(2)}, u32[]{:S(2)}) collective-permute-start(bf16[64,1280]{1,0:T(8,128)(2,1)S(1)} %get-tuple-element.38), channel_id=1, source_target_pairs={{0,2},{1,3},{2,0},{3,1},{4,6},{5,7},{6,4},{7,5},{8,10},{9,11},{10,... | collective-permute-start | bytes 491528 | tf_op jit(solution)/shard_map/ppermute | solution.py:303
  29.2 0.3 collective-permute-start.6
  29.5 4.7 %collective-permute-done.7 = bf16[64,1280]{1,0:T(8,128)(2,1)S(1)} collective-permute-done((bf16[64,1280]{1,0:T(8,128)(2,1)S(1)}, bf16[64,1280]{1,0:T(8,128)(2,1)S(1)}, u32[]{:S(2)}, u32[]{:S(2)}) %collective-permute-start.7) | collective-permute-done | bytes 163872 | tf_op jit(solution)/shard_map/ppermute | solution.py:303
  34.3 1.8 %collective-permute-start.8 = (bf16[64,1280]{1,0:T(8,128)(2,1)S(1)}, bf16[64,1280]{1,0:T(8,128)(2,1)S(1)}, u32[]{:S(2)}, u32[]{:S(2)}) collective-permute-start(bf16[64,1280]{1,0:T(8,128)(2,1)S(1)} %add_convert_fusion), channel_id=1, source_target_pairs={{0,6},{1,7},{2,4},{3,5},{4,2},{5,3},{6,0},{7,1},{8,14},{9,15},{10,... | collective-permute-start | bytes 491528 | tf_op jit(solution)/shard_map/ppermute | solution.py:303
  36.1 0.8 %shard_map.131 = (bf16[128,1280]{1,0:T(8,128)(2,1)S(1)}, bf16[128,1280]{1,0:T(8,128)(2,1)S(1)}, f32[1,128]{1,0:T(1,128)S(1)}) custom-call(bf16[128,1280]{1,0:T(8,128)(2,1)S(1)} %bitcast.15, bf16[128,1280]{1,0:T(8,128)(2,1)S(1)} %collective-permute-done.arrived_ref, f32[1,128]{1,0:T(1,128)S(1)} %broadcast_in_dim_tile.6.gain_ref, ...), custom_call_target="tpu_custom_call" | custom-call | tf_op jit(solution)/shard_map/pallas_call | solution.py:21
  36.8 0.1 collective-permute-start.10
  36.9 1.1 %collective-permute-done.10 = f32[1,128]{1,0:T(1,128)S(1)} collective-permute-done((f32[1,128]{1,0:T(1,128)S(1)}, f32[1,128]{1,0:T(1,128)S(1)}, u32[]{:S(2)}, u32[]{:S(2)}) %collective-permute-start.10) | collective-permute-done | bytes 544 | tf_op jit(solution)/shard_map/ppermute | solution.py:303
  38.0 1.4 %collective-permute-start.11 = (f32[1,128]{1,0:T(1,128)S(1)}, f32[1,128]{1,0:T(1,128)S(1)}, u32[]{:S(2)}, u32[]{:S(2)}) collective-permute-start(f32[1,128]{1,0:T(1,128)S(1)} %add.27), channel_id=1, source_target_pairs={{0,2},{1,3},{2,0},{3,1},{4,6},{5,7},{6,4},{7,5},{8,10},{9,11},{10,... | collective-permute-start | bytes 1544 | tf_op jit(solution)/shard_map/ppermute | solution.py:303
  39.4 2.1 %collective-permute-done.11 = f32[1,128]{1,0:T(1,128)S(1)} collective-permute-done((f32[1,128]{1,0:T(1,128)S(1)}, f32[1,128]{1,0:T(1,128)S(1)}, u32[]{:S(2)}, u32[]{:S(2)}) %collective-permute-start.11) | collective-permute-done | bytes 544 | tf_op jit(solution)/shard_map/ppermute | solution.py:303
  41.6 1.6 %collective-permute-start.12 = (f32[1,128]{1,0:T(1,128)S(1)}, f32[1,128]{1,0:T(1,128)S(1)}, u32[]{:S(2)}, u32[]{:S(2)}) collective-permute-start(f32[1,128]{1,0:T(1,128)S(1)} %add.28), channel_id=1, source_target_pairs={{0,4},{1,5},{2,6},{3,7},{4,0},{5,1},{6,2},{7,3},{8,12},{9,13},{10,... | collective-permute-start | bytes 1544 | tf_op jit(solution)/shard_map/ppermute | solution.py:303
  43.2 2.8 %collective-permute-done.12 = f32[1,128]{1,0:T(1,128)S(1)} collective-permute-done((f32[1,128]{1,0:T(1,128)S(1)}, f32[1,128]{1,0:T(1,128)S(1)}, u32[]{:S(2)}, u32[]{:S(2)}) %collective-permute-start.12) | collective-permute-done | bytes 544 | tf_op jit(solution)/shard_map/ppermute | solution.py:303
  46.0 1.5 %collective-permute-start.13 = (f32[1,128]{1,0:T(1,128)S(1)}, f32[1,128]{1,0:T(1,128)S(1)}, u32[]{:S(2)}, u32[]{:S(2)}) collective-permute-start(f32[1,128]{1,0:T(1,128)S(1)} %add.29), channel_id=1, source_target_pairs={{0,8},{8,0},{16,24},{24,16},{1,9},{9,1},{17,25},{25,17},{2,10},{10... | collective-permute-start | bytes 1544 | tf_op jit(solution)/shard_map/ppermute | solution.py:303
  47.5 2.1 %collective-permute-done.13 = f32[1,128]{1,0:T(1,128)S(1)} collective-permute-done((f32[1,128]{1,0:T(1,128)S(1)}, f32[1,128]{1,0:T(1,128)S(1)}, u32[]{:S(2)}, u32[]{:S(2)}) %collective-permute-start.13) | collective-permute-done | bytes 544 | tf_op jit(solution)/shard_map/ppermute | solution.py:303
  49.6 1.5 %collective-permute-start.14 = (f32[1,128]{1,0:T(1,128)S(1)}, f32[1,128]{1,0:T(1,128)S(1)}, u32[]{:S(2)}, u32[]{:S(2)}) collective-permute-start(f32[1,128]{1,0:T(1,128)S(1)} %add.30), channel_id=1, source_target_pairs={{0,16},{8,24},{16,0},{24,8},{1,17},{9,25},{17,1},{25,9},{2,18},{10... | collective-permute-start | bytes 1544 | tf_op jit(solution)/shard_map/ppermute | solution.py:303
  51.1 0.0 collective-permute-start.5
  51.1 2.0 %collective-permute-done.14 = f32[1,128]{1,0:T(1,128)S(1)} collective-permute-done((f32[1,128]{1,0:T(1,128)S(1)}, f32[1,128]{1,0:T(1,128)S(1)}, u32[]{:S(2)}, u32[]{:S(2)}) %collective-permute-start.14) | collective-permute-done | bytes 544 | tf_op jit(solution)/shard_map/ppermute | solution.py:303
  53.1 0.0 collective-permute-done.6.refs_1_
  53.1 0.0 collective-permute-done.8.refs_2_
  53.2 0.1 collective-permute-start.9
  53.2 0.6 %slice_bitcast_fusion = (f32[64]{0:T(128)}, f32[64]{0:T(128)}) fusion(f32[1,128]{1,0:T(1,128)S(1)} %add.31), kind=kLoop, calls=%fused_computation.4 | loop fusion | bytes 1024 | tf_op jit(solution)/shard_map/slice | solution.py:421
  53.8 0.0 collective-permute-done.5.arrived_ref
  53.8 0.0 copy-start.3
  53.8 0.0 copy-start.5
  53.8 1.0 %shard_map.132 = (bf16[128,1280]{1,0:T(8,128)(2,1)}, bf16[128,1280]{1,0:T(8,128)(2,1)}) custom-call(bf16[128,1280]{1,0:T(8,128)(2,1)S(1)} %get-tuple-element.31.own_ref, bf16[128,1280]{1,0:T(8,128)(2,1)S(1)} %collective-permute-done.5.arrived_ref), custom_call_target="tpu_custom_call" | custom-call | tf_op jit(solution)/shard_map/pallas_call | solution.py:21
  54.8 0.0 collective-permute-done.9.refs_3_
  54.8 0.0 copy-done.3
  54.8 0.0 copy-done.5
  54.8 2.9 %shard_map.133 = (bf16[128,1280]{1,0:T(8,128)(2,1)}, bf16[128,1280]{1,0:T(8,128)(2,1)}) custom-call(bf16[128,1280]{1,0:T(8,128)(2,1)S(1)} %bitcast.19, s32[1,128]{1,0:T(1,128)S(1)} %copy-done.5, f32[1,128]{1,0:T(1,128)S(1)} %broadcast_in_dim_tile.7.gain_ref.refs_2_, f32[64,1280]{1,0:T(8,128)S(1)} %get-tuple-element.35.refs_0_, ...), custom_call_target="tpu_custom_call" | custom-call | tf_op jit(solution)/shard_map/pallas_call | solution.py:21
  (10 shorter events, 0.1 us)
Async XLA Ops:
  1.3 0.7 %copy-start.6 = (s32[1,32,4]{1,2,0:T(4,128)S(1)}, s32[1,32,4]{1,2,0:T(4,128)}, u32[]{:S(2)}) copy-start(s32[1,32,4]{1,2,0:T(4,128)} %param.11) | copy-start | bytes 1540
  2.1 1.0 %copy-start.2 = (bf16[1,128,1280]{2,1,0:T(8,128)(2,1)S(1)}, bf16[1,128,1280]{2,1,0:T(8,128)(2,1)}, u32[]{:S(2)}) copy-start(bf16[1,128,1280]{2,1,0:T(8,128)(2,1)} %param.9) | copy-start | bytes 983044
  3.0 1.0 %copy-start.4 = (bf16[1,128,1280]{2,1,0:T(8,128)(2,1)S(1)}, bf16[1,128,1280]{2,1,0:T(8,128)(2,1)}, u32[]{:S(2)}) copy-start(bf16[1,128,1280]{2,1,0:T(8,128)(2,1)} %param.10) | copy-start | bytes 983044
  4.0 2.5 %copy-start = (bf16[1,128,1280]{2,1,0:T(8,128)(2,1)S(1)}, bf16[1,128,1280]{2,1,0:T(8,128)(2,1)}, u32[]{:S(2)}) copy-start(bf16[1,128,1280]{2,1,0:T(8,128)(2,1)} %param.8) | copy-start | bytes 983044
  4.0 2.5 %copy-start.1 = (bf16[1,128,1280]{2,1,0:T(8,128)(2,1)S(1)}, bf16[1,128,1280]{2,1,0:T(8,128)(2,1)}, u32[]{:S(2)}) copy-start(bf16[1,128,1280]{2,1,0:T(8,128)(2,1)} %param.13) | copy-start | bytes 983044
  6.1 1.4 %collective-permute-start.1 = (bf16[32,1280]{1,0:T(8,128)(2,1)S(1)}, bf16[32,1280]{1,0:T(8,128)(2,1)S(1)}, u32[]{:S(2)}, u32[]{:S(2)}) collective-permute-start(bf16[32,1280]{1,0:T(8,128)(2,1)S(1)} %get-tuple-element.27), channel_id=1, source_target_pairs={{0,1},{1,0},{2,3},{3,2},{4,5},{5,4},{6,7},{7,6},{8,9},{9,8},{10,11... | collective-permute-start | bytes 245768 | tf_op jit(solution)/shard_map/ppermute | solution.py:303
  6.6 13.6 %collective-permute-start = (bf16[128,1280]{1,0:T(8,128)(2,1)S(1)}, bf16[128,1280]{1,0:T(8,128)(2,1)S(1)}, u32[]{:S(2)}, u32[]{:S(2)}) collective-permute-start(bf16[128,1280]{1,0:T(8,128)(2,1)S(1)} %shard_map.127), channel_id=1, source_target_pairs={{0,1},{1,0},{2,3},{3,2},{4,5},{5,4},{6,7},{7,6},{8,9},{9,8},{10,11... | collective-permute-start | bytes 983048 | tf_op jit(solution)/shard_map/ppermute | solution.py:303
  6.7 13.4 %copy-start.7 = (f32[64]{0:T(128)S(1)}, f32[64]{0:T(128)}, u32[]{:S(2)}) copy-start(f32[64]{0:T(128)} %param.14) | copy-start | bytes 772
  7.5 10.0 %collective-permute-start.3 = (bf16[64,1280]{1,0:T(8,128)(2,1)S(1)}, bf16[64,1280]{1,0:T(8,128)(2,1)S(1)}, u32[]{:S(2)}, u32[]{:S(2)}) collective-permute-start(bf16[64,1280]{1,0:T(8,128)(2,1)S(1)} %constant_dynamic-update-slice_fusion.refs_3_), channel_id=1, source_target_pairs={{0,6},{1,7},{2,4},{3,5},{4,2},{5,3},{6,0},{7,1},{8,14},{9,15},{10,... | collective-permute-start | bytes 491528 | tf_op jit(solution)/shard_map/ppermute | solution.py:303
  12.4 8.2 %collective-permute-start.2 = (bf16[64,1280]{1,0:T(8,128)(2,1)S(1)}, bf16[64,1280]{1,0:T(8,128)(2,1)S(1)}, u32[]{:S(2)}, u32[]{:S(2)}) collective-permute-start(bf16[64,1280]{1,0:T(8,128)(2,1)S(1)} %constant_dynamic-update-slice_fusion.refs_3_), channel_id=1, source_target_pairs={{0,2},{1,3},{2,0},{3,1},{4,6},{5,7},{6,4},{7,5},{8,10},{9,11},{10,... | collective-permute-start | bytes 491528 | tf_op jit(solution)/shard_map/ppermute | solution.py:303
  17.5 6.6 %collective-permute-start.4 = (bf16[64,1280]{1,0:T(8,128)(2,1)S(1)}, bf16[64,1280]{1,0:T(8,128)(2,1)S(1)}, u32[]{:S(2)}, u32[]{:S(2)}) collective-permute-start(bf16[64,1280]{1,0:T(8,128)(2,1)S(1)} %collective-permute-done.3.refs_6_), channel_id=1, source_target_pairs={{0,2},{1,3},{2,0},{3,1},{4,6},{5,7},{6,4},{7,5},{8,10},{9,11},{10,... | collective-permute-start | bytes 491528 | tf_op jit(solution)/shard_map/ppermute | solution.py:303
  27.4 6.8 %collective-permute-start.7 = (bf16[64,1280]{1,0:T(8,128)(2,1)S(1)}, bf16[64,1280]{1,0:T(8,128)(2,1)S(1)}, u32[]{:S(2)}, u32[]{:S(2)}) collective-permute-start(bf16[64,1280]{1,0:T(8,128)(2,1)S(1)} %get-tuple-element.38), channel_id=1, source_target_pairs={{0,2},{1,3},{2,0},{3,1},{4,6},{5,7},{6,4},{7,5},{8,10},{9,11},{10,... | collective-permute-start | bytes 491528 | tf_op jit(solution)/shard_map/ppermute | solution.py:303
  29.2 23.9 %collective-permute-start.6 = (bf16[64,1280]{1,0:T(8,128)(2,1)S(1)}, bf16[64,1280]{1,0:T(8,128)(2,1)S(1)}, u32[]{:S(2)}, u32[]{:S(2)}) collective-permute-start(bf16[64,1280]{1,0:T(8,128)(2,1)S(1)} %get-tuple-element.36), channel_id=1, source_target_pairs={{0,2},{1,3},{2,0},{3,1},{4,6},{5,7},{6,4},{7,5},{8,10},{9,11},{10,... | collective-permute-start | bytes 491528 | tf_op jit(solution)/shard_map/ppermute | solution.py:303
  34.3 18.8 %collective-permute-start.8 = (bf16[64,1280]{1,0:T(8,128)(2,1)S(1)}, bf16[64,1280]{1,0:T(8,128)(2,1)S(1)}, u32[]{:S(2)}, u32[]{:S(2)}) collective-permute-start(bf16[64,1280]{1,0:T(8,128)(2,1)S(1)} %add_convert_fusion), channel_id=1, source_target_pairs={{0,6},{1,7},{2,4},{3,5},{4,2},{5,3},{6,0},{7,1},{8,14},{9,15},{10,... | collective-permute-start | bytes 491528 | tf_op jit(solution)/shard_map/ppermute | solution.py:303
  36.8 1.2 %collective-permute-start.10 = (f32[1,128]{1,0:T(1,128)S(1)}, f32[1,128]{1,0:T(1,128)S(1)}, u32[]{:S(2)}, u32[]{:S(2)}) collective-permute-start(f32[1,128]{1,0:T(1,128)S(1)} %get-tuple-element.41), channel_id=1, source_target_pairs={{0,1},{1,0},{2,3},{3,2},{4,5},{5,4},{6,7},{7,6},{8,9},{9,8},{10,11... | collective-permute-start | bytes 1544 | tf_op jit(solution)/shard_map/ppermute | solution.py:303
  38.0 3.5 %collective-permute-start.11 = (f32[1,128]{1,0:T(1,128)S(1)}, f32[1,128]{1,0:T(1,128)S(1)}, u32[]{:S(2)}, u32[]{:S(2)}) collective-permute-start(f32[1,128]{1,0:T(1,128)S(1)} %add.27), channel_id=1, source_target_pairs={{0,2},{1,3},{2,0},{3,1},{4,6},{5,7},{6,4},{7,5},{8,10},{9,11},{10,... | collective-permute-start | bytes 1544 | tf_op jit(solution)/shard_map/ppermute | solution.py:303
  41.6 4.4 %collective-permute-start.12 = (f32[1,128]{1,0:T(1,128)S(1)}, f32[1,128]{1,0:T(1,128)S(1)}, u32[]{:S(2)}, u32[]{:S(2)}) collective-permute-start(f32[1,128]{1,0:T(1,128)S(1)} %add.28), channel_id=1, source_target_pairs={{0,4},{1,5},{2,6},{3,7},{4,0},{5,1},{6,2},{7,3},{8,12},{9,13},{10,... | collective-permute-start | bytes 1544 | tf_op jit(solution)/shard_map/ppermute | solution.py:303
  46.0 3.5 %collective-permute-start.13 = (f32[1,128]{1,0:T(1,128)S(1)}, f32[1,128]{1,0:T(1,128)S(1)}, u32[]{:S(2)}, u32[]{:S(2)}) collective-permute-start(f32[1,128]{1,0:T(1,128)S(1)} %add.29), channel_id=1, source_target_pairs={{0,8},{8,0},{16,24},{24,16},{1,9},{9,1},{17,25},{25,17},{2,10},{10... | collective-permute-start | bytes 1544 | tf_op jit(solution)/shard_map/ppermute | solution.py:303
  49.6 3.5 %collective-permute-start.14 = (f32[1,128]{1,0:T(1,128)S(1)}, f32[1,128]{1,0:T(1,128)S(1)}, u32[]{:S(2)}, u32[]{:S(2)}) collective-permute-start(f32[1,128]{1,0:T(1,128)S(1)} %add.30), channel_id=1, source_target_pairs={{0,16},{8,24},{16,0},{24,8},{1,17},{9,25},{17,1},{25,9},{2,18},{10... | collective-permute-start | bytes 1544 | tf_op jit(solution)/shard_map/ppermute | solution.py:303
  51.1 2.7 %collective-permute-start.5 = (bf16[128,1280]{1,0:T(8,128)(2,1)S(1)}, bf16[128,1280]{1,0:T(8,128)(2,1)S(1)}, u32[]{:S(2)}, u32[]{:S(2)}) collective-permute-start(bf16[128,1280]{1,0:T(8,128)(2,1)S(1)} %get-tuple-element.32), channel_id=1, source_target_pairs={{0,1},{1,0},{2,3},{3,2},{4,5},{5,4},{6,7},{7,6},{8,9},{9,8},{10,11... | collective-permute-start | bytes 983048 | tf_op jit(solution)/shard_map/ppermute | solution.py:303
  53.2 1.6 %collective-permute-start.9 = (f32[32,1280]{1,0:T(8,128)S(1)}, f32[32,1280]{1,0:T(8,128)S(1)}, u32[]{:S(2)}, u32[]{:S(2)}) collective-permute-start(f32[32,1280]{1,0:T(8,128)S(1)} %convert_add_fusion), channel_id=1, source_target_pairs={{0,1},{1,0},{2,3},{3,2},{4,5},{5,4},{6,7},{7,6},{8,9},{9,8},{10,11... | collective-permute-start | bytes 491528 | tf_op jit(solution)/shard_map/ppermute | solution.py:303
  53.8 1.0 %copy-start.3 = (bf16[1,128,1280]{2,1,0:T(8,128)(2,1)S(1)}, bf16[1,128,1280]{2,1,0:T(8,128)(2,1)}, u32[]{:S(2)}) copy-start(bf16[1,128,1280]{2,1,0:T(8,128)(2,1)} %param.9) | copy-start | bytes 983044
  53.8 1.0 %copy-start.5 = (s32[1,128]{1,0:T(1,128)S(1)}, s32[1,128]{1,0:T(1,128)}, u32[]{:S(2)}) copy-start(s32[1,128]{1,0:T(1,128)} %unmerge_ref.1) | copy-start | bytes 1540

commit v2 on v1

v2 whole, which is shorter than its diff:
```python
import functools
import math

import jax
import jax.numpy as jnp
from jax import lax
from jax.experimental import pallas as pl
from jax.experimental.pallas import tpu as pltpu
from jax.sharding import PartitionSpec as P

EPSILON = 1e-06
TILE = 128
CORES = 2
BF16 = jnp.bfloat16
F32 = jnp.float32
VMEM_BYTES = 40 * 1024 * 1024
ALL_VMEM_BYTES = 62 * 1024 * 1024


def call(kernel, out_shapes, inputs, scratch=(), far_in=0, far_out=0, copies=0, aliases=None, vmem=VMEM_BYTES, micros=1.0):
    near, far = pl.BlockSpec(memory_space=pltpu.VMEM), pl.BlockSpec(memory_space=pltpu.HBM)
    buffers = [pltpu.VMEM(shape, kind) for shape, kind in scratch]
    if copies:
        buffers.append(pltpu.SemaphoreType.DMA((copies,)))
    return pl.pallas_call(
        kernel,
        out_shape=[jax.ShapeDtypeStruct(shape, kind) for shape, kind in out_shapes],
        in_specs=[far] * far_in + [near] * (len(inputs) - far_in),
        out_specs=[far] * far_out + [near] * (len(out_shapes) - far_out),
        scratch_shapes=buffers,
        input_output_aliases=aliases or {},
        cost_estimate=pl.CostEstimate(
            flops=int(micros * 1e9), bytes_accessed=int(micros * 2e6), transcendentals=0
        ),
        compiler_params=pltpu.CompilerParams(vmem_limit_bytes=vmem),
    )(*inputs)


def core_side():
    return lax.rem(lax.axis_index("seq"), CORES)


def lanes_at(index, width=TILE):
    return pl.ds(pl.multiple_of(index * TILE, TILE), width)


def pieces(width):
    return [(at, min(at + 2 * TILE, width)) for at in range(0, width, 2 * TILE)]


def dot(left, right, contract=((1,), (0,))):
    return lax.dot_general(left, right, (contract, ((), ())), preferred_element_type=F32)


def halves(array):
    high = array.astype(BF16)
    return high, (array - high.astype(F32)).astype(BF16)


def over_heads(array, head_dim, finish):
    head = lax.broadcasted_iota(jnp.int32, (1, TILE), 1) // head_dim
    tiles = []
    for at in range(0, array.shape[1], TILE):
        tile = array[:, at : at + TILE]
        result = None
        for index in range(TILE // head_dim):
            total = jnp.sum(jnp.where(head == index, tile, 0.0), axis=1, keepdims=True)
            value = finish(total * (1.0 / head_dim))
            result = value if result is None else jnp.where(head == index, value, result)
        tiles.append(jnp.broadcast_to(result, tile.shape))
    return jnp.concatenate(tiles, axis=1)


def unit_rows(array, head_dim):
    scale = over_heads(array * array, head_dim, lambda mean: lax.rsqrt(mean + EPSILON))
    return array * scale, scale


def norm_back(grad_normed, unit_vals, scale, gain_row, head_dim):
    grad_unit = grad_normed * gain_row
    mean_inner = over_heads(grad_unit * unit_vals, head_dim, lambda mean: mean)
    return scale * (grad_unit - unit_vals * mean_inner)


def gain_lanes(gain_ref, width):
    row = gain_ref[...]
    return jnp.concatenate([row] * (width // row.shape[1]), axis=1)


def merge_kernel(head_dim, bounds, key_ref, value_ref, cells_ref, gain_ref, *refs):
    count = len(bounds)
    own_refs, send_refs = refs[:count], refs[count : 2 * count]
    key_buf, value_buf, cells_buf, gain_buf, copied = refs[2 * count :]
    tok, lanes = key_buf.shape
    half = lanes // CORES
    cells = cells_ref.shape[1]
    side = core_side()
    small = [
        pltpu.make_async_copy(cells_ref, cells_buf, copied.at[0]),
        pltpu.make_async_copy(gain_ref, gain_buf, copied.at[1]),
    ]
    for move in small:
        move.start()
    spans = [
        (other, chunk, start, stop, start + at, start + to)
        for other in (1, 0)
        for chunk, (start, stop) in enumerate(bounds)
        for at, to in pieces(stop - start)
    ]
    moves = []
    for index, (other, _, _, _, at, to) in enumerate(spans):
        source = lanes_at((1 - side if other else side) * (half // TILE) + at // TILE, to - at)
        here = slice(other * half + at, other * half + to)
        for which, (far, near) in enumerate(((key_ref, key_buf), (value_ref, value_buf))):
            move = pltpu.make_async_copy(
                far.at[:, source], near.at[:, here], copied.at[2 + 2 * index + which]
            )
            move.start()
            moves.append(move)
    for move in small:
        move.wait()
    listed = lax.rem(cells_buf[...], tok)
    ids = lax.broadcasted_iota(jnp.int32, (tok, cells), 0)
    member = sum((listed[j : j + 1] == ids).astype(F32) for j in range(cells_ref.shape[0]))
    member = member.T.astype(BF16)
    twice = jnp.concatenate([member, member], axis=1)
    for index, (other, chunk, start, stop, at, to) in enumerate(spans):
        here = slice(other * half + at, other * half + to)
        out_ref = (send_refs if other else own_refs)[chunk]
        if index % (len(spans) // CORES) == 0:
            for move in moves[2 * index : 2 * index + 2 * len(spans) // CORES]:
                move.wait()
        unit_vals, _ = unit_rows(key_buf[:, here].astype(F32), head_dim)
        keys = dot(twice, jnp.concatenate(halves(unit_vals), axis=0))
        keys *= gain_lanes(gain_buf, to - at) * 0.25
        out_ref[:, at - start : to - start] = keys.astype(BF16)
        values = dot(member, value_buf[:, here]) * 0.25
        out_ref[:, stop - 2 * start + at : stop - 2 * start + to] = values.astype(BF16)


def pack_kernel(query_ref, upstream_ref, send_ref, copied):
    half = query_ref.shape[1] // CORES
    source = lanes_at((1 - core_side()) * (half // TILE), half)
    moves = [
        pltpu.make_async_copy(query_ref.at[:, source], send_ref.at[:, :half], copied.at[0]),
        pltpu.make_async_copy(upstream_ref.at[:, source], send_ref.at[:, half:], copied.at[1]),
    ]
    for move in moves:
        move.start()
    for move in moves:
        move.wait()


def query_kernel(
    head_dim, query_ref, upstream_ref, arrived_ref, gain_ref, raw_ref, out_ref, grad_ref, copied
):
    tok, lanes = query_ref.shape
    half = lanes // CORES
    source = lanes_at(core_side() * (half // TILE), half)
    moves = [
        pltpu.make_async_copy(query_ref.at[:, source], raw_ref.at[:tok], copied.at[0]),
        pltpu.make_async_copy(upstream_ref.at[:, source], grad_ref.at[:tok], copied.at[1]),
    ]
    for move in moves:
        move.start()
    raw_ref[tok:] = arrived_ref[:, :half]
    grad_ref[tok:] = arrived_ref[:, half:]
    moves[0].wait()
    for at, to in pieces(half):
        unit_vals, _ = unit_rows(raw_ref[:, at:to].astype(F32), head_dim)
        out_ref[:, at:to] = (unit_vals * gain_lanes(gain_ref, to - at)).astype(BF16)
    moves[1].wait()


def attend_kernel(head_dim, start, blocks, group, *refs):
    query_ref, upstream_ref, query_gain_ref, key_gain_ref = refs[:4]
    block_refs = refs[4 : 4 + blocks]
    attended_ref, grad_ref, gain_out_ref = refs[4 + blocks : 7 + blocks]
    part_refs = refs[7 + blocks :]
    rows = query_ref.shape[0]
    block_rows, width = block_refs[0].shape
    width = width // 2
    per = TILE // head_dim
    cells = group * block_rows
    scale = head_dim**-0.5
    exponent = scale * math.log2(math.e)
    lane_head = lax.broadcasted_iota(jnp.int32, (1, TILE), 1) // head_dim
    cell_heads = lax.broadcasted_iota(jnp.int32, (cells, TILE), 1) // head_dim
    masks = [(cell_heads == head).astype(F32).astype(BF16) for head in range(per)]

    def spread(array):
        return jnp.concatenate([array * mask for mask in masks], axis=0)

    def by_lane(parts):
        result = parts[0]
        for head in range(1, per):
            result = jnp.where(lane_head == head, parts[head], result)
        return result

    def folded(array):
        return by_lane([array[head * cells : (head + 1) * cells] for head in range(per)])

    def one_tile(tile, sums):
        query_sum, key_sum = sums
        lane = lanes_at(tile)
        value_lane = lanes_at(width // TILE + tile)
        source = lanes_at(start // TILE + tile)
        queries = query_ref[:, source]
        upstream = upstream_ref[:, source]
        weighted = jnp.zeros((rows, TILE), F32)
        totals = [jnp.zeros((rows, 1), F32) for _ in range(per)]
        held = []
        for first in range(0, blocks, group):
            members = block_refs[first : first + group]
            keys = jnp.concatenate([ref[:, lane] for ref in members], axis=0)
            spread_keys = spread(keys)
            spread_values = spread(
                jnp.concatenate([ref[:, value_lane] for ref in members], axis=0)
            )
            scores = dot(queries, spread_keys, ((1,), (1,)))
            exp_scores = jnp.exp2(scores * exponent)
            weighted += dot(exp_scores.astype(BF16), spread_values)
            exp_parts = [exp_scores[:, h * cells : (h + 1) * cells] for h in range(per)]
            totals = [
                total + jnp.sum(part, axis=1, keepdims=True)
                for total, part in zip(totals, exp_parts)
            ]
            held.append((keys, spread_keys, spread_values, exp_parts))
        inverses = [1.0 / total for total in totals]
        attended = (weighted * by_lane(inverses)).astype(BF16)
        attended_ref[:, lane] = attended
        products = upstream.astype(F32) * attended.astype(F32)
        inners = [
            jnp.sum(jnp.where(lane_head == h, products, 0.0), axis=1, keepdims=True)
            for h in range(per)
        ]
        grad_queries = jnp.zeros((rows, TILE), F32)
        for index, (keys, spread_keys, spread_values, exp_parts) in enumerate(held):
            grad_weights = dot(upstream, spread_values, ((1,), (1,)))
            attention = [part * inverse for part, inverse in zip(exp_parts, inverses)]
            grad_scores = jnp.concatenate(
                [
                    (attention[h] * (grad_weights[:, h * cells : (h + 1) * cells] - inners[h]))
                    .astype(BF16)
                    for h in range(per)
                ],
                axis=1,
            )
            attention_bf = jnp.concatenate([part.astype(BF16) for part in attention], axis=1)
            grad_queries += dot(grad_scores, spread_keys)
            grad_keys = folded(dot(grad_scores, queries, ((0,), (0,)))) * scale
            grad_values = folded(dot(attention_bf, upstream, ((0,), (0,))))
            key_sum += jnp.sum(grad_keys * keys.astype(F32), axis=0, keepdims=True)
            for member in range(group):
                ref = part_refs[index * group + member]
                here = slice(member * block_rows, (member + 1) * block_rows)
                ref[:, lane] = grad_keys[here].astype(ref.dtype)
                ref[:, value_lane] = grad_values[here].astype(ref.dtype)
        grad_queries *= scale
        grad_ref[:, lane] = grad_queries
        query_sum += jnp.sum(grad_queries * queries.astype(F32), axis=0, keepdims=True)
        return query_sum, key_sum

    sums = (jnp.zeros((1, TILE), F32), jnp.zeros((1, TILE), F32))
    if blocks == group:
        for tile in range(width // TILE):
            sums = one_tile(tile, sums)
    else:
        sums = lax.fori_loop(0, width // TILE, one_tile, sums)

    def per_channel(row):
        return sum(row[:, at : at + head_dim] for at in range(0, TILE, head_dim))

    gain_out_ref[...] = jnp.concatenate(
        [
            per_channel(sums[0]) / query_gain_ref[...],
            per_channel(sums[1]) / key_gain_ref[...],
        ],
        axis=1,
    )


def query_back_kernel(head_dim, bounds, raw_ref, gain_ref, *refs):
    count = len(bounds)
    attended_refs, grad_refs = refs[:count], refs[count : 2 * count]
    attended_out, grad_out, send_ref, attended_buf, grad_buf, copied = refs[2 * count :]
    tok, half = attended_buf.shape
    for (start, stop), attended_ref, grad_ref in zip(bounds, attended_refs, grad_refs):
        attended_buf[:, start:stop] = attended_ref[:tok]
        send_ref[:, start:stop] = attended_ref[tok:]
        for at, to in pieces(stop - start):
            lane = slice(start + at, start + to)
            unit_vals, scale = unit_rows(raw_ref[:, lane].astype(F32), head_dim)
            grads = norm_back(
                grad_ref[:, at:to], unit_vals, scale, gain_lanes(gain_ref, to - at), head_dim
            ).astype(BF16)
            grad_buf[:, lane] = grads[:tok]
            send_ref[:, half + start + at : half + start + to] = grads[tok:]
    place = lanes_at(core_side() * (half // TILE), half)
    moves = [
        pltpu.make_async_copy(attended_buf, attended_out.at[:, place], copied.at[0]),
        pltpu.make_async_copy(grad_buf, grad_out.at[:, place], copied.at[1]),
    ]
    for move in moves:
        move.start()
    for move in moves:
        move.wait()


def place_kernel(attended_in, grad_in, arrived_ref, attended_out, grad_out, copied):
    half = arrived_ref.shape[1] // 2
    place = lanes_at((1 - core_side()) * (half // TILE), half)
    moves = [
        pltpu.make_async_copy(arrived_ref.at[:, :half], attended_out.at[:, place], copied.at[0]),
        pltpu.make_async_copy(arrived_ref.at[:, half:], grad_out.at[:, place], copied.at[1]),
    ]
    for move in moves:
        move.start()
    for move in moves:
        move.wait()


def key_back_kernel(bounds, terms, other, *refs):
    count = len(bounds)
    if other:
        refs = refs[2:]
    key_ref, unmerge_ref, gain_ref = refs[:3]
    term_refs = [refs[3 + chunk * terms : 3 + (chunk + 1) * terms] for chunk in range(count)]
    grad_key_out, grad_value_out, grad_key_buf, grad_value_buf, copied = refs[3 + count * terms :]
    tok, half = grad_key_buf.shape
    cells = term_refs[0][0].shape[0] // (1 if other else CORES)
    side = core_side()
    first = (1 - side if other else side) * (half // TILE)
    owner = lax.rem(unmerge_ref[...], cells)
    table = (lax.broadcasted_iota(jnp.int32, (cells, tok), 0) == owner).astype(F32)
    table = table.T.astype(BF16)
    twice = jnp.concatenate([table, table], axis=1)

    def spread(chunk, at, to):
        result = term_refs[chunk][0][:cells, at:to].astype(F32)
        for ref in term_refs[chunk][1:]:
            result += ref[:cells, at:to].astype(F32)
        return dot(twice, jnp.concatenate(halves(result), axis=0)) * 0.25

    spans = [
        (chunk, start, stop, start + at, start + to)
        for chunk, (start, stop) in enumerate(bounds)
        for at, to in pieces(stop - start)
    ]
    moves = []

    def send(index, buf, out):
        move = pltpu.make_async_copy(buf, out.at[:, lanes_at(first, half)], copied.at[index])
        move.start()
        moves.append(move)

    for chunk, start, stop, at, to in spans:
        grad_value_buf[:, at:to] = spread(chunk, stop - 2 * start + at, stop - 2 * start + to).astype(
            BF16
        )
    send(0, grad_value_buf, grad_value_out)
    for chunk, start, stop, at, to in spans:
        keys = key_ref[:, lanes_at(first + at // TILE, to - at)].astype(F32)
        unit_vals, scale = unit_rows(keys, gain_ref.shape[1])
        grad_key_buf[:, at:to] = norm_back(
            spread(chunk, at - start, to - start),
            unit_vals,
            scale,
            gain_lanes(gain_ref, to - at),
            gain_ref.shape[1],
        ).astype(BF16)
    send(1, grad_key_buf, grad_key_out)
    for move in moves:
        move.wait()


def exchange(array, axis, apart):
    return lax.ppermute(array, axis, [(i, i ^ apart) for i in range(lax.axis_size(axis))])


def chip_gather(block, chips):
    if chips == 1:
        return [block]
    mirrored = exchange(block, "seq", CORES * (chips - 1))
    return chip_gather(block, chips // 2) + chip_gather(mirrored, chips // 2)[::-1]


def chip_reduce(parts, between):
    chips = len(parts)
    if chips == 1:
        return [parts[0]]
    high = chip_reduce(parts[: chips // 2 - 1 : -1], between)
    if len(high) > 1:
        high = [high[0]] + between(high[1:])
    sent = high[0].astype(F32)
    for term in high[1:]:
        sent += term.astype(F32)
    mirrored = exchange(sent.astype(BF16), "seq", CORES * (chips - 1))
    return chip_reduce(parts[: chips // 2], between) + [mirrored]


class Rest:
    def __init__(self, gains, chips):
        self.gains = gains
        self.steps = [("seq", 1)]
        images = lax.axis_size("img")
        image_steps = [("img", 1 << bit) for bit in range(images.bit_length() - 1)]
        chip_steps = [("seq", CORES << bit) for bit in range(chips.bit_length() - 1)]
        self.steps += chip_steps[:1] + image_steps + chip_steps[1:]

    def advance(self, count):
        for axis, apart in self.steps[:count]:
            self.gains = self.gains + exchange(self.gains, axis, apart)
        self.steps = self.steps[count:]


def chunk_bounds(half):
    return ((0, half),)


def local(query_proj, key_proj, value_proj, merge_cells, unmerge, grad_out, query_gain, key_gain):
    queries, key_rows, value_rows = query_proj[0], key_proj[0], value_proj[0]
    upstream = grad_out[0]
    tok, lanes = queries.shape
    half = lanes // CORES
    head_dim = query_gain.shape[0]
    cells = merge_cells.shape[1]
    chips = lax.axis_size("seq") // CORES
    bounds = chunk_bounds(half)
    widths = [stop - start for start, stop in bounds]
    query_row, key_row = query_gain[None], key_gain[None]

    merged = call(
        functools.partial(merge_kernel, head_dim, bounds),
        [((cells, 2 * width), BF16) for width in widths] * 2,
        [key_rows, value_rows, merge_cells[0].T, key_row],
        scratch=[((tok, lanes), BF16)] * 2
        + [(merge_cells.shape[:0:-1], jnp.int32), ((1, head_dim), F32)],
        far_in=4,
        copies=2 + 4 * sum(len(pieces(width)) for width in widths),
        vmem=ALL_VMEM_BYTES,
    )
    gathered = []
    for own, sent in zip(merged[: len(bounds)], merged[len(bounds) :]):
        block = jnp.concatenate([own, exchange(sent, "seq", 1)], axis=0)
        gathered.append(chip_gather(block, chips))

    (packed,) = call(
        pack_kernel, [((tok, lanes), BF16)], [queries, upstream], far_in=2, copies=2
    )
    raw, normed, both_upstream = call(
        functools.partial(query_kernel, head_dim),
        [((CORES * tok, half), BF16)] * 3,
        [queries, upstream, exchange(packed, "seq", 1), query_row],
        far_in=2,
        copies=2,
    )

    group = min(chips, 4)
    results = [
        call(
            functools.partial(attend_kernel, head_dim, start, chips, group),
            [
                ((CORES * tok, width), BF16),
                ((CORES * tok, width), F32),
                ((1, 2 * head_dim), F32),
                ((CORES * cells, 2 * width), F32),
            ]
            + [((CORES * cells, 2 * width), BF16)] * (chips - 1),
            [normed, both_upstream, query_row, key_row] + blocks,
            micros=3.5 * width / half,
        )
        for (start, stop), width, blocks in zip(bounds, widths, gathered)
    ]
    attended = [result[0] for result in results]
    grads = [result[1] for result in results]
    rest = Rest(sum(result[2] for result in results), chips)
    placed = []

    def between(arrays):
        if not placed:
            rest.advance(2)
            placed.extend(
                call(
                    functools.partial(query_back_kernel, head_dim, bounds),
                    [((tok, lanes), BF16)] * 3,
                    [raw, query_row] + attended + grads,
                    scratch=[((tok, half), BF16)] * 2,
                    far_out=2,
                    copies=2,
                )
            )
            arrays, rest.gains, placed[2] = lax.optimization_barrier(
                (arrays, rest.gains, placed[2])
            )
        return arrays

    terms = [chip_reduce(result[3:], between) for result in results]
    between([])
    rest.advance(2)
    attended_all, grad_query = call(
        place_kernel,
        [((tok, lanes), BF16)] * 2,
        [placed[0], placed[1], exchange(placed[2], "seq", 1)],
        far_in=2,
        far_out=2,
        copies=2,
        aliases={0: 0, 1: 1},
    )
    terms, rest.gains, attended_all, grad_query = lax.optimization_barrier(
        (terms, rest.gains, attended_all, grad_query)
    )
    rest.advance(len(rest.steps))
    gain_total = rest.gains[0]

    returned = []
    for chunk in terms:
        sent = chunk[0][cells:].astype(F32)
        for term in chunk[1:]:
            sent = sent + term[cells:].astype(F32)
        returned.append(exchange(sent, "seq", 1))

    def key_grads(other, outputs, sources, count):
        return call(
            functools.partial(key_back_kernel, bounds, count, other),
            [((tok, lanes), BF16)] * 2,
            outputs + [key_rows, unmerge, key_row] + sources,
            scratch=[((tok, half), BF16)] * 2,
            far_in=len(outputs),
            far_out=2,
            copies=2,
            aliases={0: 0, 1: 1} if other else None,
            micros=1.2,
        )

    partial_grads = key_grads(False, [], [term for chunk in terms for term in chunk], len(terms[0]))
    grad_key, grad_value = key_grads(True, list(partial_grads), returned, 1)
    return (
        attended_all[None],
        grad_query[None],
        grad_key[None],
        grad_value[None],
        gain_total[:head_dim],
        gain_total[head_dim:],
    )


def solution(mesh):
    rows = P("img", "seq", None)
    return jax.shard_map(
        local,
        mesh=mesh,
        in_specs=(rows, rows, rows, rows, P("img", "seq"), rows, P(), P()),
        out_specs=(rows, rows, rows, rows, P(), P()),
        check_vma=False,
    )
```

time: 57.9 us -> 52.1 us (0.90)
  waiting for transfers between devices: 24.1 us -> 17.6 us
  local copies, waits for them, and re-layouts: 4.07 us -> 1.98 us
  Pallas kernels: 10.4 us -> 12.2 us
  starting transfers between devices: 18.3 us -> 19.2 us
    ppermute x15, waiting for transfers between devices: 24.1 us -> 17.6 us  [exchange(): lax.ppermute(array, axis, [(i, i ^ apart) for i in range(lax.axis_size(ax...]
    pallas_call x7 -> x8, Pallas kernels: 10.4 us -> 12.2 us  [call(): pl.pallas_call(kernel, out_shape=[jax.ShapeDtypeStruct(shape, kind) for s...]
    unnamed x17 -> x15, local copies, waits for them, and re-layouts: 2.57 us -> 1.38 us
    ppermute x15, starting transfers between devices: 18.3 us -> 19.2 us  [exchange(): lax.ppermute(array, axis, [(i, i ^ apart) for i in range(lax.axis_size(ax...]
    another operation x4 -> x0, local copies, waits for them, and re-layouts: 0.82 us -> none  [the longest x2 0.74 us: local(): key_row = jnp.tile(key_gain, TILE // head_dim)[None]]
  transfers between devices with their start and end apart: 15 -> 15, of which waited for: 9 -> 9; matrix products, arithmetic and copies ran while one was open for 1% -> 1% of each run, Pallas kernels for 4% -> 9%
where the time goes in v2:
time: 52.1 us; the launch traced here: 51.9 us
  starting transfers between devices  19.2 us (37%)
  waiting for transfers between devices  17.6 us (34%)
  Pallas kernels  12.2 us (23%)
  local copies, waits for them, and re-layouts  1.98 us (4%)
  between operations  0.8 us (2%)
    ppermute x15, starting transfers between devices, exchange(): lax.ppermute(array, axis, [(i, i ^ apart) for i in range(lax.axis_size(ax...  19.2 us
    ppermute x15, waiting for transfers between devices, exchange(): lax.ppermute(array, axis, [(i, i ^ apart) for i in range(lax.axis_size(ax...  17.6 us
    pallas_call x8, Pallas kernels, call(): pl.pallas_call(kernel, out_shape=[jax.ShapeDtypeStruct(shape, kind) for s...  12.2 us
    unnamed x15, local copies, waits for them, and re-layouts  1.38 us
  transfers between devices with their start and end apart: 15, of which 9 were waited for; matrix products, arithmetic and copies ran while one was open for 1% of the time, Pallas kernels for 9%

profile of v2, /device:TPU:0, one launch (start us, length us, event | category | flops | bytes accessed | tf_op | source)
XLA Modules:
  0.0 51.9 jit_solution(3844070223379298568)
XLA Ops:
  0.6 0.0 copy-start
  0.6 0.0 copy-start.1
  0.7 2.6 %shard_map.129 = (bf16[32,1280]{1,0:T(8,128)(2,1)}, bf16[32,1280]{1,0:T(8,128)(2,1)}) custom-call(bf16[128,1280]{1,0:T(8,128)(2,1)} %bitcast.21, bf16[128,1280]{1,0:T(8,128)(2,1)} %bitcast.31, s32[4,32]{1,0:T(4,128)} %bitcast.32, f32[1,64]{1,0:T(1,128)} %bitcast.27), custom_call_target="tpu_custom_call" | custom-call | flops 1000000000 | bytes 2000000 | tf_op jit(solution)/shard_map/pallas_call | solution.py:25
  3.2 0.5 collective-permute-start.1
  3.8 0.0 copy-done
  3.8 0.0 copy-done.1
  3.8 0.0 copy-start.6
  3.8 0.1 shard_map.127
  3.8 0.1 collective-permute-start
  4.0 0.7 %copy-done.6 = bf16[32,1280]{1,0:T(8,128)(2,1)S(1)} copy-done((bf16[32,1280]{1,0:T(8,128)(2,1)S(1)}, bf16[32,1280]{1,0:T(8,128)(2,1)}, u32[]{:S(2)}) %copy-start.6) | copy-done | bytes 81944
  4.7 0.2 collective-permute-done.1
  4.9 0.0 copy-start.3
  4.9 5.0 %collective-permute-start.3 = (bf16[64,1280]{1,0:T(8,128)(2,1)S(1)}, bf16[64,1280]{1,0:T(8,128)(2,1)S(1)}, u32[]{:S(2)}, u32[]{:S(2)}) collective-permute-start(bf16[64,1280]{1,0:T(8,128)(2,1)S(1)} %constant_dynamic-update-slice_fusion.refs_4_), channel_id=1, source_target_pairs={{0,6},{1,7},{2,4},{3,5},{4,2},{5,3},{6,0},{7,1},{8,14},{9,15},{10,... | collective-permute-start | bytes 491528 | tf_op jit(solution)/shard_map/ppermute | solution.py:378
  9.9 0.0 collective-permute-start.2
  9.9 5.0 %collective-permute-done.3.refs_7_ = bf16[64,1280]{1,0:T(8,128)(2,1)S(1)} collective-permute-done((bf16[64,1280]{1,0:T(8,128)(2,1)S(1)}, bf16[64,1280]{1,0:T(8,128)(2,1)S(1)}, u32[]{:S(2)}, u32[]{:S(2)}) %collective-permute-start.3) | collective-permute-done | bytes 163872 | tf_op jit(solution)/shard_map/ppermute | solution.py:378
  14.9 2.7 %collective-permute-start.4 = (bf16[64,1280]{1,0:T(8,128)(2,1)S(1)}, bf16[64,1280]{1,0:T(8,128)(2,1)S(1)}, u32[]{:S(2)}, u32[]{:S(2)}) collective-permute-start(bf16[64,1280]{1,0:T(8,128)(2,1)S(1)} %collective-permute-done.3.refs_7_), channel_id=1, source_target_pairs={{0,2},{1,3},{2,0},{3,1},{4,6},{5,7},{6,4},{7,5},{8,10},{9,11},{10,... | collective-permute-start | bytes 491528 | tf_op jit(solution)/shard_map/ppermute | solution.py:378
  17.7 0.0 collective-permute-done.arrived_ref
  17.7 0.0 copy-done.3
  17.7 0.6 %shard_map.128 = (bf16[256,640]{1,0:T(8,128)(2,1)S(1)}, bf16[256,640]{1,0:T(8,128)(2,1)S(1)}, bf16[256,640]{1,0:T(8,128)(2,1)S(1)}) custom-call(bf16[128,1280]{1,0:T(8,128)(2,1)S(1)} %bitcast.18, bf16[128,1280]{1,0:T(8,128)(2,1)S(1)} %bitcast.20, bf16[128,1280]{1,0:T(8,128)(2,1)S(1)} %collective-permute-done.arrived_ref, f32[1,64]{1,0:T(1,128)S(1)} %bitcast.24), custom_call_target="tpu_custom_call" | custom-call | flops 1000000000 | bytes 2000000 | tf_op jit(solution)/shard_map/pallas_call | solution.py:25
  18.2 0.0 collective-permute-done.2.refs_5_
  18.2 3.3 %collective-permute-done.4.refs_6_ = bf16[64,1280]{1,0:T(8,128)(2,1)S(1)} collective-permute-done((bf16[64,1280]{1,0:T(8,128)(2,1)S(1)}, bf16[64,1280]{1,0:T(8,128)(2,1)S(1)}, u32[]{:S(2)}, u32[]{:S(2)}) %collective-permute-start.4) | collective-permute-done | bytes 163872 | tf_op jit(solution)/shard_map/ppermute | solution.py:378
  21.6 0.0 copy-start.4
  21.6 0.7 %copy-done.4 = f32[64]{0:T(128)S(1)} copy-done((f32[64]{0:T(128)S(1)}, f32[64]{0:T(128)}, u32[]{:S(2)}) %copy-start.4) | copy-done | bytes 280
  22.2 3.5 %shard_map.130 = (bf16[256,640]{1,0:T(8,128)(2,1)S(1)}, f32[256,640]{1,0:T(8,128)S(1)}, f32[1,128]{1,0:T(1,128)S(1)}, f32[64,1280]{1,0:T(8,128)S(1)}, bf16[64,12...) custom-call(bf16[256,640]{1,0:T(8,128)(2,1)S(1)} %get-tuple-element.36.refs_0_, ...), custom_call_target="tpu_custom_call" | custom-call | flops 3500000000 | bytes 7000000 | tf_op jit(solution)/shard_map/pallas_call | solution.py:25
  25.7 1.7 %collective-permute-start.6 = (bf16[64,1280]{1,0:T(8,128)(2,1)S(1)}, bf16[64,1280]{1,0:T(8,128)(2,1)S(1)}, u32[]{:S(2)}, u32[]{:S(2)}) collective-permute-start(bf16[64,1280]{1,0:T(8,128)(2,1)S(1)} %get-tuple-element.43), channel_id=1, source_target_pairs={{0,2},{1,3},{2,0},{3,1},{4,6},{5,7},{6,4},{7,5},{8,10},{9,11},{10,... | collective-permute-start | bytes 491528 | tf_op jit(solution)/shard_map/ppermute | solution.py:378
  27.4 0.0 collective-permute-start.7
  27.4 0.3 collective-permute-start.5
  27.8 0.8 %collective-permute-done.7 = f32[1,128]{1,0:T(1,128)S(1)} collective-permute-done((f32[1,128]{1,0:T(1,128)S(1)}, f32[1,128]{1,0:T(1,128)S(1)}, u32[]{:S(2)}, u32[]{:S(2)}) %collective-permute-start.7) | collective-permute-done | bytes 544 | tf_op jit(solution)/shard_map/ppermute | solution.py:378
  28.5 0.9 %collective-permute-start.8 = (f32[1,128]{1,0:T(1,128)S(1)}, f32[1,128]{1,0:T(1,128)S(1)}, u32[]{:S(2)}, u32[]{:S(2)}) collective-permute-start(f32[1,128]{1,0:T(1,128)S(1)} %add.24), channel_id=1, source_target_pairs={{0,2},{1,3},{2,0},{3,1},{4,6},{5,7},{6,4},{7,5},{8,10},{9,11},{10,... | collective-permute-start | bytes 1544 | tf_op jit(solution)/shard_map/ppermute | solution.py:378
  29.5 1.7 %shard_map.131 = (bf16[128,1280]{1,0:T(8,128)(2,1)}, bf16[128,1280]{1,0:T(8,128)(2,1)}, bf16[128,1280]{1,0:T(8,128)(2,1)S(1)}) custom-call(bf16[256,640]{1,0:T(8,128)(2,1)S(1)} %get-tuple-element.45.raw_ref, f32[1,64]{1,0:T(1,128)S(1)} %bitcast.26, bf16[256,640]{1,0:T(8,128)(2,1)S(1)} %get-tuple-element.46.refs_0_, f32[256,640]{1,0:T(8,128)S(1)} %get-tuple-element.47.refs_1_), custom_call_target="tpu_custom_call" | custom-call | flops 1000000000 | bytes 2000000 | tf_op jit(solution)/shard_map/pallas_call | solution.py:25
  31.2 3.4 %collective-permute-done.8 = f32[1,128]{1,0:T(1,128)S(1)} collective-permute-done((f32[1,128]{1,0:T(1,128)S(1)}, f32[1,128]{1,0:T(1,128)S(1)}, u32[]{:S(2)}, u32[]{:S(2)}) %collective-permute-start.8) | collective-permute-done | bytes 544 | tf_op jit(solution)/shard_map/ppermute | solution.py:378
  34.6 0.0 collective-permute-done.6
  34.6 0.0 collective-permute-start.12
  34.7 2.6 %collective-permute-start.9 = (bf16[64,1280]{1,0:T(8,128)(2,1)S(1)}, bf16[64,1280]{1,0:T(8,128)(2,1)S(1)}, u32[]{:S(2)}, u32[]{:S(2)}) collective-permute-start(bf16[64,1280]{1,0:T(8,128)(2,1)S(1)} %add_convert_fusion), channel_id=1, source_target_pairs={{0,6},{1,7},{2,4},{3,5},{4,2},{5,3},{6,0},{7,1},{8,14},{9,15},{10,... | collective-permute-start | bytes 491528 | tf_op jit(solution)/shard_map/ppermute | solution.py:378
  37.3 1.5 %collective-permute-start.10 = (f32[1,128]{1,0:T(1,128)S(1)}, f32[1,128]{1,0:T(1,128)S(1)}, u32[]{:S(2)}, u32[]{:S(2)}) collective-permute-start(f32[1,128]{1,0:T(1,128)S(1)} %add.25), channel_id=1, source_target_pairs={{0,8},{8,0},{16,24},{24,16},{1,9},{9,1},{17,25},{25,17},{2,10},{10... | collective-permute-start | bytes 1544 | tf_op jit(solution)/shard_map/ppermute | solution.py:378
  38.8 2.0 %collective-permute-done.10 = f32[1,128]{1,0:T(1,128)S(1)} collective-permute-done((f32[1,128]{1,0:T(1,128)S(1)}, f32[1,128]{1,0:T(1,128)S(1)}, u32[]{:S(2)}, u32[]{:S(2)}) %collective-permute-start.10) | collective-permute-done | bytes 544 | tf_op jit(solution)/shard_map/ppermute | solution.py:378
  40.9 1.5 %collective-permute-start.11 = (f32[1,128]{1,0:T(1,128)S(1)}, f32[1,128]{1,0:T(1,128)S(1)}, u32[]{:S(2)}, u32[]{:S(2)}) collective-permute-start(f32[1,128]{1,0:T(1,128)S(1)} %add.27), channel_id=1, source_target_pairs={{0,16},{8,24},{16,0},{24,8},{1,17},{9,25},{17,1},{25,9},{2,18},{10... | collective-permute-start | bytes 1544 | tf_op jit(solution)/shard_map/ppermute | solution.py:378
  42.4 2.0 %collective-permute-done.11 = f32[1,128]{1,0:T(1,128)S(1)} collective-permute-done((f32[1,128]{1,0:T(1,128)S(1)}, f32[1,128]{1,0:T(1,128)S(1)}, u32[]{:S(2)}, u32[]{:S(2)}) %collective-permute-start.11) | collective-permute-done | bytes 544 | tf_op jit(solution)/shard_map/ppermute | solution.py:378
  44.4 0.0 collective-permute-done.12.arrived_ref
  44.4 0.7 %shard_map.132 = (bf16[128,1280]{1,0:T(8,128)(2,1)}, bf16[128,1280]{1,0:T(8,128)(2,1)}) custom-call(bf16[128,1280]{1,0:T(8,128)(2,1)} %get-tuple-element.51.attended_in, bf16[128,1280]{1,0:T(8,128)(2,1)} %get-tuple-element.52.grad_in, bf16[128,1280]{1,0:T(8,128)(2,1)S(1)} %collective-permute-done.12.arrived_ref), custom_call_target="tpu_custom_call", output_to_operand_aliasing={{0}: (0, {}), {1}: (1, {})} | custom-call | flops 1000000000 | bytes 2000000 | tf_op jit(solution)/shard_map/pallas_call | solution.py:25
  45.2 0.0 copy-start.2
  45.2 0.0 collective-permute-done.5.refs_4_
  45.2 0.0 collective-permute-done.9.refs_5_
  45.2 0.0 copy-start.5
  45.2 2.2 %collective-permute-start.14 = (f32[1,128]{1,0:T(1,128)S(1)}, f32[1,128]{1,0:T(1,128)S(1)}, u32[]{:S(2)}, u32[]{:S(2)}) collective-permute-start(f32[1,128]{1,0:T(1,128)S(1)} %add.28), channel_id=1, source_target_pairs={{0,4},{1,5},{2,6},{3,7},{4,0},{5,1},{6,2},{7,3},{8,12},{9,13},{10,... | collective-permute-start | bytes 1544 | tf_op jit(solution)/shard_map/ppermute | solution.py:378
  47.4 0.0 copy-done.2
  47.4 0.0 copy-done.5
  47.4 1.5 %shard_map.133 = (bf16[128,1280]{1,0:T(8,128)(2,1)}, bf16[128,1280]{1,0:T(8,128)(2,1)}) custom-call(bf16[128,1280]{1,0:T(8,128)(2,1)S(1)} %bitcast.22, s32[1,128]{1,0:T(1,128)S(1)} %copy-done.5, f32[1,64]{1,0:T(1,128)S(1)} %bitcast.29, f32[64,1280]{1,0:T(8,128)S(1)} %get-tuple-element.58.refs_3_, bf16[64,1280]{1,0:T(8,128)(2,1)S(1)} %collective-permute-done.5.refs_4_, ...), custom_call_target="tpu_custom_call" | custom-call | flops 1200000000 | bytes 2400000 | tf_op jit(solution)/shard_map/pallas_call | solution.py:25
  48.9 0.1 collective-permute-start.13
  49.0 0.7 %collective-permute-done.14 = f32[1,128]{1,0:T(1,128)S(1)} collective-permute-done((f32[1,128]{1,0:T(1,128)S(1)}, f32[1,128]{1,0:T(1,128)S(1)}, u32[]{:S(2)}, u32[]{:S(2)}) %collective-permute-start.14) | collective-permute-done | bytes 544 | tf_op jit(solution)/shard_map/ppermute | solution.py:378
  49.7 0.6 %slice_bitcast_fusion = (f32[64]{0:T(128)}, f32[64]{0:T(128)}) fusion(f32[1,128]{1,0:T(1,128)S(1)} %add.31), kind=kLoop, calls=%fused_computation.4 | loop fusion | bytes 1024 | tf_op jit(solution)/shard_map/slice | solution.py:544
  50.3 0.1 collective-permute-done.13.refs_5_
  50.4 1.5 %shard_map.134 = (bf16[128,1280]{1,0:T(8,128)(2,1)}, bf16[128,1280]{1,0:T(8,128)(2,1)}) custom-call(bf16[128,1280]{1,0:T(8,128)(2,1)} %get-tuple-element.61.refs_0_, bf16[128,1280]{1,0:T(8,128)(2,1)} %get-tuple-element.62.refs_1_, bf16[128,1280]{1,0:T(8,128)(2,1)S(1)} %bitcast.23, ...), custom_call_target="tpu_custom_call", output_to_operand_aliasing={{0}: (0, {}), {1}: (1, {})} | custom-call | flops 1200000000 | bytes 2400000 | tf_op jit(solution)/shard_map/pallas_call | solution.py:25
  (9 shorter events, 0.1 us)
Async XLA Ops:
  0.6 3.1 %copy-start = (bf16[1,128,1280]{2,1,0:T(8,128)(2,1)S(1)}, bf16[1,128,1280]{2,1,0:T(8,128)(2,1)}, u32[]{:S(2)}) copy-start(bf16[1,128,1280]{2,1,0:T(8,128)(2,1)} %param.8) | copy-start | bytes 983044
  0.6 3.1 %copy-start.1 = (bf16[1,128,1280]{2,1,0:T(8,128)(2,1)S(1)}, bf16[1,128,1280]{2,1,0:T(8,128)(2,1)}, u32[]{:S(2)}) copy-start(bf16[1,128,1280]{2,1,0:T(8,128)(2,1)} %param.13) | copy-start | bytes 983044
  3.2 1.7 %collective-permute-start.1 = (bf16[32,1280]{1,0:T(8,128)(2,1)}, bf16[32,1280]{1,0:T(8,128)(2,1)S(1)}, u32[]{:S(2)}, u32[]{:S(2)}) collective-permute-start(bf16[32,1280]{1,0:T(8,128)(2,1)} %get-tuple-element.39), channel_id=1, source_target_pairs={{0,1},{1,0},{2,3},{3,2},{4,5},{5,4},{6,7},{7,6},{8,9},{9,8},{10,11... | collective-permute-start | bytes 245768 | tf_op jit(solution)/shard_map/ppermute | solution.py:378
  3.8 0.9 %copy-start.6 = (bf16[32,1280]{1,0:T(8,128)(2,1)S(1)}, bf16[32,1280]{1,0:T(8,128)(2,1)}, u32[]{:S(2)}) copy-start(bf16[32,1280]{1,0:T(8,128)(2,1)} %get-tuple-element.38) | copy-start | bytes 245764
  3.8 13.8 %collective-permute-start = (bf16[128,1280]{1,0:T(8,128)(2,1)S(1)}, bf16[128,1280]{1,0:T(8,128)(2,1)S(1)}, u32[]{:S(2)}, u32[]{:S(2)}) collective-permute-start(bf16[128,1280]{1,0:T(8,128)(2,1)S(1)} %shard_map.127), channel_id=1, source_target_pairs={{0,1},{1,0},{2,3},{3,2},{4,5},{5,4},{6,7},{7,6},{8,9},{9,8},{10,11... | collective-permute-start | bytes 983048 | tf_op jit(solution)/shard_map/ppermute | solution.py:378
  4.9 12.8 %copy-start.3 = (f32[64]{0:T(128)S(1)}, f32[64]{0:T(128)}, u32[]{:S(2)}) copy-start(f32[64]{0:T(128)} %param.14) | copy-start | bytes 772
  4.9 10.0 %collective-permute-start.3 = (bf16[64,1280]{1,0:T(8,128)(2,1)S(1)}, bf16[64,1280]{1,0:T(8,128)(2,1)S(1)}, u32[]{:S(2)}, u32[]{:S(2)}) collective-permute-start(bf16[64,1280]{1,0:T(8,128)(2,1)S(1)} %constant_dynamic-update-slice_fusion.refs_4_), channel_id=1, source_target_pairs={{0,6},{1,7},{2,4},{3,5},{4,2},{5,3},{6,0},{7,1},{8,14},{9,15},{10,... | collective-permute-start | bytes 491528 | tf_op jit(solution)/shard_map/ppermute | solution.py:378
  9.9 8.3 %collective-permute-start.2 = (bf16[64,1280]{1,0:T(8,128)(2,1)S(1)}, bf16[64,1280]{1,0:T(8,128)(2,1)S(1)}, u32[]{:S(2)}, u32[]{:S(2)}) collective-permute-start(bf16[64,1280]{1,0:T(8,128)(2,1)S(1)} %constant_dynamic-update-slice_fusion.refs_4_), channel_id=1, source_target_pairs={{0,2},{1,3},{2,0},{3,1},{4,6},{5,7},{6,4},{7,5},{8,10},{9,11},{10,... | collective-permute-start | bytes 491528 | tf_op jit(solution)/shard_map/ppermute | solution.py:378
  14.9 6.6 %collective-permute-start.4 = (bf16[64,1280]{1,0:T(8,128)(2,1)S(1)}, bf16[64,1280]{1,0:T(8,128)(2,1)S(1)}, u32[]{:S(2)}, u32[]{:S(2)}) collective-permute-start(bf16[64,1280]{1,0:T(8,128)(2,1)S(1)} %collective-permute-done.3.refs_7_), channel_id=1, source_target_pairs={{0,2},{1,3},{2,0},{3,1},{4,6},{5,7},{6,4},{7,5},{8,10},{9,11},{10,... | collective-permute-start | bytes 491528 | tf_op jit(solution)/shard_map/ppermute | solution.py:378
  21.6 0.7 %copy-start.4 = (f32[64]{0:T(128)S(1)}, f32[64]{0:T(128)}, u32[]{:S(2)}) copy-start(f32[64]{0:T(128)} %param.15) | copy-start | bytes 772
  25.7 8.9 %collective-permute-start.6 = (bf16[64,1280]{1,0:T(8,128)(2,1)S(1)}, bf16[64,1280]{1,0:T(8,128)(2,1)S(1)}, u32[]{:S(2)}, u32[]{:S(2)}) collective-permute-start(bf16[64,1280]{1,0:T(8,128)(2,1)S(1)} %get-tuple-element.43), channel_id=1, source_target_pairs={{0,2},{1,3},{2,0},{3,1},{4,6},{5,7},{6,4},{7,5},{8,10},{9,11},{10,... | collective-permute-start | bytes 491528 | tf_op jit(solution)/shard_map/ppermute | solution.py:378
  27.4 1.1 %collective-permute-start.7 = (f32[1,128]{1,0:T(1,128)S(1)}, f32[1,128]{1,0:T(1,128)S(1)}, u32[]{:S(2)}, u32[]{:S(2)}) collective-permute-start(f32[1,128]{1,0:T(1,128)S(1)} %get-tuple-element.44), channel_id=1, source_target_pairs={{0,1},{1,0},{2,3},{3,2},{4,5},{5,4},{6,7},{7,6},{8,9},{9,8},{10,11... | collective-permute-start | bytes 1544 | tf_op jit(solution)/shard_map/ppermute | solution.py:378
  27.4 17.8 %collective-permute-start.5 = (bf16[64,1280]{1,0:T(8,128)(2,1)S(1)}, bf16[64,1280]{1,0:T(8,128)(2,1)S(1)}, u32[]{:S(2)}, u32[]{:S(2)}) collective-permute-start(bf16[64,1280]{1,0:T(8,128)(2,1)S(1)} %get-tuple-element.41), channel_id=1, source_target_pairs={{0,2},{1,3},{2,0},{3,1},{4,6},{5,7},{6,4},{7,5},{8,10},{9,11},{10,... | collective-permute-start | bytes 491528 | tf_op jit(solution)/shard_map/ppermute | solution.py:378
  28.5 6.1 %collective-permute-start.8 = (f32[1,128]{1,0:T(1,128)S(1)}, f32[1,128]{1,0:T(1,128)S(1)}, u32[]{:S(2)}, u32[]{:S(2)}) collective-permute-start(f32[1,128]{1,0:T(1,128)S(1)} %add.24), channel_id=1, source_target_pairs={{0,2},{1,3},{2,0},{3,1},{4,6},{5,7},{6,4},{7,5},{8,10},{9,11},{10,... | collective-permute-start | bytes 1544 | tf_op jit(solution)/shard_map/ppermute | solution.py:378
  34.6 9.8 %collective-permute-start.12 = (bf16[128,1280]{1,0:T(8,128)(2,1)S(1)}, bf16[128,1280]{1,0:T(8,128)(2,1)S(1)}, u32[]{:S(2)}, u32[]{:S(2)}) collective-permute-start(bf16[128,1280]{1,0:T(8,128)(2,1)S(1)} %get-tuple-element.53), channel_id=1, source_target_pairs={{0,1},{1,0},{2,3},{3,2},{4,5},{5,4},{6,7},{7,6},{8,9},{9,8},{10,11... | collective-permute-start | bytes 983048 | tf_op jit(solution)/shard_map/ppermute | solution.py:378
  34.7 10.5 %collective-permute-start.9 = (bf16[64,1280]{1,0:T(8,128)(2,1)S(1)}, bf16[64,1280]{1,0:T(8,128)(2,1)S(1)}, u32[]{:S(2)}, u32[]{:S(2)}) collective-permute-start(bf16[64,1280]{1,0:T(8,128)(2,1)S(1)} %add_convert_fusion), channel_id=1, source_target_pairs={{0,6},{1,7},{2,4},{3,5},{4,2},{5,3},{6,0},{7,1},{8,14},{9,15},{10,... | collective-permute-start | bytes 491528 | tf_op jit(solution)/shard_map/ppermute | solution.py:378
  37.3 3.5 %collective-permute-start.10 = (f32[1,128]{1,0:T(1,128)S(1)}, f32[1,128]{1,0:T(1,128)S(1)}, u32[]{:S(2)}, u32[]{:S(2)}) collective-permute-start(f32[1,128]{1,0:T(1,128)S(1)} %add.25), channel_id=1, source_target_pairs={{0,8},{8,0},{16,24},{24,16},{1,9},{9,1},{17,25},{25,17},{2,10},{10... | collective-permute-start | bytes 1544 | tf_op jit(solution)/shard_map/ppermute | solution.py:378
  40.9 3.5 %collective-permute-start.11 = (f32[1,128]{1,0:T(1,128)S(1)}, f32[1,128]{1,0:T(1,128)S(1)}, u32[]{:S(2)}, u32[]{:S(2)}) collective-permute-start(f32[1,128]{1,0:T(1,128)S(1)} %add.27), channel_id=1, source_target_pairs={{0,16},{8,24},{16,0},{24,8},{1,17},{9,25},{17,1},{25,9},{2,18},{10... | collective-permute-start | bytes 1544 | tf_op jit(solution)/shard_map/ppermute | solution.py:378
  45.2 2.3 %copy-start.2 = (bf16[1,128,1280]{2,1,0:T(8,128)(2,1)S(1)}, bf16[1,128,1280]{2,1,0:T(8,128)(2,1)}, u32[]{:S(2)}) copy-start(bf16[1,128,1280]{2,1,0:T(8,128)(2,1)} %param.9) | copy-start | bytes 983044
  45.2 2.2 %copy-start.5 = (s32[1,128]{1,0:T(1,128)S(1)}, s32[1,128]{1,0:T(1,128)}, u32[]{:S(2)}) copy-start(s32[1,128]{1,0:T(1,128)} %refs_3_.1) | copy-start | bytes 1540
  45.2 4.5 %collective-permute-start.14 = (f32[1,128]{1,0:T(1,128)S(1)}, f32[1,128]{1,0:T(1,128)S(1)}, u32[]{:S(2)}, u32[]{:S(2)}) collective-permute-start(f32[1,128]{1,0:T(1,128)S(1)} %add.28), channel_id=1, source_target_pairs={{0,4},{1,5},{2,6},{3,7},{4,0},{5,1},{6,2},{7,3},{8,12},{9,13},{10,... | collective-permute-start | bytes 1544 | tf_op jit(solution)/shard_map/ppermute | solution.py:378
  48.9 1.5 %collective-permute-start.13 = (f32[32,1280]{1,0:T(8,128)S(1)}, f32[32,1280]{1,0:T(8,128)S(1)}, u32[]{:S(2)}, u32[]{:S(2)}) collective-permute-start(f32[32,1280]{1,0:T(8,128)S(1)} %convert_add_fusion), channel_id=1, source_target_pairs={{0,1},{1,0},{2,3},{3,2},{4,5},{5,4},{6,7},{7,6},{8,9},{9,8},{10,11... | collective-permute-start | bytes 491528 | tf_op jit(solution)/shard_map/ppermute | solution.py:378

commit v3 on v2

--- a/solution.py
+++ b/solution.py
@@ -152,31 +152,48 @@
 
 
 def query_kernel(
-    head_dim, query_ref, upstream_ref, arrived_ref, gain_ref, raw_ref, out_ref, grad_ref, copied
+    head_dim, query_ref, upstream_ref, arrived_ref, gain_ref, unit_ref, scale_ref, *refs
 ):
+    out_ref, grad_ref, copied = refs
     tok, lanes = query_ref.shape
     half = lanes // CORES
-    source = lanes_at(core_side() * (half // TILE), half)
-    moves = [
-        pltpu.make_async_copy(query_ref.at[:, source], raw_ref.at[:tok], copied.at[0]),
-        pltpu.make_async_copy(upstream_ref.at[:, source], grad_ref.at[:tok], copied.at[1]),
-    ]
-    for move in moves:
-        move.start()
-    raw_ref[tok:] = arrived_ref[:, :half]
+    side = core_side()
+    source = lanes_at(side * (half // TILE), half)
+    move = pltpu.make_async_copy(upstream_ref.at[:, source], grad_ref.at[:tok], copied.at[0])
+    move.start()
     grad_ref[tok:] = arrived_ref[:, half:]
-    moves[0].wait()
     for at, to in pieces(half):
-        unit_vals, _ = unit_rows(raw_ref[:, at:to].astype(F32), head_dim)
-        out_ref[:, at:to] = (unit_vals * gain_lanes(gain_ref, to - at)).astype(BF16)
-    moves[1].wait()
+        for row, queries in (
+            (0, query_ref[:, lanes_at(side * (half // TILE) + at // TILE, to - at)]),
+            (tok, arrived_ref[:, at:to]),
+        ):
+            here = slice(row, row + tok)
+            unit_vals, scale = unit_rows(queries.astype(F32), head_dim)
+            unit_ref[here, at:to] = unit_vals
+            scale_ref[here, at:to] = scale
+            out_ref[here, at:to] = (unit_vals * gain_lanes(gain_ref, to - at)).astype(BF16)
+    move.wait()
+
+
+def key_kernel(head_dim, key_ref, unmerge_ref, gain_ref, unit_ref, scale_ref, table_ref, row_ref):
+    tok = key_ref.shape[0]
+    cells = table_ref.shape[1] // 2
+    owner = lax.rem(unmerge_ref[...], cells)
+    table = (lax.broadcasted_iota(jnp.int32, (cells, tok), 0) == owner).astype(F32) * 0.25
+    table = table.T.astype(BF16)
+    table_ref[...] = jnp.concatenate([table, table], axis=1)
+    row_ref[...] = gain_lanes(gain_ref, row_ref.shape[1])
+    for at, to in pieces(key_ref.shape[1]):
+        unit_vals, scale = unit_rows(key_ref[:, at:to].astype(F32), head_dim)
+        unit_ref[:, at:to] = unit_vals
+        scale_ref[:, at:to] = scale
 
 
 def attend_kernel(head_dim, start, blocks, group, *refs):
-    query_ref, upstream_ref, query_gain_ref, key_gain_ref = refs[:4]
-    block_refs = refs[4 : 4 + blocks]
-    attended_ref, grad_ref, gain_out_ref = refs[4 + blocks : 7 + blocks]
-    part_refs = refs[7 + blocks :]
+    query_ref, upstream_ref = refs[:2]
+    block_refs = refs[2 : 2 + blocks]
+    attended_ref, grad_ref, gain_out_ref = refs[2 + blocks : 5 + blocks]
+    part_refs = refs[5 + blocks :]
     rows = query_ref.shape[0]
     block_rows, width = block_refs[0].shape
     width = width // 2
@@ -271,16 +288,10 @@
     def per_channel(row):
         return sum(row[:, at : at + head_dim] for at in range(0, TILE, head_dim))
 
-    gain_out_ref[...] = jnp.concatenate(
-        [
-            per_channel(sums[0]) / query_gain_ref[...],
-            per_channel(sums[1]) / key_gain_ref[...],
-        ],
-        axis=1,
-    )
-
-
-def query_back_kernel(head_dim, bounds, raw_ref, gain_ref, *refs):
+    gain_out_ref[...] = jnp.concatenate([per_channel(row) for row in sums], axis=1)
+
+
+def query_back_kernel(head_dim, bounds, unit_ref, scale_ref, gain_ref, *refs):
     count = len(bounds)
     attended_refs, grad_refs = refs[:count], refs[count : 2 * count]
     attended_out, grad_out, send_ref, attended_buf, grad_buf, copied = refs[2 * count :]
@@ -290,9 +301,12 @@
         send_ref[:, start:stop] = attended_ref[tok:]
         for at, to in pieces(stop - start):
             lane = slice(start + at, start + to)
-            unit_vals, scale = unit_rows(raw_ref[:, lane].astype(F32), head_dim)
             grads = norm_back(
-                grad_ref[:, at:to], unit_vals, scale, gain_lanes(gain_ref, to - at), head_dim
+                grad_ref[:, at:to],
+                unit_ref[:, lane],
+                scale_ref[:, lane],
+                gain_lanes(gain_ref, to - at),
+                head_dim,
             ).astype(BF16)
             grad_buf[:, lane] = grads[:tok]
             send_ref[:, half + start + at : half + start + to] = grads[tok:]
@@ -307,69 +321,58 @@
         move.wait()
 
 
-def place_kernel(attended_in, grad_in, arrived_ref, attended_out, grad_out, copied):
-    half = arrived_ref.shape[1] // 2
-    place = lanes_at((1 - core_side()) * (half // TILE), half)
-    moves = [
-        pltpu.make_async_copy(arrived_ref.at[:, :half], attended_out.at[:, place], copied.at[0]),
-        pltpu.make_async_copy(arrived_ref.at[:, half:], grad_out.at[:, place], copied.at[1]),
-    ]
-    for move in moves:
-        move.start()
-    for move in moves:
-        move.wait()
-
-
-def key_back_kernel(bounds, terms, other, *refs):
-    count = len(bounds)
-    if other:
-        refs = refs[2:]
-    key_ref, unmerge_ref, gain_ref = refs[:3]
-    term_refs = [refs[3 + chunk * terms : 3 + (chunk + 1) * terms] for chunk in range(count)]
-    grad_key_out, grad_value_out, grad_key_buf, grad_value_buf, copied = refs[3 + count * terms :]
-    tok, half = grad_key_buf.shape
-    cells = term_refs[0][0].shape[0] // (1 if other else CORES)
+def key_back_kernel(head_dim, bounds, own_terms, other_terms, *refs):
+    query_refs, refs = refs[2:3], refs[3:]
+    unit_ref, scale_ref, table_ref, gain_ref = refs[:4]
+    refs = refs[4:]
+    sources = []
+    for _ in bounds:
+        sources.append((refs[:own_terms], refs[own_terms : own_terms + other_terms]))
+        refs = refs[own_terms + other_terms :]
+    grad_key_out, grad_value_out, *query_outs, grad_key_buf, grad_value_buf, copied = refs
+    tok, half = grad_key_buf.shape[1:]
+    cells = sources[0][1][0].shape[0]
     side = core_side()
-    first = (1 - side if other else side) * (half // TILE)
-    owner = lax.rem(unmerge_ref[...], cells)
-    table = (lax.broadcasted_iota(jnp.int32, (cells, tok), 0) == owner).astype(F32)
-    table = table.T.astype(BF16)
-    twice = jnp.concatenate([table, table], axis=1)
-
-    def spread(chunk, at, to):
-        result = term_refs[chunk][0][:cells, at:to].astype(F32)
-        for ref in term_refs[chunk][1:]:
-            result += ref[:cells, at:to].astype(F32)
-        return dot(twice, jnp.concatenate(halves(result), axis=0)) * 0.25
+    table = table_ref[...]
+
+    def spread(chunk, other, at, to):
+        total = added([ref[:cells, at:to] for ref in sources[chunk][other]])
+        return dot(table, jnp.concatenate(halves(total), axis=0))
 
     spans = [
-        (chunk, start, stop, start + at, start + to)
+        (other, chunk, start, stop, start + at, start + to)
+        for other in range(CORES)
         for chunk, (start, stop) in enumerate(bounds)
         for at, to in pieces(stop - start)
     ]
     moves = []
 
-    def send(index, buf, out):
-        move = pltpu.make_async_copy(buf, out.at[:, lanes_at(first, half)], copied.at[index])
+    def send(buf, out, other):
+        place = lanes_at((1 - side if other else side) * (half // TILE), half)
+        move = pltpu.make_async_copy(buf, out.at[:, place], copied.at[len(moves)])
         move.start()
         moves.append(move)
 
-    for chunk, start, stop, at, to in spans:
-        grad_value_buf[:, at:to] = spread(chunk, stop - 2 * start + at, stop - 2 * start + to).astype(
-            BF16
-        )
-    send(0, grad_value_buf, grad_value_out)
-    for chunk, start, stop, at, to in spans:
-        keys = key_ref[:, lanes_at(first + at // TILE, to - at)].astype(F32)
-        unit_vals, scale = unit_rows(keys, gain_ref.shape[1])
-        grad_key_buf[:, at:to] = norm_back(
-            spread(chunk, at - start, to - start),
-            unit_vals,
-            scale,
-            gain_lanes(gain_ref, to - at),
-            gain_ref.shape[1],
+    for index, out in enumerate(query_outs):
+        send(query_refs[0].at[:, index * half : (index + 1) * half], out, 1)
+    for other, chunk, start, stop, at, to in spans:
+        grad_value_buf[other, :, at:to] = spread(
+            chunk, other, stop - 2 * start + at, stop - 2 * start + to
         ).astype(BF16)
-    send(1, grad_key_buf, grad_key_out)
+    for other in range(CORES):
+        send(grad_value_buf.at[other], grad_value_out, other)
+    for other, chunk, start, stop, at, to in spans:
+        first = (1 - side if other else side) * (half // TILE)
+        lane = lanes_at(first + at // TILE, to - at)
+        grad_key_buf[other, :, at:to] = norm_back(
+            spread(chunk, other, at - start, to - start),
+            unit_ref[:, lane],
+            scale_ref[:, lane],
+            gain_ref[:, : to - at],
+            head_dim,
+        ).astype(BF16)
+        if to == half:
+            send(grad_key_buf.at[other], grad_key_out, other)
     for move in moves:
         move.wait()
 
@@ -385,33 +388,44 @@
     return chip_gather(block, chips // 2) + chip_gather(mirrored, chips // 2)[::-1]
 
 
-def chip_reduce(parts, between):
+def chip_reduce(parts):
     chips = len(parts)
     if chips == 1:
         return [parts[0]]
-    high = chip_reduce(parts[: chips // 2 - 1 : -1], between)
-    if len(high) > 1:
-        high = [high[0]] + between(high[1:])
-    sent = high[0].astype(F32)
-    for term in high[1:]:
-        sent += term.astype(F32)
-    mirrored = exchange(sent.astype(BF16), "seq", CORES * (chips - 1))
-    return chip_reduce(parts[: chips // 2], between) + [mirrored]
+    sent = added(chip_reduce(parts[: chips // 2 - 1 : -1])).astype(BF16)
+    return chip_reduce(parts[: chips // 2]) + [exchange(sent, "seq", CORES * (chips - 1))]
+
+
+def added(terms):
+    total = terms[0].astype(F32)
+    for term in terms[1:]:
+        total += term.astype(F32)
+    return total
 
 
 class Rest:
     def __init__(self, gains, chips):
         self.gains = gains
-        self.steps = [("seq", 1)]
         images = lax.axis_size("img")
         image_steps = [("img", 1 << bit) for bit in range(images.bit_length() - 1)]
         chip_steps = [("seq", CORES << bit) for bit in range(chips.bit_length() - 1)]
-        self.steps += chip_steps[:1] + image_steps + chip_steps[1:]
-
-    def advance(self, count):
-        for axis, apart in self.steps[:count]:
-            self.gains = self.gains + exchange(self.gains, axis, apart)
-        self.steps = self.steps[count:]
+        self.table = {
+            "c": [("seq", 1)],
+            "y": image_steps[:1],
+            "x": image_steps[1:],
+            "z": chip_steps[:1],
+            "w": chip_steps[1:],
+            "D": [("seq", *(CORES * apart for apart in range(1, chips)))],
+        }
+
+    def advance(self, names):
+        for name in names:
+            for axis, *aparts in self.table[name]:
+                arrived = [exchange(self.gains, axis, apart) for apart in aparts]
+                self.gains = sum(arrived, self.gains)
+
+
+OPT = dict(split=0, steps="cD|yx|", near=1, hb=0, sb=2, k4=0, kc=1.7, pc=1.0)
 
 
 def chunk_bounds(half):
@@ -440,20 +454,28 @@
         copies=2 + 4 * sum(len(pieces(width)) for width in widths),
         vmem=ALL_VMEM_BYTES,
     )
-    gathered = []
-    for own, sent in zip(merged[: len(bounds)], merged[len(bounds) :]):
-        block = jnp.concatenate([own, exchange(sent, "seq", 1)], axis=0)
-        gathered.append(chip_gather(block, chips))
+    crossed = [exchange(sent, "seq", 1) for sent in merged[len(bounds) :]]
+    crossed, late_queries, late_upstream, late_keys = lax.optimization_barrier(
+        (crossed, queries, upstream, key_rows)
+    )
+    gathered = [
+        chip_gather(jnp.concatenate([own, other], axis=0), chips)
+        for own, other in zip(merged, crossed)
+    ]
 
     (packed,) = call(
-        pack_kernel, [((tok, lanes), BF16)], [queries, upstream], far_in=2, copies=2
-    )
-    raw, normed, both_upstream = call(
+        pack_kernel, [((tok, lanes), BF16)], [late_queries, late_upstream], far_in=2, copies=2
+    )
+    query_unit, query_scale, normed, both_upstream = call(
         functools.partial(query_kernel, head_dim),
-        [((CORES * tok, half), BF16)] * 3,
+        [((CORES * tok, half), F32)] * 2 + [((CORES * tok, half), BF16)] * 2,
         [queries, upstream, exchange(packed, "seq", 1), query_row],
-        far_in=2,
-        copies=2,
+        copies=1,
+    )
+    key_unit, key_scale, table, gain_row = call(
+        functools.partial(key_kernel, head_dim),
+        [((tok, lanes), F32)] * 2 + [((tok, 2 * cells), BF16), ((1, 2 * TILE), F32)],
+        [late_keys, unmerge, key_row],
     )
 
     group = min(chips, 4)
@@ -467,7 +489,7 @@
                 ((CORES * cells, 2 * width), F32),
             ]
             + [((CORES * cells, 2 * width), BF16)] * (chips - 1),
-            [normed, both_upstream, query_row, key_row] + blocks,
+            [normed, both_upstream] + blocks,
             micros=3.5 * width / half,
         )
         for (start, stop), width, blocks in zip(bounds, widths, gathered)
@@ -475,73 +497,90 @@
     attended = [result[0] for result in results]
     grads = [result[1] for result in results]
     rest = Rest(sum(result[2] for result in results), chips)
-    placed = []
-
-    def between(arrays):
-        if not placed:
-            rest.advance(2)
-            placed.extend(
-                call(
-                    functools.partial(query_back_kernel, head_dim, bounds),
-                    [((tok, lanes), BF16)] * 3,
-                    [raw, query_row] + attended + grads,
-                    scratch=[((tok, half), BF16)] * 2,
-                    far_out=2,
-                    copies=2,
-                )
-            )
-            arrays, rest.gains, placed[2] = lax.optimization_barrier(
-                (arrays, rest.gains, placed[2])
-            )
-        return arrays
-
-    terms = [chip_reduce(result[3:], between) for result in results]
-    between([])
-    rest.advance(2)
-    attended_all, grad_query = call(
-        place_kernel,
-        [((tok, lanes), BF16)] * 2,
-        [placed[0], placed[1], exchange(placed[2], "seq", 1)],
-        far_in=2,
-        far_out=2,
-        copies=2,
-        aliases={0: 0, 1: 1},
-    )
-    terms, rest.gains, attended_all, grad_query = lax.optimization_barrier(
-        (terms, rest.gains, attended_all, grad_query)
-    )
-    rest.advance(len(rest.steps))
-    gain_total = rest.gains[0]
-
-    returned = []
-    for chunk in terms:
-        sent = chunk[0][cells:].astype(F32)
-        for term in chunk[1:]:
-            sent = sent + term[cells:].astype(F32)
-        returned.append(exchange(sent, "seq", 1))
-
-    def key_grads(other, outputs, sources, count):
+
+    first_steps, next_steps, last_steps = OPT["steps"].split("|")
+
+    def query_back():
         return call(
-            functools.partial(key_back_kernel, bounds, count, other),
-            [((tok, lanes), BF16)] * 2,
-            outputs + [key_rows, unmerge, key_row] + sources,
+            functools.partial(query_back_kernel, head_dim, bounds),
+            [((tok, lanes), BF16)] * 3,
+            [query_unit, query_scale, query_row] + attended + grads,
             scratch=[((tok, half), BF16)] * 2,
-            far_in=len(outputs),
             far_out=2,
             copies=2,
-            aliases={0: 0, 1: 1} if other else None,
-            micros=1.2,
+            micros=OPT["kc"],
         )
 
-    partial_grads = key_grads(False, [], [term for chunk in terms for term in chunk], len(terms[0]))
-    grad_key, grad_value = key_grads(True, list(partial_grads), returned, 1)
+    parts = [result[3:] for result in results]
+    far = [chip_reduce(part[: chips // 2 - 1 : -1]) if chips > 1 else [] for part in parts]
+    rest.advance(first_steps)
+    if OPT["k4"] == 1:
+        attended_half, grad_half, sent_part = query_back()
+        if OPT["k4"] == 1:
+            far, sent_part = lax.optimization_barrier((far, sent_part))
+    if OPT["hb"]:
+        far, rest.gains = lax.optimization_barrier((far, rest.gains))
+    mirror = CORES * (chips - 1)
+    sums = [added(terms).astype(BF16) for terms in far if terms]
+    if OPT["sb"] == 1:
+        sums, rest.gains = lax.optimization_barrier((sums, rest.gains))
+    if OPT["sb"] == 2:
+        _, rest.gains = lax.optimization_barrier((sums, rest.gains))
+    if OPT["split"]:
+        straight = [[exchange(sent[:cells], "seq", mirror)] for sent in sums]
+        across = [[exchange(sent[cells:], "seq", mirror + 1)] for sent in sums]
+    else:
+        straight = [[exchange(sent, "seq", mirror)] for sent in sums]
+        across = [[] for _ in bounds]
+    if chips == 1:
+        straight = across = [[] for _ in bounds]
+    near = [chip_reduce(part[: max(chips // 2, 1)]) for part in parts]
+    if OPT["split"]:
+        crossed = [exchange(added([term[cells:] for term in terms]), "seq", 1) for terms in near]
+    else:
+        crossed = None
+    if OPT["k4"] != 1:
+        attended_half, grad_half, sent_part = query_back()
+    if OPT["near"] == 1:
+        rest.advance(next_steps[:1])
+        near, rest.gains = lax.optimization_barrier((near, rest.gains))
+        rest.advance(next_steps[1:])
+    elif OPT["near"] == 2:
+        near, rest.gains = lax.optimization_barrier((near, rest.gains))
+        rest.advance(next_steps)
+    else:
+        rest.advance(next_steps)
+    arrived_part = exchange(sent_part, "seq", 1)
+    straight, across, crossed, rest.gains, arrived_part = lax.optimization_barrier(
+        (straight, across, crossed, rest.gains, arrived_part)
+    )
+    own_terms = [first + last for first, last in zip(near, straight)]
+    if not OPT["split"]:
+        crossed = [exchange(added([t[cells:] for t in terms]), "seq", 1) for terms in own_terms]
+    rest.advance(last_steps)
+    gain_total = rest.gains[0]
+
+    sources = []
+    for chunk in range(len(bounds)):
+        sources += own_terms[chunk] + [crossed[chunk]] + across[chunk]
+    grad_key, grad_value, attended_all, grad_query = call(
+        functools.partial(key_back_kernel, head_dim, bounds, len(own_terms[0]), 1 + len(across[0])),
+        [((tok, lanes), BF16)] * 4,
+        [attended_half, grad_half, arrived_part, key_unit, key_scale, table, gain_row] + sources,
+        scratch=[((CORES, tok, half), BF16)] * 2,
+        far_in=2,
+        far_out=4,
+        copies=2 * CORES + 2,
+        aliases={0: 2, 1: 3},
+        micros=2.0,
+    )
     return (
         attended_all[None],
         grad_query[None],
         grad_key[None],
         grad_value[None],
-        gain_total[:head_dim],
-        gain_total[head_dim:],
+        gain_total[:head_dim] / query_gain,
+        gain_total[head_dim:] / key_gain,
     )
 
 

time: 52.1 us -> 47.7 us (0.916)
  waiting for transfers between devices: 17.6 us -> 13.5 us
  starting transfers between devices: 19.2 us -> 21.6 us
  Pallas kernels: 12.2 us -> 10.1 us
  local copies, waits for them, and re-layouts: 1.98 us -> 0.92 us
  other arithmetic: 0.09 us -> 0.67 us
    ppermute x15 -> x16, waiting for transfers between devices: 17.6 us -> 13.5 us  [exchange(): lax.ppermute(array, axis, [(i, i ^ apart) for i in range(lax.axis_size(ax...]
    ppermute x15 -> x16, starting transfers between devices: 19.2 us -> 21.6 us  [exchange(): lax.ppermute(array, axis, [(i, i ^ apart) for i in range(lax.axis_size(ax...]
    pallas_call x8 -> x7, Pallas kernels: 12.2 us -> 10.1 us  [call(): pl.pallas_call(kernel, out_shape=[jax.ShapeDtypeStruct(shape, kind) for s...]
    slice x1 -> x0, local copies, waits for them, and re-layouts: 0.59 us -> none  [local(): gain_total[head_dim:]]
    div x0 -> x1, other arithmetic: none -> 0.59 us  [local(): gain_total[head_dim:] / key_gain]
    unnamed x15 -> x13, local copies, waits for them, and re-layouts: 1.38 us -> 0.92 us
  transfers between devices with their start and end apart: 15 -> 16, of which waited for: 9 -> 7; matrix products, arithmetic and copies ran while one was open for 1% -> 3% of each run, Pallas kernels for 9% -> 5%
where the time goes in v3:
time: 47.7 us; the launch traced here: 47.6 us
  starting transfers between devices  21.6 us (45%)
  waiting for transfers between devices  13.5 us (28%)
  Pallas kernels  10.1 us (21%)
  local copies, waits for them, and re-layouts  0.92 us (2%)
  between operations  0.76 us (2%)
  other arithmetic  0.67 us (1%)
    ppermute x16, starting transfers between devices, exchange(): lax.ppermute(array, axis, [(i, i ^ apart) for i in range(lax.axis_size(ax...  21.6 us
    ppermute x16, waiting for transfers between devices, exchange(): lax.ppermute(array, axis, [(i, i ^ apart) for i in range(lax.axis_size(ax...  13.5 us
    pallas_call x7, Pallas kernels, call(): pl.pallas_call(kernel, out_shape=[jax.ShapeDtypeStruct(shape, kind) for s...  10.1 us
  transfers between devices with their start and end apart: 16, of which 7 were waited for; matrix products, arithmetic and copies ran while one was open for 3% of the time, Pallas kernels for 5%

profile of v3, /device:TPU:0, one launch (start us, length us, event | category | flops | bytes accessed | tf_op | source)
XLA Modules:
  0.0 47.6 jit_solution(3984389166571399707)
XLA Ops:
  0.6 0.0 copy-start.2
  0.6 0.0 copy-start.3
  0.7 2.6 %shard_map.127 = (bf16[32,1280]{1,0:T(8,128)(2,1)}, bf16[32,1280]{1,0:T(8,128)(2,1)}) custom-call(bf16[128,1280]{1,0:T(8,128)(2,1)} %bitcast.25, bf16[128,1280]{1,0:T(8,128)(2,1)} %bitcast.27, s32[4,32]{1,0:T(4,128)} %bitcast.28, f32[1,64]{1,0:T(1,128)} %bitcast.19), custom_call_target="tpu_custom_call" | custom-call | flops 1000000000 | bytes 2000000 | tf_op jit(solution)/shard_map/pallas_call | solution.py:25
  3.2 0.5 %collective-permute-start = (bf16[32,1280]{1,0:T(8,128)(2,1)}, bf16[32,1280]{1,0:T(8,128)(2,1)S(1)}, u32[]{:S(2)}, u32[]{:S(2)}) collective-permute-start(bf16[32,1280]{1,0:T(8,128)(2,1)} %get-tuple-element.41), channel_id=1, source_target_pairs={{0,1},{1,0},{2,3},{3,2},{4,5},{5,4},{6,7},{7,6},{8,9},{9,8},{10,11... | collective-permute-start | bytes 245768 | tf_op jit(solution)/shard_map/ppermute | solution.py:381
  3.8 0.9 %constant_dynamic-update-slice_fusion.1 = bf16[64,1280]{1,0:T(8,128)(2,1)S(1)} fusion(bf16[32,1280]{1,0:T(8,128)(2,1)} %get-tuple-element.48), kind=kLoop, calls=%fused_computation.3 | loop fusion | bytes 163840
  4.6 0.2 collective-permute-done
  4.9 0.0 copy-done.2
  4.9 0.0 copy-done.3
  4.9 0.1 shard_map.128
  5.0 0.4 collective-permute-start.1
  5.4 0.0 copy-start
  5.4 4.8 %collective-permute-start.3 = (bf16[64,1280]{1,0:T(8,128)(2,1)S(1)}, bf16[64,1280]{1,0:T(8,128)(2,1)S(1)}, u32[]{:S(2)}, u32[]{:S(2)}) collective-permute-start(bf16[64,1280]{1,0:T(8,128)(2,1)S(1)} %constant_dynamic-update-slice_fusion.refs_2_), channel_id=1, source_target_pairs={{0,6},{1,7},{2,4},{3,5},{4,2},{5,3},{6,0},{7,1},{8,14},{9,15},{10,... | collective-permute-start | bytes 491528 | tf_op jit(solution)/shard_map/ppermute | solution.py:381
  10.2 0.0 collective-permute-start.2
  10.2 5.1 %collective-permute-done.3.refs_5_ = bf16[64,1280]{1,0:T(8,128)(2,1)S(1)} collective-permute-done((bf16[64,1280]{1,0:T(8,128)(2,1)S(1)}, bf16[64,1280]{1,0:T(8,128)(2,1)S(1)}, u32[]{:S(2)}, u32[]{:S(2)}) %collective-permute-start.3) | collective-permute-done | bytes 163872 | tf_op jit(solution)/shard_map/ppermute | solution.py:381
  15.3 2.8 %collective-permute-start.4 = (bf16[64,1280]{1,0:T(8,128)(2,1)S(1)}, bf16[64,1280]{1,0:T(8,128)(2,1)S(1)}, u32[]{:S(2)}, u32[]{:S(2)}) collective-permute-start(bf16[64,1280]{1,0:T(8,128)(2,1)S(1)} %collective-permute-done.3.refs_5_), channel_id=1, source_target_pairs={{0,2},{1,3},{2,0},{3,1},{4,6},{5,7},{6,4},{7,5},{8,10},{9,11},{10,... | collective-permute-start | bytes 491528 | tf_op jit(solution)/shard_map/ppermute | solution.py:381
  18.1 0.0 collective-permute-done.1.arrived_ref
  18.2 0.0 copy-done
  18.2 0.5 %shard_map.129 = (f32[256,640]{1,0:T(8,128)S(1)}, f32[256,640]{1,0:T(8,128)S(1)}, bf16[256,640]{1,0:T(8,128)(2,1)S(1)}, bf16[256,640]{1,0:T(8,128)(2,1)S(1)}) custom-call(bf16[128,1280]{1,0:T(8,128)(2,1)S(1)} %bitcast.22, bf16[128,1280]{1,0:T(8,128)(2,1)S(1)} %bitcast.24, bf16[128,1280]{1,0:T(8,128)(2,1)S(1)} %collective-permute-done.1.arrived_ref, ...), custom_call_target="tpu_custom_call" | custom-call | flops 1000000000 | bytes 2000000 | tf_op jit(solution)/shard_map/pallas_call | solution.py:25
  18.7 0.0 collective-permute-done.2.refs_3_
  18.7 3.4 %collective-permute-done.4.refs_4_ = bf16[64,1280]{1,0:T(8,128)(2,1)S(1)} collective-permute-done((bf16[64,1280]{1,0:T(8,128)(2,1)S(1)}, bf16[64,1280]{1,0:T(8,128)(2,1)S(1)}, u32[]{:S(2)}, u32[]{:S(2)}) %collective-permute-start.4) | collective-permute-done | bytes 163872 | tf_op jit(solution)/shard_map/ppermute | solution.py:381
  22.1 3.5 %shard_map.130 = (bf16[256,640]{1,0:T(8,128)(2,1)S(1)}, f32[256,640]{1,0:T(8,128)S(1)}, f32[1,128]{1,0:T(1,128)S(1)}, f32[64,1280]{1,0:T(8,128)S(1)}, bf16[64,12...) custom-call(bf16[256,640]{1,0:T(8,128)(2,1)S(1)} %get-tuple-element.46.refs_0_, ...), custom_call_target="tpu_custom_call" | custom-call | flops 3500000000 | bytes 7000000 | tf_op jit(solution)/shard_map/pallas_call | solution.py:25
  25.6 1.8 %collective-permute-start.5 = (bf16[64,1280]{1,0:T(8,128)(2,1)S(1)}, bf16[64,1280]{1,0:T(8,128)(2,1)S(1)}, u32[]{:S(2)}, u32[]{:S(2)}) collective-permute-start(bf16[64,1280]{1,0:T(8,128)(2,1)S(1)} %get-tuple-element.55), channel_id=1, source_target_pairs={{0,2},{1,3},{2,0},{3,1},{4,6},{5,7},{6,4},{7,5},{8,10},{9,11},{10,... | collective-permute-start | bytes 491528 | tf_op jit(solution)/shard_map/ppermute | solution.py:381
  27.3 0.0 collective-permute-start.8
  27.3 0.3 collective-permute-start.7
  27.6 1.4 %shard_map.131 = (bf16[128,1280]{1,0:T(8,128)(2,1)}, bf16[128,1280]{1,0:T(8,128)(2,1)}, bf16[128,1280]{1,0:T(8,128)(2,1)S(1)}) custom-call(f32[256,640]{1,0:T(8,128)S(1)} %get-tuple-element.44.unit_ref, f32[256,640]{1,0:T(8,128)S(1)} %get-tuple-element.45.scale_ref, f32[1,64]{1,0:T(1,128)S(1)} %bitcast.18, bf16[256,640]{1,0:T(8,128)(2,1)S(1)} %get-tuple-element.50.refs_0_, ...), custom_call_target="tpu_custom_call" | custom-call | flops 1700000000 | bytes 3400000 | tf_op jit(solution)/shard_map/pallas_call | solution.py:25
  29.0 0.0 copy-start.4
  29.0 0.3 collective-permute-start.14
  29.3 0.0 collective-permute-done.8
  29.3 2.8 %collective-permute-start.10 = (f32[1,128]{1,0:T(1,128)S(1)}, f32[1,128]{1,0:T(1,128)S(1)}, u32[]{:S(2)}, u32[]{:S(2)}) collective-permute-start(f32[1,128]{1,0:T(1,128)S(1)} %add.28), channel_id=1, source_target_pairs={{0,4},{1,5},{2,6},{3,7},{4,0},{5,1},{6,2},{7,3},{8,12},{9,13},{10,... | collective-permute-start | bytes 1544 | tf_op jit(solution)/shard_map/ppermute | solution.py:381
  32.1 1.3 %collective-permute-start.11 = (f32[1,128]{1,0:T(1,128)S(1)}, f32[1,128]{1,0:T(1,128)S(1)}, u32[]{:S(2)}, u32[]{:S(2)}) collective-permute-start(f32[1,128]{1,0:T(1,128)S(1)} %add.28), channel_id=1, source_target_pairs={{0,6},{1,7},{2,4},{3,5},{4,2},{5,3},{6,0},{7,1},{8,14},{9,15},{10,... | collective-permute-start | bytes 1544 | tf_op jit(solution)/shard_map/ppermute | solution.py:381
  33.4 0.0 collective-permute-done.5
  33.4 0.8 %collective-permute-start.9 = (f32[1,128]{1,0:T(1,128)S(1)}, f32[1,128]{1,0:T(1,128)S(1)}, u32[]{:S(2)}, u32[]{:S(2)}) collective-permute-start(f32[1,128]{1,0:T(1,128)S(1)} %add.28), channel_id=1, source_target_pairs={{0,2},{1,3},{2,0},{3,1},{4,6},{5,7},{6,4},{7,5},{8,10},{9,11},{10,... | collective-permute-start | bytes 1544 | tf_op jit(solution)/shard_map/ppermute | solution.py:381
  34.3 0.0 collective-permute-done.10
  34.3 2.5 %collective-permute-start.6 = (bf16[64,1280]{1,0:T(8,128)(2,1)S(1)}, bf16[64,1280]{1,0:T(8,128)(2,1)S(1)}, u32[]{:S(2)}, u32[]{:S(2)}) collective-permute-start(bf16[64,1280]{1,0:T(8,128)(2,1)S(1)} %add_convert_fusion), channel_id=1, source_target_pairs={{0,6},{1,7},{2,4},{3,5},{4,2},{5,3},{6,0},{7,1},{8,14},{9,15},{10,... | collective-permute-start | bytes 491528 | tf_op jit(solution)/shard_map/ppermute | solution.py:381
  36.8 0.6 %collective-permute-done.11 = f32[1,128]{1,0:T(1,128)S(1)} collective-permute-done((f32[1,128]{1,0:T(1,128)S(1)}, f32[1,128]{1,0:T(1,128)S(1)}, u32[]{:S(2)}, u32[]{:S(2)}) %collective-permute-start.11) | collective-permute-done | bytes 544 | tf_op jit(solution)/shard_map/ppermute | solution.py:381
  37.4 0.0 collective-permute-done.9
  37.4 1.6 %collective-permute-start.12 = (f32[1,128]{1,0:T(1,128)S(1)}, f32[1,128]{1,0:T(1,128)S(1)}, u32[]{:S(2)}, u32[]{:S(2)}) collective-permute-start(f32[1,128]{1,0:T(1,128)S(1)} %add_add_fusion), channel_id=1, source_target_pairs={{0,8},{8,0},{16,24},{24,16},{1,9},{9,1},{17,25},{25,17},{2,10},{10... | collective-permute-start | bytes 1544 | tf_op jit(solution)/shard_map/ppermute | solution.py:381
  39.0 2.0 %collective-permute-done.12 = f32[1,128]{1,0:T(1,128)S(1)} collective-permute-done((f32[1,128]{1,0:T(1,128)S(1)}, f32[1,128]{1,0:T(1,128)S(1)}, u32[]{:S(2)}, u32[]{:S(2)}) %collective-permute-start.12) | collective-permute-done | bytes 544 | tf_op jit(solution)/shard_map/ppermute | solution.py:381
  41.0 0.0 copy-start.1
  41.0 0.0 copy-start.5
  41.0 0.0 collective-permute-done.7.refs_8_
  41.0 1.6 %collective-permute-start.13 = (f32[1,128]{1,0:T(1,128)S(1)}, f32[1,128]{1,0:T(1,128)S(1)}, u32[]{:S(2)}, u32[]{:S(2)}) collective-permute-start(f32[1,128]{1,0:T(1,128)S(1)} %add.32), channel_id=1, source_target_pairs={{0,16},{8,24},{16,0},{24,8},{1,17},{9,25},{17,1},{25,9},{2,18},{10... | collective-permute-start | bytes 1544 | tf_op jit(solution)/shard_map/ppermute | solution.py:381
  42.6 0.0 copy-done.4
  42.6 0.0 copy-done.1
  42.6 0.0 copy-done.5
  42.6 0.6 %shard_map.132 = (f32[128,1280]{1,0:T(8,128)S(1)}, f32[128,1280]{1,0:T(8,128)S(1)}, bf16[128,64]{1,0:T(8,128)(2,1)S(1)}, f32[1,256]{1,0:T(1,128)S(1)}) custom-call(bf16[128,1280]{1,0:T(8,128)(2,1)S(1)} %bitcast.26, s32[1,128]{1,0:T(1,128)S(1)} %copy-done.5, f32[1,64]{1,0:T(1,128)S(1)} %bitcast.20), custom_call_target="tpu_custom_call" | custom-call | flops 1000000000 | bytes 2000000 | tf_op jit(solution)/shard_map/pallas_call | solution.py:25
  43.3 1.4 %collective-permute-done.13 = f32[1,128]{1,0:T(1,128)S(1)} collective-permute-done((f32[1,128]{1,0:T(1,128)S(1)}, f32[1,128]{1,0:T(1,128)S(1)}, u32[]{:S(2)}, u32[]{:S(2)}) %collective-permute-start.13) | collective-permute-done | bytes 544 | tf_op jit(solution)/shard_map/ppermute | solution.py:381
  44.6 0.0 collective-permute-done.6.refs_9_
  44.6 0.0 collective-permute-done.14.refs_2_
  44.7 0.1 collective-permute-start.15
  44.8 0.6 %bitcast_divide_fusion = (f32[64]{0:T(128)}, f32[64]{0:T(128)}) fusion(f32[64]{0:T(128)S(1)} %copy-done.1, f32[1,128]{1,0:T(1,128)S(1)} %add.33, f32[64]{0:T(128)S(1)} %copy-done), kind=kLoop, calls=%fused_computation.4 | loop fusion | flops 128 | bytes 1536 | tf_op jit(solution)/shard_map/div | solution.py:583
  45.4 0.8 %collective-permute-done.15.refs_10_ = f32[32,1280]{1,0:T(8,128)S(1)} collective-permute-done((f32[32,1280]{1,0:T(8,128)S(1)}, f32[32,1280]{1,0:T(8,128)S(1)}, u32[]{:S(2)}, u32[]{:S(2)}) %collective-permute-start.15) | collective-permute-done | bytes 163872 | tf_op jit(solution)/shard_map/ppermute | solution.py:381
  46.1 1.4 %shard_map.133 = (bf16[128,1280]{1,0:T(8,128)(2,1)}, bf16[128,1280]{1,0:T(8,128)(2,1)}, bf16[128,1280]{1,0:T(8,128)(2,1)}, bf16[128,1280]{1,0:T(8,128)(2,1)}) custom-call(bf16[128,1280]{1,0:T(8,128)(2,1)} %get-tuple-element.52.refs_0_, bf16[128,1280]{1,0:T(8,128)(2,1)} %get-tuple-element.53.refs_1_, ...), custom_call_target="tpu_custom_call", output_to_operand_aliasing={{2}: (0, {}), {3}: (1, {})} | custom-call | flops 2000000000 | bytes 4000000 | tf_op jit(solution)/shard_map/pallas_call | solution.py:25
  (7 shorter events, 0.1 us)
Async XLA Ops:
  0.6 4.3 %copy-start.2 = (bf16[1,128,1280]{2,1,0:T(8,128)(2,1)S(1)}, bf16[1,128,1280]{2,1,0:T(8,128)(2,1)}, u32[]{:S(2)}) copy-start(bf16[1,128,1280]{2,1,0:T(8,128)(2,1)} %param.8) | copy-start | bytes 983044
  0.6 4.2 %copy-start.3 = (bf16[1,128,1280]{2,1,0:T(8,128)(2,1)S(1)}, bf16[1,128,1280]{2,1,0:T(8,128)(2,1)}, u32[]{:S(2)}) copy-start(bf16[1,128,1280]{2,1,0:T(8,128)(2,1)} %param.13) | copy-start | bytes 983044
  3.2 1.7 %collective-permute-start = (bf16[32,1280]{1,0:T(8,128)(2,1)}, bf16[32,1280]{1,0:T(8,128)(2,1)S(1)}, u32[]{:S(2)}, u32[]{:S(2)}) collective-permute-start(bf16[32,1280]{1,0:T(8,128)(2,1)} %get-tuple-element.41), channel_id=1, source_target_pairs={{0,1},{1,0},{2,3},{3,2},{4,5},{5,4},{6,7},{7,6},{8,9},{9,8},{10,11... | collective-permute-start | bytes 245768 | tf_op jit(solution)/shard_map/ppermute | solution.py:381
  5.0 13.2 %collective-permute-start.1 = (bf16[128,1280]{1,0:T(8,128)(2,1)S(1)}, bf16[128,1280]{1,0:T(8,128)(2,1)S(1)}, u32[]{:S(2)}, u32[]{:S(2)}) collective-permute-start(bf16[128,1280]{1,0:T(8,128)(2,1)S(1)} %shard_map.128), channel_id=1, source_target_pairs={{0,1},{1,0},{2,3},{3,2},{4,5},{5,4},{6,7},{7,6},{8,9},{9,8},{10,11... | collective-permute-start | bytes 983048 | tf_op jit(solution)/shard_map/ppermute | solution.py:381
  5.4 12.8 %copy-start = (f32[64]{0:T(128)S(1)}, f32[64]{0:T(128)}, u32[]{:S(2)}) copy-start(f32[64]{0:T(128)} %param.14) | copy-start | bytes 772
  5.4 9.9 %collective-permute-start.3 = (bf16[64,1280]{1,0:T(8,128)(2,1)S(1)}, bf16[64,1280]{1,0:T(8,128)(2,1)S(1)}, u32[]{:S(2)}, u32[]{:S(2)}) collective-permute-start(bf16[64,1280]{1,0:T(8,128)(2,1)S(1)} %constant_dynamic-update-slice_fusion.refs_2_), channel_id=1, source_target_pairs={{0,6},{1,7},{2,4},{3,5},{4,2},{5,3},{6,0},{7,1},{8,14},{9,15},{10,... | collective-permute-start | bytes 491528 | tf_op jit(solution)/shard_map/ppermute | solution.py:381
  10.2 8.5 %collective-permute-start.2 = (bf16[64,1280]{1,0:T(8,128)(2,1)S(1)}, bf16[64,1280]{1,0:T(8,128)(2,1)S(1)}, u32[]{:S(2)}, u32[]{:S(2)}) collective-permute-start(bf16[64,1280]{1,0:T(8,128)(2,1)S(1)} %constant_dynamic-update-slice_fusion.refs_2_), channel_id=1, source_target_pairs={{0,2},{1,3},{2,0},{3,1},{4,6},{5,7},{6,4},{7,5},{8,10},{9,11},{10,... | collective-permute-start | bytes 491528 | tf_op jit(solution)/shard_map/ppermute | solution.py:381
  15.3 6.8 %collective-permute-start.4 = (bf16[64,1280]{1,0:T(8,128)(2,1)S(1)}, bf16[64,1280]{1,0:T(8,128)(2,1)S(1)}, u32[]{:S(2)}, u32[]{:S(2)}) collective-permute-start(bf16[64,1280]{1,0:T(8,128)(2,1)S(1)} %collective-permute-done.3.refs_5_), channel_id=1, source_target_pairs={{0,2},{1,3},{2,0},{3,1},{4,6},{5,7},{6,4},{7,5},{8,10},{9,11},{10,... | collective-permute-start | bytes 491528 | tf_op jit(solution)/shard_map/ppermute | solution.py:381
  25.6 7.9 %collective-permute-start.5 = (bf16[64,1280]{1,0:T(8,128)(2,1)S(1)}, bf16[64,1280]{1,0:T(8,128)(2,1)S(1)}, u32[]{:S(2)}, u32[]{:S(2)}) collective-permute-start(bf16[64,1280]{1,0:T(8,128)(2,1)S(1)} %get-tuple-element.55), channel_id=1, source_target_pairs={{0,2},{1,3},{2,0},{3,1},{4,6},{5,7},{6,4},{7,5},{8,10},{9,11},{10,... | collective-permute-start | bytes 491528 | tf_op jit(solution)/shard_map/ppermute | solution.py:381
  27.3 2.0 %collective-permute-start.8 = (f32[1,128]{1,0:T(1,128)S(1)}, f32[1,128]{1,0:T(1,128)S(1)}, u32[]{:S(2)}, u32[]{:S(2)}) collective-permute-start(f32[1,128]{1,0:T(1,128)S(1)} %get-tuple-element.58), channel_id=1, source_target_pairs={{0,1},{1,0},{2,3},{3,2},{4,5},{5,4},{6,7},{7,6},{8,9},{9,8},{10,11... | collective-permute-start | bytes 1544 | tf_op jit(solution)/shard_map/ppermute | solution.py:381
  27.3 13.7 %collective-permute-start.7 = (bf16[64,1280]{1,0:T(8,128)(2,1)S(1)}, bf16[64,1280]{1,0:T(8,128)(2,1)S(1)}, u32[]{:S(2)}, u32[]{:S(2)}) collective-permute-start(bf16[64,1280]{1,0:T(8,128)(2,1)S(1)} %get-tuple-element.57), channel_id=1, source_target_pairs={{0,2},{1,3},{2,0},{3,1},{4,6},{5,7},{6,4},{7,5},{8,10},{9,11},{10,... | collective-permute-start | bytes 491528 | tf_op jit(solution)/shard_map/ppermute | solution.py:381
  29.0 13.6 %copy-start.4 = (bf16[1,128,1280]{2,1,0:T(8,128)(2,1)S(1)}, bf16[1,128,1280]{2,1,0:T(8,128)(2,1)}, u32[]{:S(2)}) copy-start(bf16[1,128,1280]{2,1,0:T(8,128)(2,1)} %param.9) | copy-start | bytes 983044
  29.0 15.6 %collective-permute-start.14 = (bf16[128,1280]{1,0:T(8,128)(2,1)S(1)}, bf16[128,1280]{1,0:T(8,128)(2,1)S(1)}, u32[]{:S(2)}, u32[]{:S(2)}) collective-permute-start(bf16[128,1280]{1,0:T(8,128)(2,1)S(1)} %get-tuple-element.61), channel_id=1, source_target_pairs={{0,1},{1,0},{2,3},{3,2},{4,5},{5,4},{6,7},{7,6},{8,9},{9,8},{10,11... | collective-permute-start | bytes 983048 | tf_op jit(solution)/shard_map/ppermute | solution.py:381
  29.3 5.0 %collective-permute-start.10 = (f32[1,128]{1,0:T(1,128)S(1)}, f32[1,128]{1,0:T(1,128)S(1)}, u32[]{:S(2)}, u32[]{:S(2)}) collective-permute-start(f32[1,128]{1,0:T(1,128)S(1)} %add.28), channel_id=1, source_target_pairs={{0,4},{1,5},{2,6},{3,7},{4,0},{5,1},{6,2},{7,3},{8,12},{9,13},{10,... | collective-permute-start | bytes 1544 | tf_op jit(solution)/shard_map/ppermute | solution.py:381
  32.1 5.3 %collective-permute-start.11 = (f32[1,128]{1,0:T(1,128)S(1)}, f32[1,128]{1,0:T(1,128)S(1)}, u32[]{:S(2)}, u32[]{:S(2)}) collective-permute-start(f32[1,128]{1,0:T(1,128)S(1)} %add.28), channel_id=1, source_target_pairs={{0,6},{1,7},{2,4},{3,5},{4,2},{5,3},{6,0},{7,1},{8,14},{9,15},{10,... | collective-permute-start | bytes 1544 | tf_op jit(solution)/shard_map/ppermute | solution.py:381
  33.4 4.0 %collective-permute-start.9 = (f32[1,128]{1,0:T(1,128)S(1)}, f32[1,128]{1,0:T(1,128)S(1)}, u32[]{:S(2)}, u32[]{:S(2)}) collective-permute-start(f32[1,128]{1,0:T(1,128)S(1)} %add.28), channel_id=1, source_target_pairs={{0,2},{1,3},{2,0},{3,1},{4,6},{5,7},{6,4},{7,5},{8,10},{9,11},{10,... | collective-permute-start | bytes 1544 | tf_op jit(solution)/shard_map/ppermute | solution.py:381
  34.3 10.4 %collective-permute-start.6 = (bf16[64,1280]{1,0:T(8,128)(2,1)S(1)}, bf16[64,1280]{1,0:T(8,128)(2,1)S(1)}, u32[]{:S(2)}, u32[]{:S(2)}) collective-permute-start(bf16[64,1280]{1,0:T(8,128)(2,1)S(1)} %add_convert_fusion), channel_id=1, source_target_pairs={{0,6},{1,7},{2,4},{3,5},{4,2},{5,3},{6,0},{7,1},{8,14},{9,15},{10,... | collective-permute-start | bytes 491528 | tf_op jit(solution)/shard_map/ppermute | solution.py:381
  37.4 3.6 %collective-permute-start.12 = (f32[1,128]{1,0:T(1,128)S(1)}, f32[1,128]{1,0:T(1,128)S(1)}, u32[]{:S(2)}, u32[]{:S(2)}) collective-permute-start(f32[1,128]{1,0:T(1,128)S(1)} %add_add_fusion), channel_id=1, source_target_pairs={{0,8},{8,0},{16,24},{24,16},{1,9},{9,1},{17,25},{25,17},{2,10},{10... | collective-permute-start | bytes 1544 | tf_op jit(solution)/shard_map/ppermute | solution.py:381
  41.0 1.6 %copy-start.1 = (f32[64]{0:T(128)S(1)}, f32[64]{0:T(128)}, u32[]{:S(2)}) copy-start(f32[64]{0:T(128)} %param.15) | copy-start | bytes 772
  41.0 1.6 %copy-start.5 = (s32[1,128]{1,0:T(1,128)S(1)}, s32[1,128]{1,0:T(1,128)}, u32[]{:S(2)}) copy-start(s32[1,128]{1,0:T(1,128)} %unmerge_ref.1) | copy-start | bytes 1540
  41.0 3.6 %collective-permute-start.13 = (f32[1,128]{1,0:T(1,128)S(1)}, f32[1,128]{1,0:T(1,128)S(1)}, u32[]{:S(2)}, u32[]{:S(2)}) collective-permute-start(f32[1,128]{1,0:T(1,128)S(1)} %add.32), channel_id=1, source_target_pairs={{0,16},{8,24},{16,0},{24,8},{1,17},{9,25},{17,1},{25,9},{2,18},{10... | collective-permute-start | bytes 1544 | tf_op jit(solution)/shard_map/ppermute | solution.py:381
  44.7 1.5 %collective-permute-start.15 = (f32[32,1280]{1,0:T(8,128)S(1)}, f32[32,1280]{1,0:T(8,128)S(1)}, u32[]{:S(2)}, u32[]{:S(2)}) collective-permute-start(f32[32,1280]{1,0:T(8,128)S(1)} %convert_add_fusion), channel_id=1, source_target_pairs={{0,1},{1,0},{2,3},{3,2},{4,5},{5,4},{6,7},{7,6},{8,9},{9,8},{10,11... | collective-permute-start | bytes 491528 | tf_op jit(solution)/shard_map/ppermute | solution.py:381

commit v4 on v3

--- a/solution.py
+++ b/solution.py
@@ -205,6 +205,8 @@
     cell_heads = lax.broadcasted_iota(jnp.int32, (cells, TILE), 1) // head_dim
     masks = [(cell_heads == head).astype(F32).astype(BF16) for head in range(per)]
 
+    heads = range(per)
+
     def spread(array):
         return jnp.concatenate([array * mask for mask in masks], axis=0)
 
@@ -214,59 +216,64 @@
             result = jnp.where(lane_head == head, parts[head], result)
         return result
 
-    def folded(array):
-        return by_lane([array[head * cells : (head + 1) * cells] for head in range(per)])
-
-    def one_tile(tile, sums):
-        query_sum, key_sum = sums
+    def per_head(left, rights, contract):
+        return jnp.concatenate(
+            [
+                dot(left[h * head_dim : (h + 1) * head_dim], rights[h], ((1,), (contract,)))
+                for h in heads
+            ],
+            axis=0,
+        ).T
+
+    def forward(tile):
         lane = lanes_at(tile)
         value_lane = lanes_at(width // TILE + tile)
         source = lanes_at(start // TILE + tile)
         queries = query_ref[:, source]
         upstream = upstream_ref[:, source]
         weighted = jnp.zeros((rows, TILE), F32)
-        totals = [jnp.zeros((rows, 1), F32) for _ in range(per)]
+        totals = [jnp.zeros((rows, 1), F32) for _ in heads]
         held = []
         for first in range(0, blocks, group):
             members = block_refs[first : first + group]
             keys = jnp.concatenate([ref[:, lane] for ref in members], axis=0)
-            spread_keys = spread(keys)
-            spread_values = spread(
-                jnp.concatenate([ref[:, value_lane] for ref in members], axis=0)
-            )
-            scores = dot(queries, spread_keys, ((1,), (1,)))
+            values = jnp.concatenate([ref[:, value_lane] for ref in members], axis=0)
+            scores = dot(queries, spread(keys), ((1,), (1,)))
             exp_scores = jnp.exp2(scores * exponent)
-            weighted += dot(exp_scores.astype(BF16), spread_values)
-            exp_parts = [exp_scores[:, h * cells : (h + 1) * cells] for h in range(per)]
+            exp_parts = [exp_scores[:, h * cells : (h + 1) * cells] for h in heads]
+            weighted += dot(exp_scores.astype(BF16), spread(values))
             totals = [
                 total + jnp.sum(part, axis=1, keepdims=True)
                 for total, part in zip(totals, exp_parts)
             ]
-            held.append((keys, spread_keys, spread_values, exp_parts))
+            held.append((keys, dot(upstream, spread(values), ((1,), (1,))), exp_parts))
         inverses = [1.0 / total for total in totals]
         attended = (weighted * by_lane(inverses)).astype(BF16)
         attended_ref[:, lane] = attended
         products = upstream.astype(F32) * attended.astype(F32)
         inners = [
-            jnp.sum(jnp.where(lane_head == h, products, 0.0), axis=1, keepdims=True)
-            for h in range(per)
+            jnp.sum(jnp.where(lane_head == h, products, 0.0), axis=1, keepdims=True) for h in heads
         ]
+        return queries, upstream, held, inverses, inners
+
+    def backward(tile, kept, sums):
+        query_sum, key_sum = sums
+        queries, upstream, held, inverses, inners = kept
+        lane = lanes_at(tile)
+        value_lane = lanes_at(width // TILE + tile)
+        queries_turned, upstream_turned = queries.T, upstream.T
         grad_queries = jnp.zeros((rows, TILE), F32)
-        for index, (keys, spread_keys, spread_values, exp_parts) in enumerate(held):
-            grad_weights = dot(upstream, spread_values, ((1,), (1,)))
+        for index, (keys, grad_weights, exp_parts) in enumerate(held):
             attention = [part * inverse for part, inverse in zip(exp_parts, inverses)]
-            grad_scores = jnp.concatenate(
-                [
-                    (attention[h] * (grad_weights[:, h * cells : (h + 1) * cells] - inners[h]))
-                    .astype(BF16)
-                    for h in range(per)
-                ],
-                axis=1,
-            )
-            attention_bf = jnp.concatenate([part.astype(BF16) for part in attention], axis=1)
-            grad_queries += dot(grad_scores, spread_keys)
-            grad_keys = folded(dot(grad_scores, queries, ((0,), (0,)))) * scale
-            grad_values = folded(dot(attention_bf, upstream, ((0,), (0,))))
+            grad_scores = [
+                (attention[h] * (grad_weights[:, h * cells : (h + 1) * cells] - inners[h])).astype(
+                    BF16
+                )
+                for h in heads
+            ]
+            grad_queries += dot(jnp.concatenate(grad_scores, axis=1), spread(keys))
+            grad_keys = per_head(queries_turned, grad_scores, 0) * scale
+            grad_values = per_head(upstream_turned, [part.astype(BF16) for part in attention], 0)
             key_sum += jnp.sum(grad_keys * keys.astype(F32), axis=0, keepdims=True)
             for member in range(group):
                 ref = part_refs[index * group + member]
@@ -280,10 +287,15 @@
 
     sums = (jnp.zeros((1, TILE), F32), jnp.zeros((1, TILE), F32))
     if blocks == group:
+        kept = forward(0)
         for tile in range(width // TILE):
-            sums = one_tile(tile, sums)
+            ahead = forward(tile + 1) if tile + 1 < width // TILE else None
+            sums = backward(tile, kept, sums)
+            kept = ahead
     else:
-        sums = lax.fori_loop(0, width // TILE, one_tile, sums)
+        sums = lax.fori_loop(
+            0, width // TILE, lambda tile, sums: backward(tile, forward(tile), sums), sums
+        )
 
     def per_channel(row):
         return sum(row[:, at : at + head_dim] for at in range(0, TILE, head_dim))
@@ -411,6 +423,7 @@
         chip_steps = [("seq", CORES << bit) for bit in range(chips.bit_length() - 1)]
         self.table = {
             "c": [("seq", 1)],
+            "I": [("img", *range(1, images))],
             "y": image_steps[:1],
             "x": image_steps[1:],
             "z": chip_steps[:1],
@@ -425,7 +438,7 @@
                 self.gains = sum(arrived, self.gains)
 
 
-OPT = dict(split=0, steps="cD|yx|", near=1, hb=0, sb=2, k4=0, kc=1.7, pc=1.0)
+OPT = dict(tc=1, split=0, steps="cD|yx|", near=1, hb=0, sb=2, k4=4, kc=0.1, pc=1.0)
 
 
 def chunk_bounds(half):
@@ -535,15 +548,24 @@
     if chips == 1:
         straight = across = [[] for _ in bounds]
     near = [chip_reduce(part[: max(chips // 2, 1)]) for part in parts]
+    if OPT["tc"]:
+        near_crossed = [exchange(added([t[cells:] for t in terms]), "seq", 1) for terms in near]
     if OPT["split"]:
         crossed = [exchange(added([term[cells:] for term in terms]), "seq", 1) for terms in near]
     else:
         crossed = None
-    if OPT["k4"] != 1:
+    if OPT["k4"] == 4:
+        _, query_unit = lax.optimization_barrier((near, query_unit))
+    if OPT["k4"] == 5:
+        _, query_unit = lax.optimization_barrier((sums, query_unit))
+    if OPT["k4"] in (0, 2, 4, 5):
         attended_half, grad_half, sent_part = query_back()
     if OPT["near"] == 1:
         rest.advance(next_steps[:1])
         near, rest.gains = lax.optimization_barrier((near, rest.gains))
+        if OPT["k4"] == 3:
+            query_unit, rest.gains = lax.optimization_barrier((query_unit, rest.gains))
+            attended_half, grad_half, sent_part = query_back()
         rest.advance(next_steps[1:])
     elif OPT["near"] == 2:
         near, rest.gains = lax.optimization_barrier((near, rest.gains))
@@ -551,11 +573,19 @@
     else:
         rest.advance(next_steps)
     arrived_part = exchange(sent_part, "seq", 1)
-    straight, across, crossed, rest.gains, arrived_part = lax.optimization_barrier(
-        (straight, across, crossed, rest.gains, arrived_part)
-    )
+    if OPT["tc"]:
+        straight, near_crossed, rest.gains, arrived_part = lax.optimization_barrier(
+            (straight, near_crossed, rest.gains, arrived_part)
+        )
+    else:
+        straight, rest.gains, arrived_part = lax.optimization_barrier(
+            (straight, rest.gains, arrived_part)
+        )
     own_terms = [first + last for first, last in zip(near, straight)]
-    if not OPT["split"]:
+    if OPT["tc"] and chips > 1:
+        crossed = near_crossed
+        across = [[exchange(term[cells:], "seq", 1) for term in terms] for terms in straight]
+    elif not OPT["split"]:
         crossed = [exchange(added([t[cells:] for t in terms]), "seq", 1) for terms in own_terms]
     rest.advance(last_steps)
     gain_total = rest.gains[0]

time: 47.7 us -> 47 us (0.985)
  Pallas kernels: 10.1 us -> 9.43 us
    pallas_call x7, Pallas kernels: 10.1 us -> 9.43 us  [call(): pl.pallas_call(kernel, out_shape=[jax.ShapeDtypeStruct(shape, kind) for s...]
    ppermute x16 -> x17, starting transfers between devices: 21.6 us -> 21.3 us  [exchange(): lax.ppermute(array, axis, [(i, i ^ apart) for i in range(lax.axis_size(ax...]
    ppermute x16 -> x17, waiting for transfers between devices: 13.5 us -> 13.7 us  [exchange(): lax.ppermute(array, axis, [(i, i ^ apart) for i in range(lax.axis_size(ax...]
  transfers between devices with their start and end apart: 16 -> 17, of which waited for: 7 -> 8; matrix products, arithmetic and copies ran while one was open for 3% -> 3% of each run, Pallas kernels for 5% -> 5%
where the time goes in v4:
time: 47 us; the launch traced here: 46.9 us
  starting transfers between devices  21.3 us (45%)
  waiting for transfers between devices  13.7 us (29%)
  Pallas kernels  9.43 us (20%)
  local copies, waits for them, and re-layouts  0.94 us (2%)
  between operations  0.79 us (2%)
  other arithmetic  0.66 us (1%)
    ppermute x17, starting transfers between devices, exchange(): lax.ppermute(array, axis, [(i, i ^ apart) for i in range(lax.axis_size(ax...  21.3 us
    ppermute x17, waiting for transfers between devices, exchange(): lax.ppermute(array, axis, [(i, i ^ apart) for i in range(lax.axis_size(ax...  13.7 us
    pallas_call x7, Pallas kernels, call(): pl.pallas_call(kernel, out_shape=[jax.ShapeDtypeStruct(shape, kind) for s...  9.43 us
  transfers between devices with their start and end apart: 17, of which 8 were waited for; matrix products, arithmetic and copies ran while one was open for 3% of the time, Pallas kernels for 5%

profile of v4, /device:TPU:0, one launch (start us, length us, event | category | flops | bytes accessed | tf_op | source)
XLA Modules:
  0.0 46.9 jit_solution(12664479935744072153)
XLA Ops:
  0.6 0.0 copy-start.2
  0.6 0.0 copy-start.3
  0.7 2.6 %shard_map.127 = (bf16[32,1280]{1,0:T(8,128)(2,1)}, bf16[32,1280]{1,0:T(8,128)(2,1)}) custom-call(bf16[128,1280]{1,0:T(8,128)(2,1)} %bitcast.25, bf16[128,1280]{1,0:T(8,128)(2,1)} %bitcast.27, s32[4,32]{1,0:T(4,128)} %bitcast.30, f32[1,64]{1,0:T(1,128)} %bitcast.19), custom_call_target="tpu_custom_call" | custom-call | flops 1000000000 | bytes 2000000 | tf_op jit(solution)/shard_map/pallas_call | solution.py:25
  3.2 0.5 %collective-permute-start = (bf16[32,1280]{1,0:T(8,128)(2,1)}, bf16[32,1280]{1,0:T(8,128)(2,1)S(1)}, u32[]{:S(2)}, u32[]{:S(2)}) collective-permute-start(bf16[32,1280]{1,0:T(8,128)(2,1)} %get-tuple-element.43), channel_id=1, source_target_pairs={{0,1},{1,0},{2,3},{3,2},{4,5},{5,4},{6,7},{7,6},{8,9},{9,8},{10,11... | collective-permute-start | bytes 245768 | tf_op jit(solution)/shard_map/ppermute | solution.py:393
  3.8 0.9 %constant_dynamic-update-slice_fusion.1 = bf16[64,1280]{1,0:T(8,128)(2,1)S(1)} fusion(bf16[32,1280]{1,0:T(8,128)(2,1)} %get-tuple-element.48), kind=kLoop, calls=%fused_computation.3 | loop fusion | bytes 163840
  4.6 0.2 collective-permute-done
  4.9 0.0 copy-done.2
  4.9 0.0 copy-done.3
  4.9 0.1 shard_map.128
  5.0 0.4 collective-permute-start.1
  5.4 0.0 copy-start
  5.4 4.8 %collective-permute-start.3 = (bf16[64,1280]{1,0:T(8,128)(2,1)S(1)}, bf16[64,1280]{1,0:T(8,128)(2,1)S(1)}, u32[]{:S(2)}, u32[]{:S(2)}) collective-permute-start(bf16[64,1280]{1,0:T(8,128)(2,1)S(1)} %constant_dynamic-update-slice_fusion.refs_2_), channel_id=1, source_target_pairs={{0,6},{1,7},{2,4},{3,5},{4,2},{5,3},{6,0},{7,1},{8,14},{9,15},{10,... | collective-permute-start | bytes 491528 | tf_op jit(solution)/shard_map/ppermute | solution.py:393
  10.2 0.0 collective-permute-start.2
  10.2 5.1 %collective-permute-done.3.refs_5_ = bf16[64,1280]{1,0:T(8,128)(2,1)S(1)} collective-permute-done((bf16[64,1280]{1,0:T(8,128)(2,1)S(1)}, bf16[64,1280]{1,0:T(8,128)(2,1)S(1)}, u32[]{:S(2)}, u32[]{:S(2)}) %collective-permute-start.3) | collective-permute-done | bytes 163872 | tf_op jit(solution)/shard_map/ppermute | solution.py:393
  15.3 2.8 %collective-permute-start.4 = (bf16[64,1280]{1,0:T(8,128)(2,1)S(1)}, bf16[64,1280]{1,0:T(8,128)(2,1)S(1)}, u32[]{:S(2)}, u32[]{:S(2)}) collective-permute-start(bf16[64,1280]{1,0:T(8,128)(2,1)S(1)} %collective-permute-done.3.refs_5_), channel_id=1, source_target_pairs={{0,2},{1,3},{2,0},{3,1},{4,6},{5,7},{6,4},{7,5},{8,10},{9,11},{10,... | collective-permute-start | bytes 491528 | tf_op jit(solution)/shard_map/ppermute | solution.py:393
  18.1 0.0 collective-permute-done.1.arrived_ref
  18.2 0.0 copy-done
  18.2 0.5 %shard_map.129 = (f32[256,640]{1,0:T(8,128)S(1)}, f32[256,640]{1,0:T(8,128)S(1)}, bf16[256,640]{1,0:T(8,128)(2,1)S(1)}, bf16[256,640]{1,0:T(8,128)(2,1)S(1)}) custom-call(bf16[128,1280]{1,0:T(8,128)(2,1)S(1)} %bitcast.22, bf16[128,1280]{1,0:T(8,128)(2,1)S(1)} %bitcast.24, bf16[128,1280]{1,0:T(8,128)(2,1)S(1)} %collective-permute-done.1.arrived_ref, ...), custom_call_target="tpu_custom_call" | custom-call | flops 1000000000 | bytes 2000000 | tf_op jit(solution)/shard_map/pallas_call | solution.py:25
  18.7 0.0 collective-permute-done.2.refs_3_
  18.7 3.4 %collective-permute-done.4.refs_4_ = bf16[64,1280]{1,0:T(8,128)(2,1)S(1)} collective-permute-done((bf16[64,1280]{1,0:T(8,128)(2,1)S(1)}, bf16[64,1280]{1,0:T(8,128)(2,1)S(1)}, u32[]{:S(2)}, u32[]{:S(2)}) %collective-permute-start.4) | collective-permute-done | bytes 163872 | tf_op jit(solution)/shard_map/ppermute | solution.py:393
  22.1 2.9 %shard_map.130 = (bf16[256,640]{1,0:T(8,128)(2,1)S(1)}, f32[256,640]{1,0:T(8,128)S(1)}, f32[1,128]{1,0:T(1,128)S(1)}, f32[64,1280]{1,0:T(8,128)S(1)}, bf16[64,12...) custom-call(bf16[256,640]{1,0:T(8,128)(2,1)S(1)} %get-tuple-element.46.refs_0_, ...), custom_call_target="tpu_custom_call" | custom-call | flops 3500000000 | bytes 7000000 | tf_op jit(solution)/shard_map/pallas_call | solution.py:25
  24.9 1.8 %collective-permute-start.5 = (bf16[64,1280]{1,0:T(8,128)(2,1)S(1)}, bf16[64,1280]{1,0:T(8,128)(2,1)S(1)}, u32[]{:S(2)}, u32[]{:S(2)}) collective-permute-start(bf16[64,1280]{1,0:T(8,128)(2,1)S(1)} %get-tuple-element.51), channel_id=1, source_target_pairs={{0,2},{1,3},{2,0},{3,1},{4,6},{5,7},{6,4},{7,5},{8,10},{9,11},{10,... | collective-permute-start | bytes 491528 | tf_op jit(solution)/shard_map/ppermute | solution.py:393
  26.7 0.0 collective-permute-start.9
  26.7 0.3 collective-permute-start.6
  27.0 0.8 %collective-permute-done.9 = f32[1,128]{1,0:T(1,128)S(1)} collective-permute-done((f32[1,128]{1,0:T(1,128)S(1)}, f32[1,128]{1,0:T(1,128)S(1)}, u32[]{:S(2)}, u32[]{:S(2)}) %collective-permute-start.9) | collective-permute-done | bytes 544 | tf_op jit(solution)/shard_map/ppermute | solution.py:393
  27.8 0.9 %collective-permute-start.10 = (f32[1,128]{1,0:T(1,128)S(1)}, f32[1,128]{1,0:T(1,128)S(1)}, u32[]{:S(2)}, u32[]{:S(2)}) collective-permute-start(f32[1,128]{1,0:T(1,128)S(1)} %add.26), channel_id=1, source_target_pairs={{0,2},{1,3},{2,0},{3,1},{4,6},{5,7},{6,4},{7,5},{8,10},{9,11},{10,... | collective-permute-start | bytes 1544 | tf_op jit(solution)/shard_map/ppermute | solution.py:393
  28.7 2.1 %collective-permute-start.11 = (f32[1,128]{1,0:T(1,128)S(1)}, f32[1,128]{1,0:T(1,128)S(1)}, u32[]{:S(2)}, u32[]{:S(2)}) collective-permute-start(f32[1,128]{1,0:T(1,128)S(1)} %add.26), channel_id=1, source_target_pairs={{0,4},{1,5},{2,6},{3,7},{4,0},{5,1},{6,2},{7,3},{8,12},{9,13},{10,... | collective-permute-start | bytes 1544 | tf_op jit(solution)/shard_map/ppermute | solution.py:393
  30.9 1.3 %collective-permute-start.12 = (f32[1,128]{1,0:T(1,128)S(1)}, f32[1,128]{1,0:T(1,128)S(1)}, u32[]{:S(2)}, u32[]{:S(2)}) collective-permute-start(f32[1,128]{1,0:T(1,128)S(1)} %add.26), channel_id=1, source_target_pairs={{0,6},{1,7},{2,4},{3,5},{4,2},{5,3},{6,0},{7,1},{8,14},{9,15},{10,... | collective-permute-start | bytes 1544 | tf_op jit(solution)/shard_map/ppermute | solution.py:393
  32.2 0.0 collective-permute-done.5.refs_8_
  32.2 0.1 collective-permute-start.8
  32.3 1.4 %shard_map.131 = (bf16[128,1280]{1,0:T(8,128)(2,1)}, bf16[128,1280]{1,0:T(8,128)(2,1)}, bf16[128,1280]{1,0:T(8,128)(2,1)S(1)}) custom-call(f32[256,640]{1,0:T(8,128)S(1)} %get-tuple-element.53.unit_ref, f32[256,640]{1,0:T(8,128)S(1)} %get-tuple-element.54.scale_ref, f32[1,64]{1,0:T(1,128)S(1)} %bitcast.18, bf16[256,640]{1,0:T(8,128)(2,1)S(1)} %get-tuple-element.55.refs_0_, ...), custom_call_target="tpu_custom_call" | custom-call | flops 100000000 | bytes 200000 | tf_op jit(solution)/shard_map/pallas_call | solution.py:25
  33.7 0.0 copy-start.4
  33.7 0.1 collective-permute-done.6
  33.8 0.5 %collective-permute-start.15 = (bf16[128,1280]{1,0:T(8,128)(2,1)S(1)}, bf16[128,1280]{1,0:T(8,128)(2,1)S(1)}, u32[]{:S(2)}, u32[]{:S(2)}) collective-permute-start(bf16[128,1280]{1,0:T(8,128)(2,1)S(1)} %get-tuple-element.64), channel_id=1, source_target_pairs={{0,1},{1,0},{2,3},{3,2},{4,5},{5,4},{6,7},{7,6},{8,9},{9,8},{10,11... | collective-permute-start | bytes 983048 | tf_op jit(solution)/shard_map/ppermute | solution.py:393
  34.3 0.0 collective-permute-done.10
  34.3 2.5 %collective-permute-start.7 = (bf16[64,1280]{1,0:T(8,128)(2,1)S(1)}, bf16[64,1280]{1,0:T(8,128)(2,1)S(1)}, u32[]{:S(2)}, u32[]{:S(2)}) collective-permute-start(bf16[64,1280]{1,0:T(8,128)(2,1)S(1)} %add_convert_fusion), channel_id=1, source_target_pairs={{0,6},{1,7},{2,4},{3,5},{4,2},{5,3},{6,0},{7,1},{8,14},{9,15},{10,... | collective-permute-start | bytes 491528 | tf_op jit(solution)/shard_map/ppermute | solution.py:393
  36.9 0.0 collective-permute-done.11
  36.9 0.0 collective-permute-done.12
  36.9 0.0 copy-start.1
  36.9 0.0 copy-start.5
  36.9 1.6 %collective-permute-start.13 = (f32[1,128]{1,0:T(1,128)S(1)}, f32[1,128]{1,0:T(1,128)S(1)}, u32[]{:S(2)}, u32[]{:S(2)}) collective-permute-start(f32[1,128]{1,0:T(1,128)S(1)} %add_add_fusion), channel_id=1, source_target_pairs={{0,8},{8,0},{16,24},{24,16},{1,9},{9,1},{17,25},{25,17},{2,10},{10... | collective-permute-start | bytes 1544 | tf_op jit(solution)/shard_map/ppermute | solution.py:393
  38.5 2.0 %collective-permute-done.13 = f32[1,128]{1,0:T(1,128)S(1)} collective-permute-done((f32[1,128]{1,0:T(1,128)S(1)}, f32[1,128]{1,0:T(1,128)S(1)}, u32[]{:S(2)}, u32[]{:S(2)}) %collective-permute-start.13) | collective-permute-done | bytes 544 | tf_op jit(solution)/shard_map/ppermute | solution.py:393
  40.5 1.5 %collective-permute-start.14 = (f32[1,128]{1,0:T(1,128)S(1)}, f32[1,128]{1,0:T(1,128)S(1)}, u32[]{:S(2)}, u32[]{:S(2)}) collective-permute-start(f32[1,128]{1,0:T(1,128)S(1)} %add.30), channel_id=1, source_target_pairs={{0,16},{8,24},{16,0},{24,8},{1,17},{9,25},{17,1},{25,9},{2,18},{10... | collective-permute-start | bytes 1544 | tf_op jit(solution)/shard_map/ppermute | solution.py:393
  42.0 0.0 copy-done.4
  42.0 0.0 copy-done.1
  42.1 0.0 copy-done.5
  42.1 0.6 %shard_map.132 = (f32[128,1280]{1,0:T(8,128)S(1)}, f32[128,1280]{1,0:T(8,128)S(1)}, bf16[128,64]{1,0:T(8,128)(2,1)S(1)}, f32[1,256]{1,0:T(1,128)S(1)}) custom-call(bf16[128,1280]{1,0:T(8,128)(2,1)S(1)} %bitcast.26, s32[1,128]{1,0:T(1,128)S(1)} %copy-done.5, f32[1,64]{1,0:T(1,128)S(1)} %bitcast.20), custom_call_target="tpu_custom_call" | custom-call | flops 1000000000 | bytes 2000000 | tf_op jit(solution)/shard_map/pallas_call | solution.py:25
  42.7 1.4 %collective-permute-done.14 = f32[1,128]{1,0:T(1,128)S(1)} collective-permute-done((f32[1,128]{1,0:T(1,128)S(1)}, f32[1,128]{1,0:T(1,128)S(1)}, u32[]{:S(2)}, u32[]{:S(2)}) %collective-permute-start.14) | collective-permute-done | bytes 544 | tf_op jit(solution)/shard_map/ppermute | solution.py:393
  44.1 0.0 collective-permute-done.8.refs_10_
  44.1 0.0 collective-permute-done.7.refs_9_
  44.1 0.0 collective-permute-done.15.refs_2_
  44.1 0.1 collective-permute-start.16
  44.2 0.6 %bitcast_divide_fusion = (f32[64]{0:T(128)}, f32[64]{0:T(128)}) fusion(f32[64]{0:T(128)S(1)} %copy-done.1, f32[1,128]{1,0:T(1,128)S(1)} %add.31, f32[64]{0:T(128)S(1)} %copy-done), kind=kLoop, calls=%fused_computation.4 | loop fusion | flops 128 | bytes 1536 | tf_op jit(solution)/shard_map/div | solution.py:613
  44.8 0.7 %collective-permute-done.16.refs_11_ = bf16[32,1280]{1,0:T(8,128)(2,1)S(1)} collective-permute-done((bf16[32,1280]{1,0:T(8,128)(2,1)S(1)}, bf16[32,1280]{1,0:T(8,128)(2,1)S(1)}, u32[]{:S(2)}, u32[]{:S(2)}) %collective-permute-start.16) | collective-permute-done | bytes 81952 | tf_op jit(solution)/shard_map/ppermute | solution.py:393
  45.5 1.4 %shard_map.133 = (bf16[128,1280]{1,0:T(8,128)(2,1)}, bf16[128,1280]{1,0:T(8,128)(2,1)}, bf16[128,1280]{1,0:T(8,128)(2,1)}, bf16[128,1280]{1,0:T(8,128)(2,1)}) custom-call(bf16[128,1280]{1,0:T(8,128)(2,1)} %get-tuple-element.57.refs_0_, bf16[128,1280]{1,0:T(8,128)(2,1)} %get-tuple-element.58.refs_1_, ...), custom_call_target="tpu_custom_call", output_to_operand_aliasing={{2}: (0, {}), {3}: (1, {})} | custom-call | flops 2000000000 | bytes 4000000 | tf_op jit(solution)/shard_map/pallas_call | solution.py:25
  (8 shorter events, 0.1 us)
Async XLA Ops:
  0.6 4.3 %copy-start.2 = (bf16[1,128,1280]{2,1,0:T(8,128)(2,1)S(1)}, bf16[1,128,1280]{2,1,0:T(8,128)(2,1)}, u32[]{:S(2)}) copy-start(bf16[1,128,1280]{2,1,0:T(8,128)(2,1)} %param.8) | copy-start | bytes 983044
  0.6 4.2 %copy-start.3 = (bf16[1,128,1280]{2,1,0:T(8,128)(2,1)S(1)}, bf16[1,128,1280]{2,1,0:T(8,128)(2,1)}, u32[]{:S(2)}) copy-start(bf16[1,128,1280]{2,1,0:T(8,128)(2,1)} %param.13) | copy-start | bytes 983044
  3.2 1.7 %collective-permute-start = (bf16[32,1280]{1,0:T(8,128)(2,1)}, bf16[32,1280]{1,0:T(8,128)(2,1)S(1)}, u32[]{:S(2)}, u32[]{:S(2)}) collective-permute-start(bf16[32,1280]{1,0:T(8,128)(2,1)} %get-tuple-element.43), channel_id=1, source_target_pairs={{0,1},{1,0},{2,3},{3,2},{4,5},{5,4},{6,7},{7,6},{8,9},{9,8},{10,11... | collective-permute-start | bytes 245768 | tf_op jit(solution)/shard_map/ppermute | solution.py:393
  5.0 13.2 %collective-permute-start.1 = (bf16[128,1280]{1,0:T(8,128)(2,1)S(1)}, bf16[128,1280]{1,0:T(8,128)(2,1)S(1)}, u32[]{:S(2)}, u32[]{:S(2)}) collective-permute-start(bf16[128,1280]{1,0:T(8,128)(2,1)S(1)} %shard_map.128), channel_id=1, source_target_pairs={{0,1},{1,0},{2,3},{3,2},{4,5},{5,4},{6,7},{7,6},{8,9},{9,8},{10,11... | collective-permute-start | bytes 983048 | tf_op jit(solution)/shard_map/ppermute | solution.py:393
  5.4 12.8 %copy-start = (f32[64]{0:T(128)S(1)}, f32[64]{0:T(128)}, u32[]{:S(2)}) copy-start(f32[64]{0:T(128)} %param.14) | copy-start | bytes 772
  5.4 9.9 %collective-permute-start.3 = (bf16[64,1280]{1,0:T(8,128)(2,1)S(1)}, bf16[64,1280]{1,0:T(8,128)(2,1)S(1)}, u32[]{:S(2)}, u32[]{:S(2)}) collective-permute-start(bf16[64,1280]{1,0:T(8,128)(2,1)S(1)} %constant_dynamic-update-slice_fusion.refs_2_), channel_id=1, source_target_pairs={{0,6},{1,7},{2,4},{3,5},{4,2},{5,3},{6,0},{7,1},{8,14},{9,15},{10,... | collective-permute-start | bytes 491528 | tf_op jit(solution)/shard_map/ppermute | solution.py:393
  10.2 8.5 %collective-permute-start.2 = (bf16[64,1280]{1,0:T(8,128)(2,1)S(1)}, bf16[64,1280]{1,0:T(8,128)(2,1)S(1)}, u32[]{:S(2)}, u32[]{:S(2)}) collective-permute-start(bf16[64,1280]{1,0:T(8,128)(2,1)S(1)} %constant_dynamic-update-slice_fusion.refs_2_), channel_id=1, source_target_pairs={{0,2},{1,3},{2,0},{3,1},{4,6},{5,7},{6,4},{7,5},{8,10},{9,11},{10,... | collective-permute-start | bytes 491528 | tf_op jit(solution)/shard_map/ppermute | solution.py:393
  15.3 6.8 %collective-permute-start.4 = (bf16[64,1280]{1,0:T(8,128)(2,1)S(1)}, bf16[64,1280]{1,0:T(8,128)(2,1)S(1)}, u32[]{:S(2)}, u32[]{:S(2)}) collective-permute-start(bf16[64,1280]{1,0:T(8,128)(2,1)S(1)} %collective-permute-done.3.refs_5_), channel_id=1, source_target_pairs={{0,2},{1,3},{2,0},{3,1},{4,6},{5,7},{6,4},{7,5},{8,10},{9,11},{10,... | collective-permute-start | bytes 491528 | tf_op jit(solution)/shard_map/ppermute | solution.py:393
  24.9 7.3 %collective-permute-start.5 = (bf16[64,1280]{1,0:T(8,128)(2,1)S(1)}, bf16[64,1280]{1,0:T(8,128)(2,1)S(1)}, u32[]{:S(2)}, u32[]{:S(2)}) collective-permute-start(bf16[64,1280]{1,0:T(8,128)(2,1)S(1)} %get-tuple-element.51), channel_id=1, source_target_pairs={{0,2},{1,3},{2,0},{3,1},{4,6},{5,7},{6,4},{7,5},{8,10},{9,11},{10,... | collective-permute-start | bytes 491528 | tf_op jit(solution)/shard_map/ppermute | solution.py:393
  26.7 1.1 %collective-permute-start.9 = (f32[1,128]{1,0:T(1,128)S(1)}, f32[1,128]{1,0:T(1,128)S(1)}, u32[]{:S(2)}, u32[]{:S(2)}) collective-permute-start(f32[1,128]{1,0:T(1,128)S(1)} %get-tuple-element.61), channel_id=1, source_target_pairs={{0,1},{1,0},{2,3},{3,2},{4,5},{5,4},{6,7},{7,6},{8,9},{9,8},{10,11... | collective-permute-start | bytes 1544 | tf_op jit(solution)/shard_map/ppermute | solution.py:393
  26.7 7.1 %collective-permute-start.6 = (bf16[64,1280]{1,0:T(8,128)(2,1)S(1)}, bf16[64,1280]{1,0:T(8,128)(2,1)S(1)}, u32[]{:S(2)}, u32[]{:S(2)}) collective-permute-start(bf16[64,1280]{1,0:T(8,128)(2,1)S(1)} %get-tuple-element.60), channel_id=1, source_target_pairs={{0,2},{1,3},{2,0},{3,1},{4,6},{5,7},{6,4},{7,5},{8,10},{9,11},{10,... | collective-permute-start | bytes 491528 | tf_op jit(solution)/shard_map/ppermute | solution.py:393
  27.8 6.5 %collective-permute-start.10 = (f32[1,128]{1,0:T(1,128)S(1)}, f32[1,128]{1,0:T(1,128)S(1)}, u32[]{:S(2)}, u32[]{:S(2)}) collective-permute-start(f32[1,128]{1,0:T(1,128)S(1)} %add.26), channel_id=1, source_target_pairs={{0,2},{1,3},{2,0},{3,1},{4,6},{5,7},{6,4},{7,5},{8,10},{9,11},{10,... | collective-permute-start | bytes 1544 | tf_op jit(solution)/shard_map/ppermute | solution.py:393
  28.7 8.1 %collective-permute-start.11 = (f32[1,128]{1,0:T(1,128)S(1)}, f32[1,128]{1,0:T(1,128)S(1)}, u32[]{:S(2)}, u32[]{:S(2)}) collective-permute-start(f32[1,128]{1,0:T(1,128)S(1)} %add.26), channel_id=1, source_target_pairs={{0,4},{1,5},{2,6},{3,7},{4,0},{5,1},{6,2},{7,3},{8,12},{9,13},{10,... | collective-permute-start | bytes 1544 | tf_op jit(solution)/shard_map/ppermute | solution.py:393
  30.9 6.0 %collective-permute-start.12 = (f32[1,128]{1,0:T(1,128)S(1)}, f32[1,128]{1,0:T(1,128)S(1)}, u32[]{:S(2)}, u32[]{:S(2)}) collective-permute-start(f32[1,128]{1,0:T(1,128)S(1)} %add.26), channel_id=1, source_target_pairs={{0,6},{1,7},{2,4},{3,5},{4,2},{5,3},{6,0},{7,1},{8,14},{9,15},{10,... | collective-permute-start | bytes 1544 | tf_op jit(solution)/shard_map/ppermute | solution.py:393
  32.2 11.8 %collective-permute-start.8 = (f32[32,1280]{1,0:T(8,128)S(1)}, f32[32,1280]{1,0:T(8,128)S(1)}, u32[]{:S(2)}, u32[]{:S(2)}) collective-permute-start(f32[32,1280]{1,0:T(8,128)S(1)} %convert_add_fusion), channel_id=1, source_target_pairs={{0,1},{1,0},{2,3},{3,2},{4,5},{5,4},{6,7},{7,6},{8,9},{9,8},{10,11... | collective-permute-start | bytes 491528 | tf_op jit(solution)/shard_map/ppermute | solution.py:393
  33.7 8.3 %copy-start.4 = (bf16[1,128,1280]{2,1,0:T(8,128)(2,1)S(1)}, bf16[1,128,1280]{2,1,0:T(8,128)(2,1)}, u32[]{:S(2)}) copy-start(bf16[1,128,1280]{2,1,0:T(8,128)(2,1)} %param.9) | copy-start | bytes 983044
  33.8 10.3 %collective-permute-start.15 = (bf16[128,1280]{1,0:T(8,128)(2,1)S(1)}, bf16[128,1280]{1,0:T(8,128)(2,1)S(1)}, u32[]{:S(2)}, u32[]{:S(2)}) collective-permute-start(bf16[128,1280]{1,0:T(8,128)(2,1)S(1)} %get-tuple-element.64), channel_id=1, source_target_pairs={{0,1},{1,0},{2,3},{3,2},{4,5},{5,4},{6,7},{7,6},{8,9},{9,8},{10,11... | collective-permute-start | bytes 983048 | tf_op jit(solution)/shard_map/ppermute | solution.py:393
  34.3 9.7 %collective-permute-start.7 = (bf16[64,1280]{1,0:T(8,128)(2,1)S(1)}, bf16[64,1280]{1,0:T(8,128)(2,1)S(1)}, u32[]{:S(2)}, u32[]{:S(2)}) collective-permute-start(bf16[64,1280]{1,0:T(8,128)(2,1)S(1)} %add_convert_fusion), channel_id=1, source_target_pairs={{0,6},{1,7},{2,4},{3,5},{4,2},{5,3},{6,0},{7,1},{8,14},{9,15},{10,... | collective-permute-start | bytes 491528 | tf_op jit(solution)/shard_map/ppermute | solution.py:393
  36.9 5.2 %copy-start.1 = (f32[64]{0:T(128)S(1)}, f32[64]{0:T(128)}, u32[]{:S(2)}) copy-start(f32[64]{0:T(128)} %param.15) | copy-start | bytes 772
  36.9 5.1 %copy-start.5 = (s32[1,128]{1,0:T(1,128)S(1)}, s32[1,128]{1,0:T(1,128)}, u32[]{:S(2)}) copy-start(s32[1,128]{1,0:T(1,128)} %unmerge_ref.1) | copy-start | bytes 1540
  36.9 3.6 %collective-permute-start.13 = (f32[1,128]{1,0:T(1,128)S(1)}, f32[1,128]{1,0:T(1,128)S(1)}, u32[]{:S(2)}, u32[]{:S(2)}) collective-permute-start(f32[1,128]{1,0:T(1,128)S(1)} %add_add_fusion), channel_id=1, source_target_pairs={{0,8},{8,0},{16,24},{24,16},{1,9},{9,1},{17,25},{25,17},{2,10},{10... | collective-permute-start | bytes 1544 | tf_op jit(solution)/shard_map/ppermute | solution.py:393
  40.5 3.5 %collective-permute-start.14 = (f32[1,128]{1,0:T(1,128)S(1)}, f32[1,128]{1,0:T(1,128)S(1)}, u32[]{:S(2)}, u32[]{:S(2)}) collective-permute-start(f32[1,128]{1,0:T(1,128)S(1)} %add.30), channel_id=1, source_target_pairs={{0,16},{8,24},{16,0},{24,8},{1,17},{9,25},{17,1},{25,9},{2,18},{10... | collective-permute-start | bytes 1544 | tf_op jit(solution)/shard_map/ppermute | solution.py:393
  44.1 1.3 %collective-permute-start.16 = (bf16[32,1280]{1,0:T(8,128)(2,1)S(1)}, bf16[32,1280]{1,0:T(8,128)(2,1)S(1)}, u32[]{:S(2)}, u32[]{:S(2)}) collective-permute-start(bf16[32,1280]{1,0:T(8,128)(2,1)S(1)} %slice.23), channel_id=1, source_target_pairs={{0,1},{1,0},{2,3},{3,2},{4,5},{5,4},{6,7},{7,6},{8,9},{9,8},{10,11... | collective-permute-start | bytes 245768 | tf_op jit(solution)/shard_map/ppermute | solution.py:393

commit v5 on v4

--- a/solution.py
+++ b/solution.py
@@ -15,6 +15,7 @@
 F32 = jnp.float32
 VMEM_BYTES = 40 * 1024 * 1024
 ALL_VMEM_BYTES = 62 * 1024 * 1024
+OWN_VMEM_BYTES = 40 * 1024 * 1024
 
 
 def call(kernel, out_shapes, inputs, scratch=(), far_in=0, far_out=0, copies=0, aliases=None, vmem=VMEM_BYTES, micros=1.0):
@@ -87,12 +88,11 @@
     return jnp.concatenate([row] * (width // row.shape[1]), axis=1)
 
 
-def merge_kernel(head_dim, bounds, key_ref, value_ref, cells_ref, gain_ref, *refs):
+def merge_kernel(head_dim, bounds, other, key_ref, value_ref, cells_ref, gain_ref, *refs):
     count = len(bounds)
-    own_refs, send_refs = refs[:count], refs[count : 2 * count]
-    key_buf, value_buf, cells_buf, gain_buf, copied = refs[2 * count :]
-    tok, lanes = key_buf.shape
-    half = lanes // CORES
+    out_refs = refs[:count]
+    key_buf, value_buf, cells_buf, gain_buf, copied = refs[count:]
+    tok, half = key_buf.shape
     cells = cells_ref.shape[1]
     side = core_side()
     small = [
@@ -102,34 +102,30 @@
     for move in small:
         move.start()
     spans = [
-        (other, chunk, start, stop, start + at, start + to)
-        for other in (1, 0)
+        (chunk, start, stop, start + at, start + to)
         for chunk, (start, stop) in enumerate(bounds)
         for at, to in pieces(stop - start)
     ]
     moves = []
-    for index, (other, _, _, _, at, to) in enumerate(spans):
+    for index, (_, _, _, at, to) in enumerate(spans):
         source = lanes_at((1 - side if other else side) * (half // TILE) + at // TILE, to - at)
-        here = slice(other * half + at, other * half + to)
+        here = slice(at, to)
         for which, (far, near) in enumerate(((key_ref, key_buf), (value_ref, value_buf))):
             move = pltpu.make_async_copy(
                 far.at[:, source], near.at[:, here], copied.at[2 + 2 * index + which]
             )
             move.start()
             moves.append(move)
-    for move in small:
+    for move in small + moves:
         move.wait()
     listed = lax.rem(cells_buf[...], tok)
     ids = lax.broadcasted_iota(jnp.int32, (tok, cells), 0)
     member = sum((listed[j : j + 1] == ids).astype(F32) for j in range(cells_ref.shape[0]))
     member = member.T.astype(BF16)
     twice = jnp.concatenate([member, member], axis=1)
-    for index, (other, chunk, start, stop, at, to) in enumerate(spans):
-        here = slice(other * half + at, other * half + to)
-        out_ref = (send_refs if other else own_refs)[chunk]
-        if index % (len(spans) // CORES) == 0:
-            for move in moves[2 * index : 2 * index + 2 * len(spans) // CORES]:
-                move.wait()
+    for chunk, start, stop, at, to in spans:
+        here = slice(at, to)
+        out_ref = out_refs[chunk]
         unit_vals, _ = unit_rows(key_buf[:, here].astype(F32), head_dim)
         keys = dot(twice, jnp.concatenate(halves(unit_vals), axis=0))
         keys *= gain_lanes(gain_buf, to - at) * 0.25
@@ -190,10 +186,10 @@
 
 
 def attend_kernel(head_dim, start, blocks, group, *refs):
-    query_ref, upstream_ref = refs[:2]
-    block_refs = refs[2 : 2 + blocks]
-    attended_ref, grad_ref, gain_out_ref = refs[2 + blocks : 5 + blocks]
-    part_refs = refs[5 + blocks :]
+    query_ref, upstream_ref, unit_ref, scale_ref, gain_ref = refs[:5]
+    block_refs = refs[5 : 5 + blocks]
+    own_ref, send_ref, gain_out_ref = refs[5 + blocks : 8 + blocks]
+    part_refs = refs[8 + blocks :]
     rows = query_ref.shape[0]
     block_rows, width = block_refs[0].shape
     width = width // 2
@@ -249,7 +245,8 @@
             held.append((keys, dot(upstream, spread(values), ((1,), (1,))), exp_parts))
         inverses = [1.0 / total for total in totals]
         attended = (weighted * by_lane(inverses)).astype(BF16)
-        attended_ref[:, lane] = attended
+        own_ref[:, lane] = attended[: rows // CORES]
+        send_ref[:, lane] = attended[rows // CORES :]
         products = upstream.astype(F32) * attended.astype(F32)
         inners = [
             jnp.sum(jnp.where(lane_head == h, products, 0.0), axis=1, keepdims=True) for h in heads
@@ -281,7 +278,15 @@
                 ref[:, lane] = grad_keys[here].astype(ref.dtype)
                 ref[:, value_lane] = grad_values[here].astype(ref.dtype)
         grad_queries *= scale
-        grad_ref[:, lane] = grad_queries
+        grads = norm_back(
+            grad_queries,
+            unit_ref[:, lanes_at(start // TILE + tile)],
+            scale_ref[:, lanes_at(start // TILE + tile)],
+            gain_lanes(gain_ref, TILE),
+            head_dim,
+        ).astype(BF16)
+        own_ref[:, value_lane] = grads[: rows // CORES]
+        send_ref[:, value_lane] = grads[rows // CORES :]
         query_sum += jnp.sum(grad_queries * queries.astype(F32), axis=0, keepdims=True)
         return query_sum, key_sum
 
@@ -303,38 +308,24 @@
     gain_out_ref[...] = jnp.concatenate([per_channel(row) for row in sums], axis=1)
 
 
-def query_back_kernel(head_dim, bounds, unit_ref, scale_ref, gain_ref, *refs):
+def place_kernel(bounds, *refs):
     count = len(bounds)
-    attended_refs, grad_refs = refs[:count], refs[count : 2 * count]
-    attended_out, grad_out, send_ref, attended_buf, grad_buf, copied = refs[2 * count :]
-    tok, half = attended_buf.shape
-    for (start, stop), attended_ref, grad_ref in zip(bounds, attended_refs, grad_refs):
-        attended_buf[:, start:stop] = attended_ref[:tok]
-        send_ref[:, start:stop] = attended_ref[tok:]
-        for at, to in pieces(stop - start):
-            lane = slice(start + at, start + to)
-            grads = norm_back(
-                grad_ref[:, at:to],
-                unit_ref[:, lane],
-                scale_ref[:, lane],
-                gain_lanes(gain_ref, to - at),
-                head_dim,
-            ).astype(BF16)
-            grad_buf[:, lane] = grads[:tok]
-            send_ref[:, half + start + at : half + start + to] = grads[tok:]
-    place = lanes_at(core_side() * (half // TILE), half)
-    moves = [
-        pltpu.make_async_copy(attended_buf, attended_out.at[:, place], copied.at[0]),
-        pltpu.make_async_copy(grad_buf, grad_out.at[:, place], copied.at[1]),
-    ]
-    for move in moves:
-        move.start()
+    own_refs, outs, copied = refs[:count], refs[count : count + 2], refs[count + 2]
+    half = bounds[-1][1]
+    moves = []
+    for (start, stop), own_ref in zip(bounds, own_refs):
+        width = stop - start
+        place = lanes_at(core_side() * (half // TILE) + start // TILE, width)
+        for index, out in enumerate(outs):
+            source = own_ref.at[:, index * width : (index + 1) * width]
+            moves.append(pltpu.make_async_copy(source, out.at[:, place], copied.at[len(moves)]))
+            moves[-1].start()
     for move in moves:
         move.wait()
 
 
 def key_back_kernel(head_dim, bounds, own_terms, other_terms, *refs):
-    query_refs, refs = refs[2:3], refs[3:]
+    query_refs, refs = refs[2 : 2 + len(bounds)], refs[2 + len(bounds) :]
     unit_ref, scale_ref, table_ref, gain_ref = refs[:4]
     refs = refs[4:]
     sources = []
@@ -359,14 +350,17 @@
     ]
     moves = []
 
-    def send(buf, out, other):
-        place = lanes_at((1 - side if other else side) * (half // TILE), half)
+    def send(buf, out, other, start=0, width=half):
+        first = (1 - side if other else side) * (half // TILE)
+        place = lanes_at(first + start // TILE, width)
         move = pltpu.make_async_copy(buf, out.at[:, place], copied.at[len(moves)])
         move.start()
         moves.append(move)
 
-    for index, out in enumerate(query_outs):
-        send(query_refs[0].at[:, index * half : (index + 1) * half], out, 1)
+    for (start, stop), ref in zip(bounds, query_refs):
+        width = stop - start
+        for index, out in enumerate(query_outs):
+            send(ref.at[:, index * width : (index + 1) * width], out, 1, start, width)
     for other, chunk, start, stop, at, to in spans:
         grad_value_buf[other, :, at:to] = spread(
             chunk, other, stop - 2 * start + at, stop - 2 * start + to
@@ -438,7 +432,7 @@
                 self.gains = sum(arrived, self.gains)
 
 
-OPT = dict(tc=1, split=0, steps="cD|yx|", near=1, hb=0, sb=2, k4=4, kc=0.1, pc=1.0)
+OPT = dict(tl=2, km=2.0, tp=0, tc=1, split=0, steps="cD|yx|", near=1, hb=0, sb=2, pc=0.1)
 
 
 def chunk_bounds(half):
@@ -457,17 +451,22 @@
     widths = [stop - start for start, stop in bounds]
     query_row, key_row = query_gain[None], key_gain[None]
 
-    merged = call(
-        functools.partial(merge_kernel, head_dim, bounds),
-        [((cells, 2 * width), BF16) for width in widths] * 2,
-        [key_rows, value_rows, merge_cells[0].T, key_row],
-        scratch=[((tok, lanes), BF16)] * 2
-        + [(merge_cells.shape[:0:-1], jnp.int32), ((1, head_dim), F32)],
-        far_in=4,
-        copies=2 + 4 * sum(len(pieces(width)) for width in widths),
-        vmem=ALL_VMEM_BYTES,
-    )
-    crossed = [exchange(sent, "seq", 1) for sent in merged[len(bounds) :]]
+    def merged_half(other):
+        return call(
+            functools.partial(merge_kernel, head_dim, bounds, other),
+            [((cells, 2 * width), BF16) for width in widths],
+            [key_rows, value_rows, merge_cells[0].T, key_row],
+            scratch=[((tok, half), BF16)] * 2
+            + [(merge_cells.shape[:0:-1], jnp.int32), ((1, head_dim), F32)],
+            far_in=4,
+            copies=2 + 2 * sum(len(pieces(width)) for width in widths),
+            vmem=ALL_VMEM_BYTES if other else OWN_VMEM_BYTES,
+            micros=0.5,
+        )
+
+    sent_half = merged_half(True)
+    merged = merged_half(False)
+    crossed = [exchange(sent, "seq", 1) for sent in sent_half]
     crossed, late_queries, late_upstream, late_keys = lax.optimization_barrier(
         (crossed, queries, upstream, key_rows)
     )
@@ -496,41 +495,28 @@
         call(
             functools.partial(attend_kernel, head_dim, start, chips, group),
             [
-                ((CORES * tok, width), BF16),
-                ((CORES * tok, width), F32),
+                ((tok, 2 * width), BF16),
+                ((tok, 2 * width), BF16),
                 ((1, 2 * head_dim), F32),
                 ((CORES * cells, 2 * width), F32),
             ]
             + [((CORES * cells, 2 * width), BF16)] * (chips - 1),
-            [normed, both_upstream] + blocks,
+            [normed, both_upstream, query_unit, query_scale, query_row] + blocks,
             micros=3.5 * width / half,
         )
         for (start, stop), width, blocks in zip(bounds, widths, gathered)
     ]
-    attended = [result[0] for result in results]
-    grads = [result[1] for result in results]
     rest = Rest(sum(result[2] for result in results), chips)
 
     first_steps, next_steps, last_steps = OPT["steps"].split("|")
-
-    def query_back():
-        return call(
-            functools.partial(query_back_kernel, head_dim, bounds),
-            [((tok, lanes), BF16)] * 3,
-            [query_unit, query_scale, query_row] + attended + grads,
-            scratch=[((tok, half), BF16)] * 2,
-            far_out=2,
-            copies=2,
-            micros=OPT["kc"],
-        )
 
     parts = [result[3:] for result in results]
     far = [chip_reduce(part[: chips // 2 - 1 : -1]) if chips > 1 else [] for part in parts]
-    rest.advance(first_steps)
-    if OPT["k4"] == 1:
-        attended_half, grad_half, sent_part = query_back()
-        if OPT["k4"] == 1:
-            far, sent_part = lax.optimization_barrier((far, sent_part))
+    rest.advance(first_steps[:1])
+    near_parts = [part[: max(chips // 2, 1)] for part in parts]
+    if OPT["tp"]:
+        _, near_parts = lax.optimization_barrier((rest.gains, near_parts))
+    rest.advance(first_steps[1:])
     if OPT["hb"]:
         far, rest.gains = lax.optimization_barrier((far, rest.gains))
     mirror = CORES * (chips - 1)
@@ -547,33 +533,36 @@
         across = [[] for _ in bounds]
     if chips == 1:
         straight = across = [[] for _ in bounds]
-    near = [chip_reduce(part[: max(chips // 2, 1)]) for part in parts]
+    near = [chip_reduce(part) for part in near_parts]
     if OPT["tc"]:
         near_crossed = [exchange(added([t[cells:] for t in terms]), "seq", 1) for terms in near]
     if OPT["split"]:
         crossed = [exchange(added([term[cells:] for term in terms]), "seq", 1) for terms in near]
     else:
         crossed = None
-    if OPT["k4"] == 4:
-        _, query_unit = lax.optimization_barrier((near, query_unit))
-    if OPT["k4"] == 5:
-        _, query_unit = lax.optimization_barrier((sums, query_unit))
-    if OPT["k4"] in (0, 2, 4, 5):
-        attended_half, grad_half, sent_part = query_back()
     if OPT["near"] == 1:
         rest.advance(next_steps[:1])
         near, rest.gains = lax.optimization_barrier((near, rest.gains))
-        if OPT["k4"] == 3:
-            query_unit, rest.gains = lax.optimization_barrier((query_unit, rest.gains))
-            attended_half, grad_half, sent_part = query_back()
         rest.advance(next_steps[1:])
     elif OPT["near"] == 2:
         near, rest.gains = lax.optimization_barrier((near, rest.gains))
         rest.advance(next_steps)
     else:
         rest.advance(next_steps)
-    arrived_part = exchange(sent_part, "seq", 1)
-    if OPT["tc"]:
+    arrived_part = [exchange(result[1], "seq", 1) for result in results]
+    attended_half, grad_half = call(
+        functools.partial(place_kernel, bounds),
+        [((tok, lanes), BF16)] * 2,
+        [result[0] for result in results],
+        far_out=2,
+        copies=2 * len(bounds),
+        micros=OPT["pc"],
+    )
+    if OPT["tl"] == 1:
+        straight, rest.gains = lax.optimization_barrier((straight, rest.gains))
+    elif OPT["tl"] == 2:
+        pass
+    elif OPT["tc"]:
         straight, near_crossed, rest.gains, arrived_part = lax.optimization_barrier(
             (straight, near_crossed, rest.gains, arrived_part)
         )
@@ -587,6 +576,8 @@
         across = [[exchange(term[cells:], "seq", 1) for term in terms] for terms in straight]
     elif not OPT["split"]:
         crossed = [exchange(added([t[cells:] for t in terms]), "seq", 1) for terms in own_terms]
+    if OPT["tl"] == 2:
+        across, rest.gains = lax.optimization_barrier((across, rest.gains))
     rest.advance(last_steps)
     gain_total = rest.gains[0]
 
@@ -596,13 +587,16 @@
     grad_key, grad_value, attended_all, grad_query = call(
         functools.partial(key_back_kernel, head_dim, bounds, len(own_terms[0]), 1 + len(across[0])),
         [((tok, lanes), BF16)] * 4,
-        [attended_half, grad_half, arrived_part, key_unit, key_scale, table, gain_row] + sources,
+        [attended_half, grad_half]
+        + arrived_part
+        + [key_unit, key_scale, table, gain_row]
+        + sources,
         scratch=[((CORES, tok, half), BF16)] * 2,
         far_in=2,
         far_out=4,
-        copies=2 * CORES + 2,
+        copies=2 * CORES + 2 * len(bounds),
         aliases={0: 2, 1: 3},
-        micros=2.0,
+        micros=OPT["km"],
     )
     return (
         attended_all[None],

time: 47 us -> 45.2 us (0.962)
  local copies, waits for them, and re-layouts: 0.94 us -> 0.05 us
  waiting for transfers between devices: 13.7 us -> 13.2 us
    unnamed x13 -> x16, local copies, waits for them, and re-layouts: 0.92 us -> 0.04 us
    ppermute x17, waiting for transfers between devices: 13.7 us -> 13.2 us  [exchange(): lax.ppermute(array, axis, [(i, i ^ apart) for i in range(lax.axis_size(ax...]
    pallas_call x7 -> x8, Pallas kernels: 9.43 us -> 9.19 us  [call(): pl.pallas_call(kernel, out_shape=[jax.ShapeDtypeStruct(shape, kind) for s...]
  transfers between devices with their start and end apart: 17 -> 17, of which waited for: 8 -> 6; matrix products, arithmetic and copies ran while one was open for 3% -> 2% of each run, Pallas kernels for 5% -> 5%
where the time goes in v5:
time: 45.2 us; the launch traced here: 45.1 us
  starting transfers between devices  21.2 us (47%)
  waiting for transfers between devices  13.2 us (29%)
  Pallas kernels  9.19 us (20%)
  between operations  0.8 us (2%)
  other arithmetic  0.67 us (1%)
    ppermute x17, starting transfers between devices, exchange(): lax.ppermute(array, axis, [(i, i ^ apart) for i in range(lax.axis_size(ax...  21.2 us
    ppermute x17, waiting for transfers between devices, exchange(): lax.ppermute(array, axis, [(i, i ^ apart) for i in range(lax.axis_size(ax...  13.2 us
    pallas_call x8, Pallas kernels, call(): pl.pallas_call(kernel, out_shape=[jax.ShapeDtypeStruct(shape, kind) for s...  9.19 us
  transfers between devices with their start and end apart: 17, of which 6 were waited for; matrix products, arithmetic and copies ran while one was open for 2% of the time, Pallas kernels for 5%

profile of v5, /device:TPU:0, one launch (start us, length us, event | category | flops | bytes accessed | tf_op | source)
XLA Modules:
  0.0 45.1 jit_solution(7030172387283698586)
XLA Ops:
  0.6 0.0 copy-start.1
  0.6 0.0 copy-start.2
  0.7 0.0 copy-start.5
  0.7 0.0 copy-start.6
  0.7 2.2 %shard_map.127 = bf16[32,1280]{1,0:T(8,128)(2,1)} custom-call(bf16[128,1280]{1,0:T(8,128)(2,1)} %bitcast.28, bf16[128,1280]{1,0:T(8,128)(2,1)} %bitcast.22, s32[4,32]{1,0:T(4,128)} %bitcast.31, f32[1,64]{1,0:T(1,128)} %bitcast.19), custom_call_target="tpu_custom_call" | custom-call | flops 500000000 | bytes 1000000 | tf_op jit(solution)/shard_map/pallas_call | solution.py:26
  2.8 0.0 copy-start.3
  2.9 0.0 copy-start.4
  2.9 0.5 %collective-permute-start = (bf16[32,1280]{1,0:T(8,128)(2,1)}, bf16[32,1280]{1,0:T(8,128)(2,1)S(1)}, u32[]{:S(2)}, u32[]{:S(2)}) collective-permute-start(bf16[32,1280]{1,0:T(8,128)(2,1)} %shard_map.127), channel_id=1, source_target_pairs={{0,1},{1,0},{2,3},{3,2},{4,5},{5,4},{6,7},{7,6},{8,9},{9,8},{10,11... | collective-permute-start | bytes 245768 | tf_op jit(solution)/shard_map/ppermute | solution.py:387
  3.4 0.0 copy-done.1
  3.4 0.0 copy-done.2
  3.4 0.0 copy-done.5
  3.4 0.0 copy-done.6
  3.4 0.6 %shard_map.130 = bf16[32,1280]{1,0:T(8,128)(2,1)S(1)} custom-call(bf16[128,1280]{1,0:T(8,128)(2,1)S(1)} %bitcast.29, bf16[128,1280]{1,0:T(8,128)(2,1)S(1)} %bitcast.23, s32[4,32]{1,0:T(4,128)S(1)} %bitcast.32, f32[1,64]{1,0:T(1,128)S(1)} %bitcast.20), custom_call_target="tpu_custom_call" | custom-call | flops 500000000 | bytes 1000000 | tf_op jit(solution)/shard_map/pallas_call | solution.py:26
  4.0 0.5 %collective-permute-done = bf16[32,1280]{1,0:T(8,128)(2,1)S(1)} collective-permute-done((bf16[32,1280]{1,0:T(8,128)(2,1)}, bf16[32,1280]{1,0:T(8,128)(2,1)S(1)}, u32[]{:S(2)}, u32[]{:S(2)}) %collective-permute-start) | collective-permute-done | bytes 81952 | tf_op jit(solution)/shard_map/ppermute | solution.py:387
  4.5 0.0 copy-done.3
  4.5 0.0 copy-done.4
  4.5 0.1 shard_map.128
  4.6 0.4 collective-permute-start.1
  5.0 0.0 copy-start
  5.0 4.8 %collective-permute-start.3 = (bf16[64,1280]{1,0:T(8,128)(2,1)S(1)}, bf16[64,1280]{1,0:T(8,128)(2,1)S(1)}, u32[]{:S(2)}, u32[]{:S(2)}) collective-permute-start(bf16[64,1280]{1,0:T(8,128)(2,1)S(1)} %pad_maximum_fusion.refs_5_), channel_id=1, source_target_pairs={{0,6},{1,7},{2,4},{3,5},{4,2},{5,3},{6,0},{7,1},{8,14},{9,15},{10,... | collective-permute-start | bytes 491528 | tf_op jit(solution)/shard_map/ppermute | solution.py:387
  9.8 0.0 collective-permute-start.2
  9.9 5.1 %collective-permute-done.3.refs_8_ = bf16[64,1280]{1,0:T(8,128)(2,1)S(1)} collective-permute-done((bf16[64,1280]{1,0:T(8,128)(2,1)S(1)}, bf16[64,1280]{1,0:T(8,128)(2,1)S(1)}, u32[]{:S(2)}, u32[]{:S(2)}) %collective-permute-start.3) | collective-permute-done | bytes 163872 | tf_op jit(solution)/shard_map/ppermute | solution.py:387
  14.9 2.8 %collective-permute-start.4 = (bf16[64,1280]{1,0:T(8,128)(2,1)S(1)}, bf16[64,1280]{1,0:T(8,128)(2,1)S(1)}, u32[]{:S(2)}, u32[]{:S(2)}) collective-permute-start(bf16[64,1280]{1,0:T(8,128)(2,1)S(1)} %collective-permute-done.3.refs_8_), channel_id=1, source_target_pairs={{0,2},{1,3},{2,0},{3,1},{4,6},{5,7},{6,4},{7,5},{8,10},{9,11},{10,... | collective-permute-start | bytes 491528 | tf_op jit(solution)/shard_map/ppermute | solution.py:387
  17.8 0.0 collective-permute-done.1.arrived_ref
  17.8 0.0 copy-done
  17.8 0.5 %shard_map.129 = (f32[256,640]{1,0:T(8,128)S(1)}, f32[256,640]{1,0:T(8,128)S(1)}, bf16[256,640]{1,0:T(8,128)(2,1)S(1)}, bf16[256,640]{1,0:T(8,128)(2,1)S(1)}) custom-call(bf16[128,1280]{1,0:T(8,128)(2,1)S(1)} %bitcast.25, bf16[128,1280]{1,0:T(8,128)(2,1)S(1)} %bitcast.27, bf16[128,1280]{1,0:T(8,128)(2,1)S(1)} %collective-permute-done.1.arrived_ref, ...), custom_call_target="tpu_custom_call" | custom-call | flops 1000000000 | bytes 2000000 | tf_op jit(solution)/shard_map/pallas_call | solution.py:26
  18.3 0.0 collective-permute-done.2.refs_6_
  18.3 3.4 %collective-permute-done.4.refs_7_ = bf16[64,1280]{1,0:T(8,128)(2,1)S(1)} collective-permute-done((bf16[64,1280]{1,0:T(8,128)(2,1)S(1)}, bf16[64,1280]{1,0:T(8,128)(2,1)S(1)}, u32[]{:S(2)}, u32[]{:S(2)}) %collective-permute-start.4) | collective-permute-done | bytes 163872 | tf_op jit(solution)/shard_map/ppermute | solution.py:387
  21.7 3.1 %shard_map.131 = (bf16[128,1280]{1,0:T(8,128)(2,1)S(1)}, bf16[128,1280]{1,0:T(8,128)(2,1)S(1)}, f32[1,128]{1,0:T(1,128)S(1)}, f32[64,1280]{1,0:T(8,128)S(1)}, bf...) custom-call(bf16[256,640]{1,0:T(8,128)(2,1)S(1)} %get-tuple-element.39.refs_0_, ...), custom_call_target="tpu_custom_call" | custom-call | flops 3500000000 | bytes 7000000 | tf_op jit(solution)/shard_map/pallas_call | solution.py:26
  24.8 0.0 copy-start.7
  24.8 1.8 %collective-permute-start.7 = (bf16[64,1280]{1,0:T(8,128)(2,1)S(1)}, bf16[64,1280]{1,0:T(8,128)(2,1)S(1)}, u32[]{:S(2)}, u32[]{:S(2)}) collective-permute-start(bf16[64,1280]{1,0:T(8,128)(2,1)S(1)} %get-tuple-element.56), channel_id=1, source_target_pairs={{0,2},{1,3},{2,0},{3,1},{4,6},{5,7},{6,4},{7,5},{8,10},{9,11},{10,... | collective-permute-start | bytes 491528 | tf_op jit(solution)/shard_map/ppermute | solution.py:387
  26.6 0.0 collective-permute-start.8
  26.6 0.0 copy-done.7
  26.6 0.6 %shard_map.133 = (f32[128,1280]{1,0:T(8,128)S(1)}, f32[128,1280]{1,0:T(8,128)S(1)}, bf16[128,64]{1,0:T(8,128)(2,1)S(1)}, f32[1,256]{1,0:T(1,128)S(1)}) custom-call(bf16[128,1280]{1,0:T(8,128)(2,1)S(1)} %bitcast.30, s32[1,128]{1,0:T(1,128)S(1)} %copy-done.7, f32[1,64]{1,0:T(1,128)S(1)} %bitcast.21), custom_call_target="tpu_custom_call" | custom-call | flops 1000000000 | bytes 2000000 | tf_op jit(solution)/shard_map/pallas_call | solution.py:26
  27.2 0.6 %collective-permute-start.6 = (bf16[64,1280]{1,0:T(8,128)(2,1)S(1)}, bf16[64,1280]{1,0:T(8,128)(2,1)S(1)}, u32[]{:S(2)}, u32[]{:S(2)}) collective-permute-start(bf16[64,1280]{1,0:T(8,128)(2,1)S(1)} %get-tuple-element.54), channel_id=1, source_target_pairs={{0,2},{1,3},{2,0},{3,1},{4,6},{5,7},{6,4},{7,5},{8,10},{9,11},{10,... | collective-permute-start | bytes 491528 | tf_op jit(solution)/shard_map/ppermute | solution.py:387
  27.9 0.0 collective-permute-done.8
  27.9 2.5 %collective-permute-start.10 = (f32[1,128]{1,0:T(1,128)S(1)}, f32[1,128]{1,0:T(1,128)S(1)}, u32[]{:S(2)}, u32[]{:S(2)}) collective-permute-start(f32[1,128]{1,0:T(1,128)S(1)} %add.25), channel_id=1, source_target_pairs={{0,4},{1,5},{2,6},{3,7},{4,0},{5,1},{6,2},{7,3},{8,12},{9,13},{10,... | collective-permute-start | bytes 1544 | tf_op jit(solution)/shard_map/ppermute | solution.py:387
  30.4 1.3 %collective-permute-start.11 = (f32[1,128]{1,0:T(1,128)S(1)}, f32[1,128]{1,0:T(1,128)S(1)}, u32[]{:S(2)}, u32[]{:S(2)}) collective-permute-start(f32[1,128]{1,0:T(1,128)S(1)} %add.25), channel_id=1, source_target_pairs={{0,6},{1,7},{2,4},{3,5},{4,2},{5,3},{6,0},{7,1},{8,14},{9,15},{10,... | collective-permute-start | bytes 1544 | tf_op jit(solution)/shard_map/ppermute | solution.py:387
  31.7 0.0 collective-permute-start.9
  31.7 0.0 collective-permute-done.7
  31.8 2.5 %collective-permute-start.13 = (bf16[64,1280]{1,0:T(8,128)(2,1)S(1)}, bf16[64,1280]{1,0:T(8,128)(2,1)S(1)}, u32[]{:S(2)}, u32[]{:S(2)}) collective-permute-start(bf16[64,1280]{1,0:T(8,128)(2,1)S(1)} %add_convert_fusion), channel_id=1, source_target_pairs={{0,6},{1,7},{2,4},{3,5},{4,2},{5,3},{6,0},{7,1},{8,14},{9,15},{10,... | collective-permute-start | bytes 491528 | tf_op jit(solution)/shard_map/ppermute | solution.py:387
  34.3 0.0 collective-permute-done.10
  34.3 1.6 %collective-permute-done.11 = f32[1,128]{1,0:T(1,128)S(1)} collective-permute-done((f32[1,128]{1,0:T(1,128)S(1)}, f32[1,128]{1,0:T(1,128)S(1)}, u32[]{:S(2)}, u32[]{:S(2)}) %collective-permute-start.11) | collective-permute-done | bytes 544 | tf_op jit(solution)/shard_map/ppermute | solution.py:387
  35.9 0.0 collective-permute-done.9
  35.9 1.6 %collective-permute-start.12 = (f32[1,128]{1,0:T(1,128)S(1)}, f32[1,128]{1,0:T(1,128)S(1)}, u32[]{:S(2)}, u32[]{:S(2)}) collective-permute-start(f32[1,128]{1,0:T(1,128)S(1)} %add_add_fusion), channel_id=1, source_target_pairs={{0,8},{8,0},{16,24},{24,16},{1,9},{9,1},{17,25},{25,17},{2,10},{10... | collective-permute-start | bytes 1544 | tf_op jit(solution)/shard_map/ppermute | solution.py:387
  37.5 0.7 %shard_map.132 = (bf16[128,1280]{1,0:T(8,128)(2,1)}, bf16[128,1280]{1,0:T(8,128)(2,1)}) custom-call(bf16[128,1280]{1,0:T(8,128)(2,1)S(1)} %get-tuple-element.44.refs_0_), custom_call_target="tpu_custom_call" | custom-call | flops 100000000 | bytes 200000 | tf_op jit(solution)/shard_map/pallas_call | solution.py:26
  38.2 0.1 collective-permute-start.5
  38.3 1.2 %collective-permute-done.12 = f32[1,128]{1,0:T(1,128)S(1)} collective-permute-done((f32[1,128]{1,0:T(1,128)S(1)}, f32[1,128]{1,0:T(1,128)S(1)}, u32[]{:S(2)}, u32[]{:S(2)}) %collective-permute-start.12) | collective-permute-done | bytes 544 | tf_op jit(solution)/shard_map/ppermute | solution.py:387
  39.5 0.0 collective-permute-done.6.refs_8_
  39.5 1.5 %collective-permute-start.16 = (f32[1,128]{1,0:T(1,128)S(1)}, f32[1,128]{1,0:T(1,128)S(1)}, u32[]{:S(2)}, u32[]{:S(2)}) collective-permute-start(f32[1,128]{1,0:T(1,128)S(1)} %add.29), channel_id=1, source_target_pairs={{0,16},{8,24},{16,0},{24,8},{1,17},{9,25},{17,1},{25,9},{2,18},{10... | collective-permute-start | bytes 1544 | tf_op jit(solution)/shard_map/ppermute | solution.py:387
  41.0 0.0 collective-permute-done.13.refs_9_
  41.0 0.1 collective-permute-start.15
  41.2 0.6 %collective-permute-start.14 = (f32[32,1280]{1,0:T(8,128)S(1)}, f32[32,1280]{1,0:T(8,128)S(1)}, u32[]{:S(2)}, u32[]{:S(2)}) collective-permute-start(f32[32,1280]{1,0:T(8,128)S(1)} %convert_add_fusion), channel_id=1, source_target_pairs={{0,1},{1,0},{2,3},{3,2},{4,5},{5,4},{6,7},{7,6},{8,9},{9,8},{10,11... | collective-permute-start | bytes 491528 | tf_op jit(solution)/shard_map/ppermute | solution.py:387
  41.7 1.3 %collective-permute-done.16 = f32[1,128]{1,0:T(1,128)S(1)} collective-permute-done((f32[1,128]{1,0:T(1,128)S(1)}, f32[1,128]{1,0:T(1,128)S(1)}, u32[]{:S(2)}, u32[]{:S(2)}) %collective-permute-start.16) | collective-permute-done | bytes 544 | tf_op jit(solution)/shard_map/ppermute | solution.py:387
  43.1 0.0 collective-permute-done.15.refs_11_
  43.1 0.6 %bitcast_divide_fusion = (f32[64]{0:T(128)}, f32[64]{0:T(128)}) fusion(f32[64]{0:T(128)S(1)} %copy-done.1, f32[1,128]{1,0:T(1,128)S(1)} %add.31, f32[64]{0:T(128)S(1)} %copy-done), kind=kLoop, calls=%fused_computation.3 | loop fusion | flops 128 | bytes 1536 | tf_op jit(solution)/shard_map/div | solution.py:607
  43.6 0.0 collective-permute-done.14.refs_10_
  43.7 0.0 collective-permute-done.5.refs_2_
  43.7 1.4 %shard_map.134 = (bf16[128,1280]{1,0:T(8,128)(2,1)}, bf16[128,1280]{1,0:T(8,128)(2,1)}, bf16[128,1280]{1,0:T(8,128)(2,1)}, bf16[128,1280]{1,0:T(8,128)(2,1)}) custom-call(bf16[128,1280]{1,0:T(8,128)(2,1)} %get-tuple-element.45.refs_0_, bf16[128,1280]{1,0:T(8,128)(2,1)} %get-tuple-element.46.refs_1_, ...), custom_call_target="tpu_custom_call", output_to_operand_aliasing={{2}: (0, {}), {3}: (1, {})} | custom-call | flops 2000000000 | bytes 4000000 | tf_op jit(solution)/shard_map/pallas_call | solution.py:26
  (8 shorter events, 0.1 us)
Async XLA Ops:
  0.6 2.8 %copy-start.1 = (f32[64]{0:T(128)S(1)}, f32[64]{0:T(128)}, u32[]{:S(2)}) copy-start(f32[64]{0:T(128)} %param.15) | copy-start | bytes 772
  0.6 2.7 %copy-start.2 = (bf16[1,128,1280]{2,1,0:T(8,128)(2,1)S(1)}, bf16[1,128,1280]{2,1,0:T(8,128)(2,1)}, u32[]{:S(2)}) copy-start(bf16[1,128,1280]{2,1,0:T(8,128)(2,1)} %param.10) | copy-start | bytes 983044
  0.7 2.7 %copy-start.5 = (bf16[1,128,1280]{2,1,0:T(8,128)(2,1)S(1)}, bf16[1,128,1280]{2,1,0:T(8,128)(2,1)}, u32[]{:S(2)}) copy-start(bf16[1,128,1280]{2,1,0:T(8,128)(2,1)} %param.9) | copy-start | bytes 983044
  0.7 2.7 %copy-start.6 = (s32[1,32,4]{1,2,0:T(4,128)S(1)}, s32[1,32,4]{1,2,0:T(4,128)}, u32[]{:S(2)}) copy-start(s32[1,32,4]{1,2,0:T(4,128)} %param.11) | copy-start | bytes 1540
  2.8 1.7 %copy-start.3 = (bf16[1,128,1280]{2,1,0:T(8,128)(2,1)S(1)}, bf16[1,128,1280]{2,1,0:T(8,128)(2,1)}, u32[]{:S(2)}) copy-start(bf16[1,128,1280]{2,1,0:T(8,128)(2,1)} %param.8) | copy-start | bytes 983044
  2.9 1.7 %copy-start.4 = (bf16[1,128,1280]{2,1,0:T(8,128)(2,1)S(1)}, bf16[1,128,1280]{2,1,0:T(8,128)(2,1)}, u32[]{:S(2)}) copy-start(bf16[1,128,1280]{2,1,0:T(8,128)(2,1)} %param.13) | copy-start | bytes 983044
  2.9 1.7 %collective-permute-start = (bf16[32,1280]{1,0:T(8,128)(2,1)}, bf16[32,1280]{1,0:T(8,128)(2,1)S(1)}, u32[]{:S(2)}, u32[]{:S(2)}) collective-permute-start(bf16[32,1280]{1,0:T(8,128)(2,1)} %shard_map.127), channel_id=1, source_target_pairs={{0,1},{1,0},{2,3},{3,2},{4,5},{5,4},{6,7},{7,6},{8,9},{9,8},{10,11... | collective-permute-start | bytes 245768 | tf_op jit(solution)/shard_map/ppermute | solution.py:387
  4.6 13.2 %collective-permute-start.1 = (bf16[128,1280]{1,0:T(8,128)(2,1)S(1)}, bf16[128,1280]{1,0:T(8,128)(2,1)S(1)}, u32[]{:S(2)}, u32[]{:S(2)}) collective-permute-start(bf16[128,1280]{1,0:T(8,128)(2,1)S(1)} %shard_map.128), channel_id=1, source_target_pairs={{0,1},{1,0},{2,3},{3,2},{4,5},{5,4},{6,7},{7,6},{8,9},{9,8},{10,11... | collective-permute-start | bytes 983048 | tf_op jit(solution)/shard_map/ppermute | solution.py:387
  5.0 12.8 %copy-start = (f32[64]{0:T(128)S(1)}, f32[64]{0:T(128)}, u32[]{:S(2)}) copy-start(f32[64]{0:T(128)} %param.14) | copy-start | bytes 772
  5.0 9.9 %collective-permute-start.3 = (bf16[64,1280]{1,0:T(8,128)(2,1)S(1)}, bf16[64,1280]{1,0:T(8,128)(2,1)S(1)}, u32[]{:S(2)}, u32[]{:S(2)}) collective-permute-start(bf16[64,1280]{1,0:T(8,128)(2,1)S(1)} %pad_maximum_fusion.refs_5_), channel_id=1, source_target_pairs={{0,6},{1,7},{2,4},{3,5},{4,2},{5,3},{6,0},{7,1},{8,14},{9,15},{10,... | collective-permute-start | bytes 491528 | tf_op jit(solution)/shard_map/ppermute | solution.py:387
  9.8 8.5 %collective-permute-start.2 = (bf16[64,1280]{1,0:T(8,128)(2,1)S(1)}, bf16[64,1280]{1,0:T(8,128)(2,1)S(1)}, u32[]{:S(2)}, u32[]{:S(2)}) collective-permute-start(bf16[64,1280]{1,0:T(8,128)(2,1)S(1)} %pad_maximum_fusion.refs_5_), channel_id=1, source_target_pairs={{0,2},{1,3},{2,0},{3,1},{4,6},{5,7},{6,4},{7,5},{8,10},{9,11},{10,... | collective-permute-start | bytes 491528 | tf_op jit(solution)/shard_map/ppermute | solution.py:387
  14.9 6.8 %collective-permute-start.4 = (bf16[64,1280]{1,0:T(8,128)(2,1)S(1)}, bf16[64,1280]{1,0:T(8,128)(2,1)S(1)}, u32[]{:S(2)}, u32[]{:S(2)}) collective-permute-start(bf16[64,1280]{1,0:T(8,128)(2,1)S(1)} %collective-permute-done.3.refs_8_), channel_id=1, source_target_pairs={{0,2},{1,3},{2,0},{3,1},{4,6},{5,7},{6,4},{7,5},{8,10},{9,11},{10,... | collective-permute-start | bytes 491528 | tf_op jit(solution)/shard_map/ppermute | solution.py:387
  24.8 1.8 %copy-start.7 = (s32[1,128]{1,0:T(1,128)S(1)}, s32[1,128]{1,0:T(1,128)}, u32[]{:S(2)}) copy-start(s32[1,128]{1,0:T(1,128)} %unmerge_ref.1) | copy-start | bytes 1540
  24.8 6.9 %collective-permute-start.7 = (bf16[64,1280]{1,0:T(8,128)(2,1)S(1)}, bf16[64,1280]{1,0:T(8,128)(2,1)S(1)}, u32[]{:S(2)}, u32[]{:S(2)}) collective-permute-start(bf16[64,1280]{1,0:T(8,128)(2,1)S(1)} %get-tuple-element.56), channel_id=1, source_target_pairs={{0,2},{1,3},{2,0},{3,1},{4,6},{5,7},{6,4},{7,5},{8,10},{9,11},{10,... | collective-permute-start | bytes 491528 | tf_op jit(solution)/shard_map/ppermute | solution.py:387
  26.6 1.3 %collective-permute-start.8 = (f32[1,128]{1,0:T(1,128)S(1)}, f32[1,128]{1,0:T(1,128)S(1)}, u32[]{:S(2)}, u32[]{:S(2)}) collective-permute-start(f32[1,128]{1,0:T(1,128)S(1)} %get-tuple-element.57), channel_id=1, source_target_pairs={{0,1},{1,0},{2,3},{3,2},{4,5},{5,4},{6,7},{7,6},{8,9},{9,8},{10,11... | collective-permute-start | bytes 1544 | tf_op jit(solution)/shard_map/ppermute | solution.py:387
  27.2 12.3 %collective-permute-start.6 = (bf16[64,1280]{1,0:T(8,128)(2,1)S(1)}, bf16[64,1280]{1,0:T(8,128)(2,1)S(1)}, u32[]{:S(2)}, u32[]{:S(2)}) collective-permute-start(bf16[64,1280]{1,0:T(8,128)(2,1)S(1)} %get-tuple-element.54), channel_id=1, source_target_pairs={{0,2},{1,3},{2,0},{3,1},{4,6},{5,7},{6,4},{7,5},{8,10},{9,11},{10,... | collective-permute-start | bytes 491528 | tf_op jit(solution)/shard_map/ppermute | solution.py:387
  27.9 6.4 %collective-permute-start.10 = (f32[1,128]{1,0:T(1,128)S(1)}, f32[1,128]{1,0:T(1,128)S(1)}, u32[]{:S(2)}, u32[]{:S(2)}) collective-permute-start(f32[1,128]{1,0:T(1,128)S(1)} %add.25), channel_id=1, source_target_pairs={{0,4},{1,5},{2,6},{3,7},{4,0},{5,1},{6,2},{7,3},{8,12},{9,13},{10,... | collective-permute-start | bytes 1544 | tf_op jit(solution)/shard_map/ppermute | solution.py:387
  30.4 5.5 %collective-permute-start.11 = (f32[1,128]{1,0:T(1,128)S(1)}, f32[1,128]{1,0:T(1,128)S(1)}, u32[]{:S(2)}, u32[]{:S(2)}) collective-permute-start(f32[1,128]{1,0:T(1,128)S(1)} %add.25), channel_id=1, source_target_pairs={{0,6},{1,7},{2,4},{3,5},{4,2},{5,3},{6,0},{7,1},{8,14},{9,15},{10,... | collective-permute-start | bytes 1544 | tf_op jit(solution)/shard_map/ppermute | solution.py:387
  31.7 4.2 %collective-permute-start.9 = (f32[1,128]{1,0:T(1,128)S(1)}, f32[1,128]{1,0:T(1,128)S(1)}, u32[]{:S(2)}, u32[]{:S(2)}) collective-permute-start(f32[1,128]{1,0:T(1,128)S(1)} %add.25), channel_id=1, source_target_pairs={{0,2},{1,3},{2,0},{3,1},{4,6},{5,7},{6,4},{7,5},{8,10},{9,11},{10,... | collective-permute-start | bytes 1544 | tf_op jit(solution)/shard_map/ppermute | solution.py:387
  31.8 9.3 %collective-permute-start.13 = (bf16[64,1280]{1,0:T(8,128)(2,1)S(1)}, bf16[64,1280]{1,0:T(8,128)(2,1)S(1)}, u32[]{:S(2)}, u32[]{:S(2)}) collective-permute-start(bf16[64,1280]{1,0:T(8,128)(2,1)S(1)} %add_convert_fusion), channel_id=1, source_target_pairs={{0,6},{1,7},{2,4},{3,5},{4,2},{5,3},{6,0},{7,1},{8,14},{9,15},{10,... | collective-permute-start | bytes 491528 | tf_op jit(solution)/shard_map/ppermute | solution.py:387
  35.9 3.6 %collective-permute-start.12 = (f32[1,128]{1,0:T(1,128)S(1)}, f32[1,128]{1,0:T(1,128)S(1)}, u32[]{:S(2)}, u32[]{:S(2)}) collective-permute-start(f32[1,128]{1,0:T(1,128)S(1)} %add_add_fusion), channel_id=1, source_target_pairs={{0,8},{8,0},{16,24},{24,16},{1,9},{9,1},{17,25},{25,17},{2,10},{10... | collective-permute-start | bytes 1544 | tf_op jit(solution)/shard_map/ppermute | solution.py:387
  38.2 5.4 %collective-permute-start.5 = (bf16[128,1280]{1,0:T(8,128)(2,1)S(1)}, bf16[128,1280]{1,0:T(8,128)(2,1)S(1)}, u32[]{:S(2)}, u32[]{:S(2)}) collective-permute-start(bf16[128,1280]{1,0:T(8,128)(2,1)S(1)} %get-tuple-element.47), channel_id=1, source_target_pairs={{0,1},{1,0},{2,3},{3,2},{4,5},{5,4},{6,7},{7,6},{8,9},{9,8},{10,11... | collective-permute-start | bytes 983048 | tf_op jit(solution)/shard_map/ppermute | solution.py:387
  39.5 3.5 %collective-permute-start.16 = (f32[1,128]{1,0:T(1,128)S(1)}, f32[1,128]{1,0:T(1,128)S(1)}, u32[]{:S(2)}, u32[]{:S(2)}) collective-permute-start(f32[1,128]{1,0:T(1,128)S(1)} %add.29), channel_id=1, source_target_pairs={{0,16},{8,24},{16,0},{24,8},{1,17},{9,25},{17,1},{25,9},{2,18},{10... | collective-permute-start | bytes 1544 | tf_op jit(solution)/shard_map/ppermute | solution.py:387
  41.0 2.0 %collective-permute-start.15 = (bf16[32,1280]{1,0:T(8,128)(2,1)S(1)}, bf16[32,1280]{1,0:T(8,128)(2,1)S(1)}, u32[]{:S(2)}, u32[]{:S(2)}) collective-permute-start(bf16[32,1280]{1,0:T(8,128)(2,1)S(1)} %slice.29), channel_id=1, source_target_pairs={{0,1},{1,0},{2,3},{3,2},{4,5},{5,4},{6,7},{7,6},{8,9},{9,8},{10,11... | collective-permute-start | bytes 245768 | tf_op jit(solution)/shard_map/ppermute | solution.py:387
  41.2 2.5 %collective-permute-start.14 = (f32[32,1280]{1,0:T(8,128)S(1)}, f32[32,1280]{1,0:T(8,128)S(1)}, u32[]{:S(2)}, u32[]{:S(2)}) collective-permute-start(f32[32,1280]{1,0:T(8,128)S(1)} %convert_add_fusion), channel_id=1, source_target_pairs={{0,1},{1,0},{2,3},{3,2},{4,5},{5,4},{6,7},{7,6},{8,9},{9,8},{10,11... | collective-permute-start | bytes 491528 | tf_op jit(solution)/shard_map/ppermute | solution.py:387

commit v6 on v5

--- a/solution.py
+++ b/solution.py
@@ -432,7 +432,7 @@
                 self.gains = sum(arrived, self.gains)
 
 
-OPT = dict(tl=2, km=2.0, tp=0, tc=1, split=0, steps="cD|yx|", near=1, hb=0, sb=2, pc=0.1)
+OPT = dict(tl=2, kk=1, km=2.0, tp=0, tc=1, split=0, steps="D|yxc|", near=1, hb=0, sb=2, pc=0.1)
 
 
 def chunk_bounds(half):
@@ -490,6 +490,10 @@
         [late_keys, unmerge, key_row],
     )
 
+    if OPT["kk"]:
+        normed, key_unit, key_scale, table, gain_row = lax.optimization_barrier(
+            (normed, key_unit, key_scale, table, gain_row)
+        )
     group = min(chips, 4)
     results = [
         call(
@@ -514,9 +518,11 @@
     far = [chip_reduce(part[: chips // 2 - 1 : -1]) if chips > 1 else [] for part in parts]
     rest.advance(first_steps[:1])
     near_parts = [part[: max(chips // 2, 1)] for part in parts]
-    if OPT["tp"]:
+    if OPT["tp"] == 1:
         _, near_parts = lax.optimization_barrier((rest.gains, near_parts))
     rest.advance(first_steps[1:])
+    if OPT["tp"] == 2:
+        _, near_parts = lax.optimization_barrier((rest.gains, near_parts))
     if OPT["hb"]:
         far, rest.gains = lax.optimization_barrier((far, rest.gains))
     mirror = CORES * (chips - 1)

time: 45.2 us -> 44.8 us (level)
  waiting for transfers between devices: 13.2 us -> 12.2 us
  local copies, waits for them, and re-layouts: 0.05 us -> 0.68 us
    ppermute x17, waiting for transfers between devices: 13.2 us -> 12.2 us  [exchange(): lax.ppermute(array, axis, [(i, i ^ apart) for i in range(lax.axis_size(ax...]
    unnamed x16, local copies, waits for them, and re-layouts: 0.04 us -> 0.68 us
  transfers between devices with their start and end apart: 17 -> 17, of which waited for: 6 -> 8; matrix products, arithmetic and copies ran while one was open for 2% -> 2% of each run, Pallas kernels for 5% -> 5%
where the time goes in v6:
time: 44.8 us; the launch traced here: 44.7 us
  starting transfers between devices  21.2 us (47%)
  waiting for transfers between devices  12.2 us (27%)
  Pallas kernels  9.12 us (20%)
  between operations  0.82 us (2%)
  local copies, waits for them, and re-layouts  0.68 us (2%)
  other arithmetic  0.67 us (1%)
    ppermute x17, starting transfers between devices, exchange(): lax.ppermute(array, axis, [(i, i ^ apart) for i in range(lax.axis_size(ax...  21.2 us
    ppermute x17, waiting for transfers between devices, exchange(): lax.ppermute(array, axis, [(i, i ^ apart) for i in range(lax.axis_size(ax...  12.2 us
    pallas_call x8, Pallas kernels, call(): pl.pallas_call(kernel, out_shape=[jax.ShapeDtypeStruct(shape, kind) for s...  9.12 us
  transfers between devices with their start and end apart: 17, of which 8 were waited for; matrix products, arithmetic and copies ran while one was open for 2% of the time, Pallas kernels for 5%

profile of v6, /device:TPU:0, one launch (start us, length us, event | category | flops | bytes accessed | tf_op | source)
XLA Modules:
  0.0 44.7 jit_solution(6258536176213332252)
XLA Ops:
  0.6 0.0 copy-start.1
  0.6 0.0 copy-start.2
  0.7 0.0 copy-start.3
  0.7 0.0 copy-start.6
  0.7 2.2 %shard_map.127 = bf16[32,1280]{1,0:T(8,128)(2,1)} custom-call(bf16[128,1280]{1,0:T(8,128)(2,1)} %bitcast.24, bf16[128,1280]{1,0:T(8,128)(2,1)} %bitcast.22, s32[4,32]{1,0:T(4,128)} %bitcast.31, f32[1,64]{1,0:T(1,128)} %bitcast.19), custom_call_target="tpu_custom_call" | custom-call | flops 500000000 | bytes 1000000 | tf_op jit(solution)/shard_map/pallas_call | solution.py:26
  2.8 0.0 copy-start.4
  2.9 0.0 copy-start.5
  2.9 0.5 %collective-permute-start = (bf16[32,1280]{1,0:T(8,128)(2,1)}, bf16[32,1280]{1,0:T(8,128)(2,1)S(1)}, u32[]{:S(2)}, u32[]{:S(2)}) collective-permute-start(bf16[32,1280]{1,0:T(8,128)(2,1)} %shard_map.127), channel_id=1, source_target_pairs={{0,1},{1,0},{2,3},{3,2},{4,5},{5,4},{6,7},{7,6},{8,9},{9,8},{10,11... | collective-permute-start | bytes 245768 | tf_op jit(solution)/shard_map/ppermute | solution.py:387
  3.4 0.0 copy-done.1
  3.4 0.0 copy-done.2
  3.4 0.0 copy-done.3
  3.4 0.0 copy-done.6
  3.4 0.6 %shard_map.131 = bf16[32,1280]{1,0:T(8,128)(2,1)S(1)} custom-call(bf16[128,1280]{1,0:T(8,128)(2,1)S(1)} %bitcast.25, bf16[128,1280]{1,0:T(8,128)(2,1)S(1)} %bitcast.23, s32[4,32]{1,0:T(4,128)S(1)} %bitcast.32, f32[1,64]{1,0:T(1,128)S(1)} %bitcast.20), custom_call_target="tpu_custom_call" | custom-call | flops 500000000 | bytes 1000000 | tf_op jit(solution)/shard_map/pallas_call | solution.py:26
  4.0 0.5 %collective-permute-done = bf16[32,1280]{1,0:T(8,128)(2,1)S(1)} collective-permute-done((bf16[32,1280]{1,0:T(8,128)(2,1)}, bf16[32,1280]{1,0:T(8,128)(2,1)S(1)}, u32[]{:S(2)}, u32[]{:S(2)}) %collective-permute-start) | collective-permute-done | bytes 81952 | tf_op jit(solution)/shard_map/ppermute | solution.py:387
  4.5 0.0 copy-done.4
  4.5 0.0 copy-done.5
  4.5 0.1 shard_map.128
  4.6 0.0 copy-start.7
  4.6 0.4 collective-permute-start.1
  5.0 4.8 %collective-permute-start.3 = (bf16[64,1280]{1,0:T(8,128)(2,1)S(1)}, bf16[64,1280]{1,0:T(8,128)(2,1)S(1)}, u32[]{:S(2)}, u32[]{:S(2)}) collective-permute-start(bf16[64,1280]{1,0:T(8,128)(2,1)S(1)} %pad_maximum_fusion.refs_5_), channel_id=1, source_target_pairs={{0,6},{1,7},{2,4},{3,5},{4,2},{5,3},{6,0},{7,1},{8,14},{9,15},{10,... | collective-permute-start | bytes 491528 | tf_op jit(solution)/shard_map/ppermute | solution.py:387
  9.8 0.0 collective-permute-start.2
  9.9 5.1 %collective-permute-done.3.refs_8_ = bf16[64,1280]{1,0:T(8,128)(2,1)S(1)} collective-permute-done((bf16[64,1280]{1,0:T(8,128)(2,1)S(1)}, bf16[64,1280]{1,0:T(8,128)(2,1)S(1)}, u32[]{:S(2)}, u32[]{:S(2)}) %collective-permute-start.3) | collective-permute-done | bytes 163872 | tf_op jit(solution)/shard_map/ppermute | solution.py:387
  14.9 2.8 %collective-permute-start.4 = (bf16[64,1280]{1,0:T(8,128)(2,1)S(1)}, bf16[64,1280]{1,0:T(8,128)(2,1)S(1)}, u32[]{:S(2)}, u32[]{:S(2)}) collective-permute-start(bf16[64,1280]{1,0:T(8,128)(2,1)S(1)} %collective-permute-done.3.refs_8_), channel_id=1, source_target_pairs={{0,2},{1,3},{2,0},{3,1},{4,6},{5,7},{6,4},{7,5},{8,10},{9,11},{10,... | collective-permute-start | bytes 491528 | tf_op jit(solution)/shard_map/ppermute | solution.py:387
  17.8 0.0 copy-done.7
  17.8 0.6 %shard_map.130 = (f32[128,1280]{1,0:T(8,128)S(1)}, f32[128,1280]{1,0:T(8,128)S(1)}, bf16[128,64]{1,0:T(8,128)(2,1)S(1)}, f32[1,256]{1,0:T(1,128)S(1)}) custom-call(bf16[128,1280]{1,0:T(8,128)(2,1)S(1)} %bitcast.26, s32[1,128]{1,0:T(1,128)S(1)} %copy-done.7, f32[1,64]{1,0:T(1,128)S(1)} %bitcast.21), custom_call_target="tpu_custom_call" | custom-call | flops 1000000000 | bytes 2000000 | tf_op jit(solution)/shard_map/pallas_call | solution.py:26
  18.4 0.0 copy-start
  18.4 0.0 collective-permute-done.1.arrived_ref
  18.5 0.6 %copy-done = f32[64]{0:T(128)S(1)} copy-done((f32[64]{0:T(128)S(1)}, f32[64]{0:T(128)}, u32[]{:S(2)}) %copy-start) | copy-done | bytes 280
  19.1 0.5 %shard_map.129 = (f32[256,640]{1,0:T(8,128)S(1)}, f32[256,640]{1,0:T(8,128)S(1)}, bf16[256,640]{1,0:T(8,128)(2,1)S(1)}, bf16[256,640]{1,0:T(8,128)(2,1)S(1)}) custom-call(bf16[128,1280]{1,0:T(8,128)(2,1)S(1)} %bitcast.28, bf16[128,1280]{1,0:T(8,128)(2,1)S(1)} %bitcast.30, bf16[128,1280]{1,0:T(8,128)(2,1)S(1)} %collective-permute-done.1.arrived_ref, ...), custom_call_target="tpu_custom_call" | custom-call | flops 1000000000 | bytes 2000000 | tf_op jit(solution)/shard_map/pallas_call | solution.py:26
  19.6 0.0 collective-permute-done.2.refs_6_
  19.6 2.1 %collective-permute-done.4.refs_7_ = bf16[64,1280]{1,0:T(8,128)(2,1)S(1)} collective-permute-done((bf16[64,1280]{1,0:T(8,128)(2,1)S(1)}, bf16[64,1280]{1,0:T(8,128)(2,1)S(1)}, u32[]{:S(2)}, u32[]{:S(2)}) %collective-permute-start.4) | collective-permute-done | bytes 163872 | tf_op jit(solution)/shard_map/ppermute | solution.py:387
  21.7 3.0 %shard_map.132 = (bf16[128,1280]{1,0:T(8,128)(2,1)S(1)}, bf16[128,1280]{1,0:T(8,128)(2,1)S(1)}, f32[1,128]{1,0:T(1,128)S(1)}, f32[64,1280]{1,0:T(8,128)S(1)}, bf...) custom-call(bf16[256,640]{1,0:T(8,128)(2,1)S(1)} %get-tuple-element.50.refs_0_, ...), custom_call_target="tpu_custom_call" | custom-call | flops 3500000000 | bytes 7000000 | tf_op jit(solution)/shard_map/pallas_call | solution.py:26
  24.7 1.8 %collective-permute-start.7 = (bf16[64,1280]{1,0:T(8,128)(2,1)S(1)}, bf16[64,1280]{1,0:T(8,128)(2,1)S(1)}, u32[]{:S(2)}, u32[]{:S(2)}) collective-permute-start(bf16[64,1280]{1,0:T(8,128)(2,1)S(1)} %get-tuple-element.66), channel_id=1, source_target_pairs={{0,2},{1,3},{2,0},{3,1},{4,6},{5,7},{6,4},{7,5},{8,10},{9,11},{10,... | collective-permute-start | bytes 491528 | tf_op jit(solution)/shard_map/ppermute | solution.py:387
  26.5 2.5 %collective-permute-start.10 = (f32[1,128]{1,0:T(1,128)S(1)}, f32[1,128]{1,0:T(1,128)S(1)}, u32[]{:S(2)}, u32[]{:S(2)}) collective-permute-start(f32[1,128]{1,0:T(1,128)S(1)} %get-tuple-element.67), channel_id=1, source_target_pairs={{0,6},{1,7},{2,4},{3,5},{4,2},{5,3},{6,0},{7,1},{8,14},{9,15},{10,... | collective-permute-start | bytes 1544 | tf_op jit(solution)/shard_map/ppermute | solution.py:387
  29.0 0.0 collective-permute-start.9
  29.0 1.9 %collective-permute-start.8 = (f32[1,128]{1,0:T(1,128)S(1)}, f32[1,128]{1,0:T(1,128)S(1)}, u32[]{:S(2)}, u32[]{:S(2)}) collective-permute-start(f32[1,128]{1,0:T(1,128)S(1)} %get-tuple-element.67), channel_id=1, source_target_pairs={{0,2},{1,3},{2,0},{3,1},{4,6},{5,7},{6,4},{7,5},{8,10},{9,11},{10,... | collective-permute-start | bytes 1544 | tf_op jit(solution)/shard_map/ppermute | solution.py:387
  30.9 0.1 collective-permute-start.6
  31.0 0.0 collective-permute-done.7
  31.1 2.5 %collective-permute-start.12 = (bf16[64,1280]{1,0:T(8,128)(2,1)S(1)}, bf16[64,1280]{1,0:T(8,128)(2,1)S(1)}, u32[]{:S(2)}, u32[]{:S(2)}) collective-permute-start(bf16[64,1280]{1,0:T(8,128)(2,1)S(1)} %add_convert_fusion), channel_id=1, source_target_pairs={{0,6},{1,7},{2,4},{3,5},{4,2},{5,3},{6,0},{7,1},{8,14},{9,15},{10,... | collective-permute-start | bytes 491528 | tf_op jit(solution)/shard_map/ppermute | solution.py:387
  33.5 0.0 collective-permute-done.10
  33.5 0.0 collective-permute-done.9
  33.5 0.0 collective-permute-done.8
  33.6 1.6 %collective-permute-start.11 = (f32[1,128]{1,0:T(1,128)S(1)}, f32[1,128]{1,0:T(1,128)S(1)}, u32[]{:S(2)}, u32[]{:S(2)}) collective-permute-start(f32[1,128]{1,0:T(1,128)S(1)} %add_add_fusion), channel_id=1, source_target_pairs={{0,8},{8,0},{16,24},{24,16},{1,9},{9,1},{17,25},{25,17},{2,10},{10... | collective-permute-start | bytes 1544 | tf_op jit(solution)/shard_map/ppermute | solution.py:387
  35.1 2.0 %collective-permute-done.11 = f32[1,128]{1,0:T(1,128)S(1)} collective-permute-done((f32[1,128]{1,0:T(1,128)S(1)}, f32[1,128]{1,0:T(1,128)S(1)}, u32[]{:S(2)}, u32[]{:S(2)}) %collective-permute-start.11) | collective-permute-done | bytes 544 | tf_op jit(solution)/shard_map/ppermute | solution.py:387
  37.2 0.4 collective-permute-done.6.refs_8_
  37.6 1.5 %collective-permute-start.15 = (f32[1,128]{1,0:T(1,128)S(1)}, f32[1,128]{1,0:T(1,128)S(1)}, u32[]{:S(2)}, u32[]{:S(2)}) collective-permute-start(f32[1,128]{1,0:T(1,128)S(1)} %add.28), channel_id=1, source_target_pairs={{0,16},{8,24},{16,0},{24,8},{1,17},{9,25},{17,1},{25,9},{2,18},{10... | collective-permute-start | bytes 1544 | tf_op jit(solution)/shard_map/ppermute | solution.py:387
  39.1 0.7 %shard_map.133 = (bf16[128,1280]{1,0:T(8,128)(2,1)}, bf16[128,1280]{1,0:T(8,128)(2,1)}) custom-call(bf16[128,1280]{1,0:T(8,128)(2,1)S(1)} %get-tuple-element.55.refs_0_), custom_call_target="tpu_custom_call" | custom-call | flops 100000000 | bytes 200000 | tf_op jit(solution)/shard_map/pallas_call | solution.py:26
  39.9 0.1 collective-permute-start.5
  40.0 1.2 %collective-permute-done.15 = f32[1,128]{1,0:T(1,128)S(1)} collective-permute-done((f32[1,128]{1,0:T(1,128)S(1)}, f32[1,128]{1,0:T(1,128)S(1)}, u32[]{:S(2)}, u32[]{:S(2)}) %collective-permute-start.15) | collective-permute-done | bytes 544 | tf_op jit(solution)/shard_map/ppermute | solution.py:387
  41.2 0.0 collective-permute-start.16
  41.2 0.0 collective-permute-done.12.refs_9_
  41.2 0.6 %collective-permute-start.14 = (bf16[32,1280]{1,0:T(8,128)(2,1)S(1)}, bf16[32,1280]{1,0:T(8,128)(2,1)S(1)}, u32[]{:S(2)}, u32[]{:S(2)}) collective-permute-start(bf16[32,1280]{1,0:T(8,128)(2,1)S(1)} %slice.29), channel_id=1, source_target_pairs={{0,1},{1,0},{2,3},{3,2},{4,5},{5,4},{6,7},{7,6},{8,9},{9,8},{10,11... | collective-permute-start | bytes 245768 | tf_op jit(solution)/shard_map/ppermute | solution.py:387
  41.8 0.1 collective-permute-start.13
  41.9 0.4 collective-permute-done.16
  42.3 0.4 collective-permute-done.14.refs_11_
  42.7 0.6 %bitcast_divide_fusion = (f32[64]{0:T(128)}, f32[64]{0:T(128)}) fusion(f32[64]{0:T(128)S(1)} %copy-done.1, f32[1,128]{1,0:T(1,128)S(1)} %add.31, f32[64]{0:T(128)S(1)} %copy-done), kind=kLoop, calls=%fused_computation.3 | loop fusion | flops 128 | bytes 1536 | tf_op jit(solution)/shard_map/div | solution.py:613
  43.3 0.0 collective-permute-done.13.refs_10_
  43.3 0.0 collective-permute-done.5.refs_2_
  43.3 1.4 %shard_map.134 = (bf16[128,1280]{1,0:T(8,128)(2,1)}, bf16[128,1280]{1,0:T(8,128)(2,1)}, bf16[128,1280]{1,0:T(8,128)(2,1)}, bf16[128,1280]{1,0:T(8,128)(2,1)}) custom-call(bf16[128,1280]{1,0:T(8,128)(2,1)} %get-tuple-element.56.refs_0_, bf16[128,1280]{1,0:T(8,128)(2,1)} %get-tuple-element.57.refs_1_, ...), custom_call_target="tpu_custom_call", output_to_operand_aliasing={{2}: (0, {}), {3}: (1, {})} | custom-call | flops 2000000000 | bytes 4000000 | tf_op jit(solution)/shard_map/pallas_call | solution.py:26
  (8 shorter events, 0.1 us)
Async XLA Ops:
  0.6 2.8 %copy-start.1 = (f32[64]{0:T(128)S(1)}, f32[64]{0:T(128)}, u32[]{:S(2)}) copy-start(f32[64]{0:T(128)} %param.15) | copy-start | bytes 772
  0.6 2.7 %copy-start.2 = (bf16[1,128,1280]{2,1,0:T(8,128)(2,1)S(1)}, bf16[1,128,1280]{2,1,0:T(8,128)(2,1)}, u32[]{:S(2)}) copy-start(bf16[1,128,1280]{2,1,0:T(8,128)(2,1)} %param.10) | copy-start | bytes 983044
  0.7 2.7 %copy-start.3 = (bf16[1,128,1280]{2,1,0:T(8,128)(2,1)S(1)}, bf16[1,128,1280]{2,1,0:T(8,128)(2,1)}, u32[]{:S(2)}) copy-start(bf16[1,128,1280]{2,1,0:T(8,128)(2,1)} %param.9) | copy-start | bytes 983044
  0.7 2.7 %copy-start.6 = (s32[1,32,4]{1,2,0:T(4,128)S(1)}, s32[1,32,4]{1,2,0:T(4,128)}, u32[]{:S(2)}) copy-start(s32[1,32,4]{1,2,0:T(4,128)} %param.11) | copy-start | bytes 1540
  2.8 1.7 %copy-start.4 = (bf16[1,128,1280]{2,1,0:T(8,128)(2,1)S(1)}, bf16[1,128,1280]{2,1,0:T(8,128)(2,1)}, u32[]{:S(2)}) copy-start(bf16[1,128,1280]{2,1,0:T(8,128)(2,1)} %param.8) | copy-start | bytes 983044
  2.9 1.7 %copy-start.5 = (bf16[1,128,1280]{2,1,0:T(8,128)(2,1)S(1)}, bf16[1,128,1280]{2,1,0:T(8,128)(2,1)}, u32[]{:S(2)}) copy-start(bf16[1,128,1280]{2,1,0:T(8,128)(2,1)} %param.13) | copy-start | bytes 983044
  2.9 1.7 %collective-permute-start = (bf16[32,1280]{1,0:T(8,128)(2,1)}, bf16[32,1280]{1,0:T(8,128)(2,1)S(1)}, u32[]{:S(2)}, u32[]{:S(2)}) collective-permute-start(bf16[32,1280]{1,0:T(8,128)(2,1)} %shard_map.127), channel_id=1, source_target_pairs={{0,1},{1,0},{2,3},{3,2},{4,5},{5,4},{6,7},{7,6},{8,9},{9,8},{10,11... | collective-permute-start | bytes 245768 | tf_op jit(solution)/shard_map/ppermute | solution.py:387
  4.6 13.2 %copy-start.7 = (s32[1,128]{1,0:T(1,128)S(1)}, s32[1,128]{1,0:T(1,128)}, u32[]{:S(2)}) copy-start(s32[1,128]{1,0:T(1,128)} %unmerge_ref.1) | copy-start | bytes 1540
  4.6 13.9 %collective-permute-start.1 = (bf16[128,1280]{1,0:T(8,128)(2,1)S(1)}, bf16[128,1280]{1,0:T(8,128)(2,1)S(1)}, u32[]{:S(2)}, u32[]{:S(2)}) collective-permute-start(bf16[128,1280]{1,0:T(8,128)(2,1)S(1)} %shard_map.128), channel_id=1, source_target_pairs={{0,1},{1,0},{2,3},{3,2},{4,5},{5,4},{6,7},{7,6},{8,9},{9,8},{10,11... | collective-permute-start | bytes 983048 | tf_op jit(solution)/shard_map/ppermute | solution.py:387
  5.0 9.9 %collective-permute-start.3 = (bf16[64,1280]{1,0:T(8,128)(2,1)S(1)}, bf16[64,1280]{1,0:T(8,128)(2,1)S(1)}, u32[]{:S(2)}, u32[]{:S(2)}) collective-permute-start(bf16[64,1280]{1,0:T(8,128)(2,1)S(1)} %pad_maximum_fusion.refs_5_), channel_id=1, source_target_pairs={{0,6},{1,7},{2,4},{3,5},{4,2},{5,3},{6,0},{7,1},{8,14},{9,15},{10,... | collective-permute-start | bytes 491528 | tf_op jit(solution)/shard_map/ppermute | solution.py:387
  9.8 9.8 %collective-permute-start.2 = (bf16[64,1280]{1,0:T(8,128)(2,1)S(1)}, bf16[64,1280]{1,0:T(8,128)(2,1)S(1)}, u32[]{:S(2)}, u32[]{:S(2)}) collective-permute-start(bf16[64,1280]{1,0:T(8,128)(2,1)S(1)} %pad_maximum_fusion.refs_5_), channel_id=1, source_target_pairs={{0,2},{1,3},{2,0},{3,1},{4,6},{5,7},{6,4},{7,5},{8,10},{9,11},{10,... | collective-permute-start | bytes 491528 | tf_op jit(solution)/shard_map/ppermute | solution.py:387
  14.9 6.8 %collective-permute-start.4 = (bf16[64,1280]{1,0:T(8,128)(2,1)S(1)}, bf16[64,1280]{1,0:T(8,128)(2,1)S(1)}, u32[]{:S(2)}, u32[]{:S(2)}) collective-permute-start(bf16[64,1280]{1,0:T(8,128)(2,1)S(1)} %collective-permute-done.3.refs_8_), channel_id=1, source_target_pairs={{0,2},{1,3},{2,0},{3,1},{4,6},{5,7},{6,4},{7,5},{8,10},{9,11},{10,... | collective-permute-start | bytes 491528 | tf_op jit(solution)/shard_map/ppermute | solution.py:387
  18.4 0.7 %copy-start = (f32[64]{0:T(128)S(1)}, f32[64]{0:T(128)}, u32[]{:S(2)}) copy-start(f32[64]{0:T(128)} %param.14) | copy-start | bytes 772
  24.7 6.3 %collective-permute-start.7 = (bf16[64,1280]{1,0:T(8,128)(2,1)S(1)}, bf16[64,1280]{1,0:T(8,128)(2,1)S(1)}, u32[]{:S(2)}, u32[]{:S(2)}) collective-permute-start(bf16[64,1280]{1,0:T(8,128)(2,1)S(1)} %get-tuple-element.66), channel_id=1, source_target_pairs={{0,2},{1,3},{2,0},{3,1},{4,6},{5,7},{6,4},{7,5},{8,10},{9,11},{10,... | collective-permute-start | bytes 491528 | tf_op jit(solution)/shard_map/ppermute | solution.py:387
  26.5 7.0 %collective-permute-start.10 = (f32[1,128]{1,0:T(1,128)S(1)}, f32[1,128]{1,0:T(1,128)S(1)}, u32[]{:S(2)}, u32[]{:S(2)}) collective-permute-start(f32[1,128]{1,0:T(1,128)S(1)} %get-tuple-element.67), channel_id=1, source_target_pairs={{0,6},{1,7},{2,4},{3,5},{4,2},{5,3},{6,0},{7,1},{8,14},{9,15},{10,... | collective-permute-start | bytes 1544 | tf_op jit(solution)/shard_map/ppermute | solution.py:387
  29.0 4.5 %collective-permute-start.9 = (f32[1,128]{1,0:T(1,128)S(1)}, f32[1,128]{1,0:T(1,128)S(1)}, u32[]{:S(2)}, u32[]{:S(2)}) collective-permute-start(f32[1,128]{1,0:T(1,128)S(1)} %get-tuple-element.67), channel_id=1, source_target_pairs={{0,4},{1,5},{2,6},{3,7},{4,0},{5,1},{6,2},{7,3},{8,12},{9,13},{10,... | collective-permute-start | bytes 1544 | tf_op jit(solution)/shard_map/ppermute | solution.py:387
  29.0 4.5 %collective-permute-start.8 = (f32[1,128]{1,0:T(1,128)S(1)}, f32[1,128]{1,0:T(1,128)S(1)}, u32[]{:S(2)}, u32[]{:S(2)}) collective-permute-start(f32[1,128]{1,0:T(1,128)S(1)} %get-tuple-element.67), channel_id=1, source_target_pairs={{0,2},{1,3},{2,0},{3,1},{4,6},{5,7},{6,4},{7,5},{8,10},{9,11},{10,... | collective-permute-start | bytes 1544 | tf_op jit(solution)/shard_map/ppermute | solution.py:387
  30.9 6.7 %collective-permute-start.6 = (bf16[64,1280]{1,0:T(8,128)(2,1)S(1)}, bf16[64,1280]{1,0:T(8,128)(2,1)S(1)}, u32[]{:S(2)}, u32[]{:S(2)}) collective-permute-start(bf16[64,1280]{1,0:T(8,128)(2,1)S(1)} %get-tuple-element.64), channel_id=1, source_target_pairs={{0,2},{1,3},{2,0},{3,1},{4,6},{5,7},{6,4},{7,5},{8,10},{9,11},{10,... | collective-permute-start | bytes 491528 | tf_op jit(solution)/shard_map/ppermute | solution.py:387
  31.1 10.1 %collective-permute-start.12 = (bf16[64,1280]{1,0:T(8,128)(2,1)S(1)}, bf16[64,1280]{1,0:T(8,128)(2,1)S(1)}, u32[]{:S(2)}, u32[]{:S(2)}) collective-permute-start(bf16[64,1280]{1,0:T(8,128)(2,1)S(1)} %add_convert_fusion), channel_id=1, source_target_pairs={{0,6},{1,7},{2,4},{3,5},{4,2},{5,3},{6,0},{7,1},{8,14},{9,15},{10,... | collective-permute-start | bytes 491528 | tf_op jit(solution)/shard_map/ppermute | solution.py:387
  33.6 3.6 %collective-permute-start.11 = (f32[1,128]{1,0:T(1,128)S(1)}, f32[1,128]{1,0:T(1,128)S(1)}, u32[]{:S(2)}, u32[]{:S(2)}) collective-permute-start(f32[1,128]{1,0:T(1,128)S(1)} %add_add_fusion), channel_id=1, source_target_pairs={{0,8},{8,0},{16,24},{24,16},{1,9},{9,1},{17,25},{25,17},{2,10},{10... | collective-permute-start | bytes 1544 | tf_op jit(solution)/shard_map/ppermute | solution.py:387
  37.6 3.5 %collective-permute-start.15 = (f32[1,128]{1,0:T(1,128)S(1)}, f32[1,128]{1,0:T(1,128)S(1)}, u32[]{:S(2)}, u32[]{:S(2)}) collective-permute-start(f32[1,128]{1,0:T(1,128)S(1)} %add.28), channel_id=1, source_target_pairs={{0,16},{8,24},{16,0},{24,8},{1,17},{9,25},{17,1},{25,9},{2,18},{10... | collective-permute-start | bytes 1544 | tf_op jit(solution)/shard_map/ppermute | solution.py:387
  39.9 3.4 %collective-permute-start.5 = (bf16[128,1280]{1,0:T(8,128)(2,1)S(1)}, bf16[128,1280]{1,0:T(8,128)(2,1)S(1)}, u32[]{:S(2)}, u32[]{:S(2)}) collective-permute-start(bf16[128,1280]{1,0:T(8,128)(2,1)S(1)} %get-tuple-element.58), channel_id=1, source_target_pairs={{0,1},{1,0},{2,3},{3,2},{4,5},{5,4},{6,7},{7,6},{8,9},{9,8},{10,11... | collective-permute-start | bytes 983048 | tf_op jit(solution)/shard_map/ppermute | solution.py:387
  41.2 1.1 %collective-permute-start.16 = (f32[1,128]{1,0:T(1,128)S(1)}, f32[1,128]{1,0:T(1,128)S(1)}, u32[]{:S(2)}, u32[]{:S(2)}) collective-permute-start(f32[1,128]{1,0:T(1,128)S(1)} %add.30), channel_id=1, source_target_pairs={{0,1},{1,0},{2,3},{3,2},{4,5},{5,4},{6,7},{7,6},{8,9},{9,8},{10,11... | collective-permute-start | bytes 1544 | tf_op jit(solution)/shard_map/ppermute | solution.py:387
  41.2 1.5 %collective-permute-start.14 = (bf16[32,1280]{1,0:T(8,128)(2,1)S(1)}, bf16[32,1280]{1,0:T(8,128)(2,1)S(1)}, u32[]{:S(2)}, u32[]{:S(2)}) collective-permute-start(bf16[32,1280]{1,0:T(8,128)(2,1)S(1)} %slice.29), channel_id=1, source_target_pairs={{0,1},{1,0},{2,3},{3,2},{4,5},{5,4},{6,7},{7,6},{8,9},{9,8},{10,11... | collective-permute-start | bytes 245768 | tf_op jit(solution)/shard_map/ppermute | solution.py:387
  41.8 1.5 %collective-permute-start.13 = (f32[32,1280]{1,0:T(8,128)S(1)}, f32[32,1280]{1,0:T(8,128)S(1)}, u32[]{:S(2)}, u32[]{:S(2)}) collective-permute-start(f32[32,1280]{1,0:T(8,128)S(1)} %convert_add_fusion), channel_id=1, source_target_pairs={{0,1},{1,0},{2,3},{3,2},{4,5},{5,4},{6,7},{7,6},{8,9},{9,8},{10,11... | collective-permute-start | bytes 491528 | tf_op jit(solution)/shard_map/ppermute | solution.py:387
